TPU v7x, 256 devices: a whole 4x4x8 slice. The times are simulated.
256 devices in a mesh: grp: 2 (over core), dev: 128 (over z, y, x).
Axes of the slice: x: 4, y: 4, z: 8, core: 2. Of those that a mesh axis runs over, the one named last changes fastest.
Arguments:
- spectra: float32 [1296, 32768], P(None, ('grp', 'dev')), may hold values from 0.05 to 1
- sea_mask: int32 [32768], P(('grp', 'dev')), may hold values 0 or 1
- card_map: int32 [32768], replicated, may hold values from 0 to 16383, as said below
- dia_table: int32 [4, 1296], replicated, may hold values from 0 to 1295
- dia_coef: float32 [1296], replicated, may hold values from 0.5 to 3
- speed: float32 [1296], replicated, may hold values from 0.1 to 0.6
- stokes_weight: float32 [1296], replicated, may hold values from 0.02 to 0.2
- couple_point: int32 [2048, 256], P(('grp', 'dev')), may hold values from -1 to 16383, as said below
- ocean_u: float32 [40, 2048, 256], P(None, ('grp', 'dev')), may hold values from -6 to 6
- ocean_v: float32 [40, 2048, 256], P(None, ('grp', 'dev')), may hold values from -6 to 6
- mixing: float32 [40], replicated, may hold values from 0.2 to 2
Outputs:
- new_spectra: float32 [1296, 32768], P(None, ('grp', 'dev'))
- new_u: float32 [40, 2048, 256], P(None, ('grp', 'dev'))
- new_v: float32 [40, 2048, 256], P(None, ('grp', 'dev'))
Inputs may be any that keep to these rules, and one draw needn't show every extreme that they name: `card_map`: within each group's 128 * 128 entries every value appears exactly once. `couple_point`: the cell in column c of ocean row x couples to a point of its own group whose row lies within one of (x mod (1024)) // 8 and whose column lies within one of c // 2; -1 marks land.
All inputs are finite; a program needn't handle non-finite values. No bound on the sum of `sea_mask` on one device may be relied on, other than what follows from the above.
Results may differ from a plain program's by a relative error of at most 0.00007.
Values sent between devices are 32-bit elements; how exact they have to be, the bound alone decides.
A program may use at most 128 MiB of HBM per device.

v0:
```python
import jax
import jax.numpy as jnp
from jax import lax
from jax.sharding import PartitionSpec as P

ND = 36
GX = 128
NZ = 40
PSTEPS = 2
OSTEPS = 2


DT_SRC = 0.5
CURRENT_GAIN = 0.3
DT_OCEAN = 0.2
VISCOSITY = 0.2
CORIOLIS = 1.0


def with_halo(block, sides, width):
    for axis, dim in sides:
        count = lax.axis_size(axis)
        forward = [(i, i + 1) for i in range(count - 1)]
        backward = [(target, source) for source, target in forward]
        low = lax.ppermute(
            lax.slice_in_dim(block, block.shape[dim] - width, None, axis=dim), axis, forward
        )
        high = lax.ppermute(lax.slice_in_dim(block, 0, width, axis=dim), axis, backward)
        block = jnp.concatenate([low, block, high], axis=dim)
    return block


def direction_cosines(index):
    theta = ((index % ND).astype(jnp.float32) + 0.5) * (2.0 * jnp.pi / ND)
    return (jnp.cos(theta), jnp.sin(theta))


def source_terms(energy, table, coef):
    plus_one = energy[table[0]]
    minus_one = energy[table[1]]
    plus_two = energy[table[2]]
    minus_two = energy[table[3]]
    scale = coef[:, None]
    first = scale * (energy * energy * (plus_one + minus_one) - 2.0 * energy * plus_one * minus_one)
    second = scale * (
        energy * energy * (plus_two + minus_two) - 2.0 * energy * plus_two * minus_two
    )
    total = -2.0 * (first + second)
    total = total.at[table[0]].add(first).at[table[1]].add(first)
    total = total.at[table[2]].add(second).at[table[3]].add(second)
    return total


def along_columns(outgoing, incoming):
    dims = outgoing.ndim
    following = jnp.pad(incoming[..., 1:], [(0, 0)] * (dims - 1) + [(0, 1)])
    preceding = jnp.pad(outgoing[..., :-1], [(0, 0)] * (dims - 1) + [(1, 0)])
    return outgoing - incoming + following - preceding


def horizontal(values, prev_rows, next_rows):
    padded = jnp.pad(values, ((0, 0), (0, 0), (1, 1)))
    return next_rows + prev_rows + padded[:, :, 2:] + padded[:, :, :-2] - 4.0 * values


def vertical(values, mixing):
    above = jnp.concatenate([jnp.zeros_like(values[:1]), values[:-1]], 0)
    flux = mixing[:, None, None] * (values - above)
    below = jnp.concatenate([flux[1:], jnp.zeros_like(flux[:1])], 0)
    return below - flux


def body(
    spectra,
    sea_mask,
    card_map,
    dia_table,
    dia_coef,
    speed,
    stokes_weight,
    couple_point,
    ocean_u,
    ocean_v,
    mixing,
):
    comp_count = spectra.shape[0]
    point_count = spectra.shape[1]
    devices = lax.axis_size("dev")
    device = lax.axis_index("dev")
    groups = lax.axis_size("grp")
    group = lax.axis_index("grp")
    total_points = card_map.shape[0]
    group_points = total_points // groups
    rows_dev = point_count // GX
    group_rows = group_points // GX
    group_map = lax.dynamic_slice_in_dim(card_map, group * group_points, group_points, 0)
    mask_float = sea_mask.astype(jnp.float32)
    forced = mask_float * (spectra + DT_SRC * source_terms(spectra, dia_table, dia_coef))
    cosine, sine = direction_cosines(jnp.arange(comp_count, dtype=jnp.int32))
    weights = jnp.stack([stokes_weight * cosine, stokes_weight * sine])
    lowest = device * rows_dev - 1
    span = (rows_dev + 2) * GX
    valid = couple_point >= 0
    valid_float = valid.astype(jnp.float32)
    local = couple_point - lowest * GX
    target = jnp.where(valid, local, span)
    surface = jnp.stack([ocean_u[0], ocean_v[0], jnp.ones_like(ocean_u[0])]).reshape(3, -1)
    partial_value = (
        jnp.zeros((3, span + 1), jnp.float32).at[:, target.reshape(-1)].add(surface)[:, :span]
    )
    partial_value = partial_value.reshape(3, rows_dev + 2, GX)
    drift = jnp.dot(weights, forced, precision=lax.Precision.HIGHEST)
    drift_all, block_all = (
        lax.all_gather(drift, "dev", axis=1, tiled=True),
        lax.all_gather(partial_value, "dev", axis=1, tiled=True),
    )
    pieces = block_all.reshape(3, devices, rows_dev + 2, GX)
    middle = pieces[:, :, 1 : rows_dev + 1]
    empty = jnp.zeros((3, 1, GX), jnp.float32)
    lower = jnp.concatenate([pieces[:, 1:, 0], empty], 1)
    upper = jnp.concatenate([empty, pieces[:, :-1, rows_dev + 1]], 1)
    middle = middle.at[:, :, rows_dev - 1].add(lower).at[:, :, 0].add(upper)
    totals = middle.reshape(3, group_rows, GX)
    inverse = (
        jnp.zeros((group_points,), jnp.int32)
        .at[group_map]
        .set(jnp.arange(group_points, dtype=jnp.int32))
    )
    cell_index = jnp.where(valid, couple_point, 0)
    drift_cells = drift_all[:, inverse[cell_index]] * valid_float
    currents = totals[:2] / (totals[2] + 1.0)
    share = -(-comp_count // devices)
    padded_count = share * devices
    padded = jnp.pad(forced, ((0, padded_count - comp_count), (0, 0)))
    arrived = lax.all_to_all(padded, "dev", split_axis=0, concat_axis=1, tiled=True)
    grid = jnp.zeros((share, group_points), jnp.float32).at[:, group_map].set(arrived)
    grid = grid.reshape(share, group_rows, GX)
    comp_index = device * share + jnp.arange(share, dtype=jnp.int32)
    speed_padded = jnp.pad(speed, (0, padded_count - comp_count))
    group_speed = lax.dynamic_slice_in_dim(speed_padded, device * share, share, 0)
    cos_own, sin_own = direction_cosines(comp_index)
    speed_x = group_speed[:, None, None] * cos_own[:, None, None] + CURRENT_GAIN * currents[0]
    speed_y = group_speed[:, None, None] * sin_own[:, None, None] + CURRENT_GAIN * currents[1]
    field = grid
    for substep in range(PSTEPS):
        out_x = jnp.maximum(speed_x, 0.0) * field
        in_x = jnp.minimum(speed_x, 0.0) * field
        out_y = jnp.maximum(speed_y, 0.0) * field
        in_y = jnp.minimum(speed_y, 0.0) * field
        edged_rows = with_halo(jnp.stack([out_y, in_y]), (("grp", 2),), 1)
        prev_y = edged_rows[0, :, :-2]
        next_y = edged_rows[1, :, 2:]
        field = field - along_columns(out_x, in_x) - (out_y - in_y + next_y - prev_y)
    leaving = field.reshape(share, group_points)[:, group_map]
    returned = lax.all_to_all(leaving, "dev", split_axis=1, concat_axis=0, tiled=True)
    new_spectra = returned[:comp_count] * mask_float
    ocean_local = ocean_u.shape[1]
    ocean_total = ocean_local * lax.axis_size(("grp", "dev"))
    ocean_start = lax.axis_index(("grp", "dev")) * ocean_local
    row_index = ocean_start + jnp.arange(ocean_local, dtype=jnp.int32)
    coriolis = CORIOLIS * (0.5 + row_index.astype(jnp.float32) / ocean_total)[:, None]
    profile = jnp.exp(-3.0 * (jnp.arange(NZ, dtype=jnp.int32).astype(jnp.float32) + 0.5) / NZ)[
        :, None, None
    ]
    drift_u = drift_cells[0]
    drift_v = drift_cells[1]
    current_u, current_v = (ocean_u, ocean_v)
    for substep in range(OSTEPS):
        edged_ocean = with_halo(jnp.stack([current_u, current_v]), ((("grp", "dev"), 2),), 1)
        lap_u = horizontal(current_u, edged_ocean[0, :, :-2], edged_ocean[0, :, 2:])
        lap_v = horizontal(current_v, edged_ocean[1, :, :-2], edged_ocean[1, :, 2:])
        next_u = current_u + DT_OCEAN * (
            VISCOSITY * lap_u
            + vertical(current_u, mixing)
            + coriolis * (current_v + profile * drift_v)
        )
        next_v = current_v + DT_OCEAN * (
            VISCOSITY * lap_v
            + vertical(current_v, mixing)
            - coriolis * (current_u + profile * drift_u)
        )
        current_u, current_v = (next_u, next_v)
    return (new_spectra, current_u, current_v)


def solution(mesh):
    in_specs = (
        P(None, ("grp", "dev")),
        P(("grp", "dev")),
        P(),
        P(),
        P(),
        P(),
        P(),
        P(("grp", "dev"), None),
        P(None, ("grp", "dev"), None),
        P(None, ("grp", "dev"), None),
        P(),
    )
    out_specs = (
        P(None, ("grp", "dev")),
        P(None, ("grp", "dev"), None),
        P(None, ("grp", "dev"), None),
    )
    return jax.shard_map(body, mesh=mesh, in_specs=in_specs, out_specs=out_specs, check_vma=False)
```

profile of v0, /device:TPU:1, one launch (start us, length us, event | category | flops | bytes accessed | tf_op | source)
XLA Modules:
  0.0 1078.3 jit_solution(17262180049799847161)
XLA Ops:
  0.6 2.1 pad_maximum_fusion.19
  2.8 13.5 %collective-permute-start.4 = (f32[2,40,1,256]{3,2,1,0:T(1,128)}, f32[2,40,1,256]{3,2,1,0:T(1,128)}, u32[]{:S(2)}, u32[]{:S(2)}) collective-permute-start(f32[2,40,1,256]{3,2,1,0:T(1,128)} %get-tuple-element.53), channel_id=1, source_target_pairs={{1,0},{2,1},{3,2},{4,3},{5,4},{6,5},{7,6},{8,7},{9,8},{10,9},{11,1... | collective-permute-start | bytes 245768 | tf_op jit(solution)/shard_map/ppermute | solution.py:28
  16.3 1.9 collective-permute-start.5
  18.2 1.0 fusion.88
  19.2 4.7 gather_fusion
  23.9 3.6 gather_fusion.1
  27.6 3.6 gather_fusion.2
  31.2 3.6 gather_fusion.3
  34.8 2.1 add_multiply_fusion.1
  36.9 9.2 scatter_fusion
  46.1 9.2 scatter_fusion.1
  55.2 9.2 scatter_fusion.2
  64.4 9.2 scatter_fusion.3
  73.8 0.5 copy-done.20
  74.3 1.1 all_to_all.28
  75.4 10.1 all-to-all-start
  85.7 0.4 fusion.74
  86.2 300.5 %all_gather.7 = f32[2,16384]{1,0:T(2,128)S(1)} all-gather(f32[2,128]{1,0:T(2,128)S(1)} %fusion.74), channel_id=1, replica_groups=mesh['grp'=2,'dev'=128] {'dev'}, dimensions={1}, use_global_device_ids=true | all-gather | bytes 132096 | tf_op jit(solution)/shard_map/all_gather | solution.py:114
  386.7 4.9 copy.100
  391.7 0.7 broadcast_clamp_fusion
  392.3 60.3 %scatter_custom_fusion.6 = s32[16384]{0:T(1024)S(1)} fusion(s32[16384]{0:T(1024)S(1)} %get-tuple-element.32, s32[16384]{0:T(1024)S(1)} %iota.27, s32[]{:T(128)} %constant.112.clone.1), kind=kCustom, calls=%fused_computation.149 | custom fusion | bytes 65540 | tf_op jit(solution)/shard_map/scatter | solution.py:127
  452.7 11.8 %gather_fusion.5 = s32[2048]{0:T(1024)S(1)} fusion(s32[16384]{0:T(1024)S(1)} %scatter_custom_fusion.6, s32[2048]{0:T(1024)S(1)} %broadcast_clamp_fusion.2), kind=kCustom, calls=%fused_computation.5 | custom fusion | bytes 24576 | tf_op jit(solution)/shard_map/gather | solution.py:130
  464.5 8.8 gather_fusion.6
  473.4 0.3 copy.101
  473.9 0.4 copy.102
  474.2 11.5 %scatter_custom_fusion.5 = f32[3,385]{0,1:T(8,128)S(1)} fusion(s32[2048]{0:T(1024)S(1)} %bitcast.158, f32[2048,3]{1,0:T(8,128)S(1)} %bitcast.152, f32[]{:T(128)} %constant.108.clone.1), kind=kCustom, calls=%fused_computation.134 | custom fusion | flops 6144 | bytes 4624 | tf_op jit(solution)/shard_map/scatter-add | solution.py:109
  485.9 287.6 %all_gather.6 = f32[3,384,128]{2,0,1:T(4,128)S(1)} all-gather(f32[3,3,128]{2,0,1:T(4,128)S(1)} %copy.88), channel_id=1, replica_groups=mesh['grp'=2,'dev'=128] {'dev'}, dimensions={1}, use_global_device_ids=true | all-gather | bytes 594432 | tf_op jit(solution)/shard_map/all_gather | solution.py:115
  773.5 0.6 multiply_bitcast_fusion
  774.8 0.2 copy-done.3
  775.0 0.8 subtract_multiply_fusion.4
  775.8 0.2 copy.85
  776.1 0.6 copy.105
  776.8 4.7 copy.86
  781.5 44.4 %scatter_custom_fusion.4 = f32[11,16384]{0,1:T(8,128)} fusion(s32[16384]{0:T(1024)S(1)} %get-tuple-element.32, f32[16384,11]{1,0:T(8,128)} %copy.86, f32[]{:T(128)} %constant.108.clone.1), kind=kCustom, calls=%fused_computation.14 | custom fusion | bytes 721408 | tf_op jit(solution)/shard_map/scatter | solution.py:136
  825.8 5.3 copy.93
  831.1 5.3 copy.96
  836.4 0.3 fusion.14
  836.7 115.0 %collective-permute-start = (f32[2,11,1,128]{3,2,1,0:T(1,128)S(1)}, f32[2,11,1,128]{3,2,1,0:T(1,128)S(1)}, u32[]{:S(2)}, u32[]{:S(2)}) collective-permute-start(f32[2,11,1,128]{3,2,1,0:T(1,128)S(1)} %get-tuple-element.40), channel_id=1, source_target_pairs={{128,0},{129,1},{130,2},{131,3},{132,4},{133,5},{134,6},{135,7},{1... | collective-permute-start | bytes 33800 | tf_op jit(solution)/shard_map/ppermute | solution.py:28
  951.7 1.3 collective-permute-start.1
  953.0 0.2 fusion.5
  953.2 0.3 slice.318
  953.5 1.3 collective-permute-done.1
  954.8 1.6 fusion.4
  956.4 2.0 fusion.24
  958.4 0.6 pad_maximum_fusion.21
  959.0 2.7 collective-permute-start.2
  961.7 1.3 collective-permute-start.3
  963.0 0.7 slice.273
  963.8 0.2 slice.321
  964.0 1.1 collective-permute-done.3
  965.1 1.9 fusion.18
  967.0 4.8 copy.98
  971.8 58.2 %gather_fusion.4 = f32[16384,11]{1,0:T(8,128)} fusion(f32[11,16384]{0,1:T(8,128)} %bitcast.121, s32[16384]{0:T(1024)S(1)} %copy-done.9), kind=kCustom, calls=%fused_computation.4 | custom fusion | bytes 1507328 | tf_op jit(solution)/shard_map/gather | solution.py:154
  1030.0 6.1 copy.99
  1036.1 8.6 all-to-all-start.1
  1044.9 1.3 fusion.36
  1046.2 1.3 subtract_multiply_fusion.2
  1047.6 9.7 collective-permute-start.6
  1057.3 1.9 collective-permute-start.7
  1059.3 7.7 collective-permute-done.6
  1067.0 7.9 collective-permute-done.7
  1074.9 1.2 fusion.40
  1076.2 1.2 fusion.32
  1077.4 0.9 slice_multiply_fusion
  (96 shorter events, 1.7 us)
Async XLA Ops:
  0.6 23.3 %copy-start = (f32[1296,128]{1,0:T(8,128)S(1)}, f32[1296,128]{1,0:T(8,128)}, u32[]{:S(2)}) copy-start(f32[1296,128]{1,0:T(8,128)} %param.15) | copy-start | bytes 1990660
  2.8 1042.1 %collective-permute-start.4 = (f32[2,40,1,256]{3,2,1,0:T(1,128)}, f32[2,40,1,256]{3,2,1,0:T(1,128)}, u32[]{:S(2)}, u32[]{:S(2)}) collective-permute-start(f32[2,40,1,256]{3,2,1,0:T(1,128)} %get-tuple-element.53), channel_id=1, source_target_pairs={{1,0},{2,1},{3,2},{4,3},{5,4},{6,5},{7,6},{8,7},{9,8},{10,9},{11,1... | collective-permute-start | bytes 245768 | tf_op jit(solution)/shard_map/ppermute | solution.py:28
  16.3 1028.5 %collective-permute-start.5 = (f32[2,40,1,256]{3,2,1,0:T(1,128)}, f32[2,40,1,256]{3,2,1,0:T(1,128)}, u32[]{:S(2)}, u32[]{:S(2)}) collective-permute-start(f32[2,40,1,256]{3,2,1,0:T(1,128)} %get-tuple-element.54), channel_id=1, source_target_pairs={{0,1},{1,2},{2,3},{3,4},{4,5},{5,6},{6,7},{7,8},{8,9},{9,10},{10,1... | collective-permute-start | bytes 245768 | tf_op jit(solution)/shard_map/ppermute | solution.py:25
  23.9 10.9 %copy-start.17 = (f32[1296]{0:T(1024)S(1)}, f32[1296]{0:T(1024)}, u32[]{:S(2)}) copy-start(f32[1296]{0:T(1024)} %param.19) | copy-start | bytes 15556
  64.4 9.2 copy-start.22
  64.4 21.2 %copy-start.2 = (f32[40,8,256]{2,1,0:T(8,128)S(1)}, f32[40,8,256]{2,1,0:T(8,128)}, u32[]{:S(2)}) copy-start(f32[40,8,256]{2,1,0:T(8,128)} %param.23) | copy-start | bytes 983044
  64.4 21.2 %copy-start.1 = (f32[40,8,256]{2,1,0:T(8,128)S(1)}, f32[40,8,256]{2,1,0:T(8,128)}, u32[]{:S(2)}) copy-start(f32[40,8,256]{2,1,0:T(8,128)} %param.24) | copy-start | bytes 983044
  64.4 21.2 %copy-start.18 = (f32[1296]{0:T(1024)S(1)}, f32[1296]{0:T(1024)}, u32[]{:S(2)}) copy-start(f32[1296]{0:T(1024)} %param.21) | copy-start | bytes 15556
  73.6 318.0 %copy-start.12 = (s32[8,256]{1,0:T(8,128)S(1)}, s32[8,256]{1,0:T(8,128)}, u32[]{:S(2)}) copy-start(s32[8,256]{1,0:T(8,128)} %param.22) | copy-start | bytes 24580
  73.6 318.0 %copy-start.11 = (s32[32768]{0:T(1024)S(1)}, s32[32768]{0:T(1024)}, u32[]{:S(2)}) copy-start(s32[32768]{0:T(1024)} %param.17) | copy-start | bytes 393220
  73.6 0.6 copy-start.20
  75.4 700.4 %all-to-all-start = ((f32[128,11,128]{2,1,0:T(8,128)}), f32[128,11,128]{2,1,0:T(8,128)S(1)}, u32[]{:S(2)}, u32[]{:S(2)}) async-start(f32[128,11,128]{2,1,0:T(8,128)} %all_to_all.28), calls=%async_computation | async-start | bytes 2097152 | tf_op jit(solution)/shard_map/all_to_all | solution.py:135
  391.6 382.5 %copy-start.19 = (f32[1296]{0:T(1024)S(1)}, f32[1296]{0:T(1024)}, u32[]{:S(2)}) copy-start(f32[1296]{0:T(1024)} %param.20) | copy-start | bytes 15556
  391.6 383.4 %copy-start.13 = (f32[40]{0:T(128)S(1)}, f32[40]{0:T(128)}, u32[]{:S(2)}) copy-start(f32[40]{0:T(128)} %param.25) | copy-start | bytes 484
  774.2 182.2 %copy-start.15 = (f32[11]{0:T(128)}, f32[11]{0:T(128)S(1)}, u32[]{:S(2)}) copy-start(f32[11]{0:T(128)S(1)} %get-tuple-element.67) | copy-start | bytes 136
  774.2 182.2 %copy-start.16 = (f32[11]{0:T(128)}, f32[11]{0:T(128)S(1)}, u32[]{:S(2)}) copy-start(f32[11]{0:T(128)S(1)} %get-tuple-element.68) | copy-start | bytes 136
  774.2 0.7 copy-start.3
  775.0 61.4 %copy-start.6 = (f32[1,128,128]{2,0,1:T(1,128)}, f32[1,128,128]{2,0,1:T(1,128)S(1)}, u32[]{:S(2)}) copy-start(f32[1,128,128]{2,0,1:T(1,128)S(1)} %get-tuple-element.59) | copy-start | bytes 196612
  775.0 178.1 %copy-start.8 = (f32[1,128,128]{2,0,1:T(1,128)}, f32[1,128,128]{2,0,1:T(1,128)S(1)}, u32[]{:S(2)}) copy-start(f32[1,128,128]{2,0,1:T(1,128)S(1)} %get-tuple-element.60) | copy-start | bytes 196612
  836.4 126.6 %copy-start.10 = (f32[2,8,256]{2,1,0:T(8,128)S(1)}, f32[2,8,256]{2,1,0:T(8,128)}, u32[]{:S(2)}) copy-start(f32[2,8,256]{2,1,0:T(8,128)} %multiply_bitcast_fusion) | copy-start | bytes 49156
  836.7 119.8 %copy-start.7 = (f32[1,128,128]{2,0,1:T(1,128)S(1)}, f32[1,128,128]{2,0,1:T(1,128)}, u32[]{:S(2)}) copy-start(f32[1,128,128]{2,0,1:T(1,128)} %copy-done.6) | copy-start | bytes 196612
  836.7 116.8 %collective-permute-start = (f32[2,11,1,128]{3,2,1,0:T(1,128)S(1)}, f32[2,11,1,128]{3,2,1,0:T(1,128)S(1)}, u32[]{:S(2)}, u32[]{:S(2)}) collective-permute-start(f32[2,11,1,128]{3,2,1,0:T(1,128)S(1)} %get-tuple-element.40), channel_id=1, source_target_pairs={{128,0},{129,1},{130,2},{131,3},{132,4},{133,5},{134,6},{135,7},{1... | collective-permute-start | bytes 33800 | tf_op jit(solution)/shard_map/ppermute | solution.py:28
  951.7 3.1 collective-permute-start.1
  959.0 5.0 collective-permute-start.2
  961.7 3.4 collective-permute-start.3
  967.0 4.8 copy-start.9
  971.8 73.1 %copy-start.4 = (f32[39,8,256]{2,1,0:T(8,128)S(1)}, f32[39,8,256]{2,1,0:T(8,128)}, u32[]{:S(2)}) copy-start(f32[39,8,256]{2,1,0:T(8,128)} %copy-done.3) | copy-start | bytes 958468
  971.8 73.1 %copy-start.5 = (f32[39,8,256]{2,1,0:T(8,128)S(1)}, f32[39,8,256]{2,1,0:T(8,128)}, u32[]{:S(2)}) copy-start(f32[39,8,256]{2,1,0:T(8,128)} %slice.273) | copy-start | bytes 958468
  971.8 73.1 %slice-start = ((f32[40,8,256]{2,1,0:T(8,128)}), f32[39,8,256]{2,1,0:T(8,128)S(1)}, s32[]{:S(2)}) async-start(f32[40,8,256]{2,1,0:T(8,128)} %subtract_multiply_fusion.4), calls=%async_computation.2 | async-start | bytes 638976 | tf_op jit(solution)/shard_map/slice | solution.py:69
  971.8 73.1 %copy-start.14 = (f32[40]{0:T(128)S(1)}, f32[40]{0:T(128)}, u32[]{:S(2)}) copy-start(f32[40]{0:T(128)} %param.25) | copy-start | bytes 484
  1036.1 41.2 %all-to-all-start.1 = ((f32[11,128,128]{2,0,1:T(8,128)}), f32[11,128,128]{2,0,1:T(8,128)S(1)}, u32[]{:S(2)}, u32[]{:S(2)}) async-start(f32[11,128,128]{2,0,1:T(8,128)} %copy.99), calls=%async_computation.1 | async-start | bytes 2097152 | tf_op jit(solution)/shard_map/all_to_all | solution.py:155
  1044.9 32.6 %copy-start.21 = (f32[128]{0:T(128)S(1)}, f32[128]{0:T(128)}, u32[]{:S(2)}) copy-start(f32[128]{0:T(128)} %copy-done.20) | copy-start | bytes 1540
  1047.6 19.5 %collective-permute-start.6 = (f32[2,40,1,256]{3,2,1,0:T(1,128)S(1)}, f32[2,40,1,256]{3,2,1,0:T(1,128)S(1)}, u32[]{:S(2)}, u32[]{:S(2)}) collective-permute-start(f32[2,40,1,256]{3,2,1,0:T(1,128)S(1)} %get-tuple-element.51), channel_id=1, source_target_pairs={{1,0},{2,1},{3,2},{4,3},{5,4},{6,5},{7,6},{8,7},{9,8},{10,9},{11,1... | collective-permute-start | bytes 245768 | tf_op jit(solution)/shard_map/ppermute | solution.py:28
  1057.3 17.6 %collective-permute-start.7 = (f32[2,40,1,256]{3,2,1,0:T(1,128)S(1)}, f32[2,40,1,256]{3,2,1,0:T(1,128)S(1)}, u32[]{:S(2)}, u32[]{:S(2)}) collective-permute-start(f32[2,40,1,256]{3,2,1,0:T(1,128)S(1)} %get-tuple-element.52), channel_id=1, source_target_pairs={{0,1},{1,2},{2,3},{3,4},{4,5},{5,6},{6,7},{7,8},{8,9},{9,10},{10,1... | collective-permute-start | bytes 245768 | tf_op jit(solution)/shard_map/ppermute | solution.py:25
where the time goes:
time: 1080 us
  blocking collectives  588 us (54%)
  local copies, waits for them, and re-layouts  236 us (22%)
  starting transfers between devices  166 us (15%)
  other arithmetic  68.7 us (6%)
  waiting for transfers between devices  18 us (2%)
    all_gather x1, blocking collectives, body(): lax.all_gather(drift, 'dev', axis=1, tiled=True)  300 us
    all_gather x1, blocking collectives, body(): lax.all_gather(partial_value, 'dev', axis=1, tiled=True)  288 us
    ppermute x4, starting transfers between devices, with_halo(): lax.ppermute(lax.slice_in_dim(block, 0, width, axis=dim), axis, backward)  141 us
    scatter x1, local copies, waits for them, and re-layouts, body(): inverse = jnp.zeros((group_points,), jnp.int32).at[group_map].set(jnp.ara...  60.3 us
    gather x1, local copies, waits for them, and re-layouts, body(): leaving = field.reshape(share, group_points)[:, group_map]  58.2 us
    scatter x1, local copies, waits for them, and re-layouts, body(): jnp.zeros((share, group_points), jnp.float32).at[:, group_map].set(arrived)  44.4 us
  transfers between devices with their start and end apart: 10, of which 4 were waited for; matrix products, arithmetic and copies ran while one was open for 28% of the time, Pallas kernels for 0%

commit v1 on v0

v1 whole, which is shorter than its diff:
```python
import jax
import jax.numpy as jnp
from jax import lax
from jax.experimental import pallas as pl
from jax.experimental.pallas import tpu as pltpu
from jax.sharding import PartitionSpec as P

ND = 36
NZ = 40
KC = 1296
KP = 1408
SHARE = 11
F32, BF16 = jnp.float32, jnp.bfloat16
NT = (((1,), (1,)), ((), ()))
HIGH = lax.Precision.HIGHEST
MESH = pl.DeviceIdType.MESH
VMEM_LIMIT = 56 << 20


def direction_cosines(index):
    theta = ((index % ND).astype(jnp.float32) + 0.5) * (2.0 * jnp.pi / ND)
    return (jnp.cos(theta), jnp.sin(theta))


def split(x):
    hi = x.astype(BF16)
    return hi, (x - hi.astype(F32)).astype(BF16)


def spread_matrix():
    wide = lax.broadcasted_iota(jnp.int32, (128, 768), 1)
    target = ((wide & 255) >> 1) + (wide >> 8) - 1
    return jnp.where(lax.broadcasted_iota(jnp.int32, (128, 768), 0) == target, 1.0, 0.0)


def couple_masks(cp, dev):
    row = (cp >> 7) - dev
    col = (cp & 127) - (lax.broadcasted_iota(jnp.int32, (8, 256), 1) >> 1)
    valid = cp >= 0
    return [
        [jnp.where(valid & (row == dr - 1) & (col == delta - 1), 1.0, 0.0) for delta in range(3)]
        for dr in range(3)
    ]


def partial_kernel(cp_ref, u_ref, v_ref, out_ref):
    masks = couple_masks(cp_ref[...], lax.axis_index("dev"))
    surface = [u_ref[...], v_ref[...], None]
    rows = []
    for dr in range(3):
        for q in range(3):
            parts = []
            for delta in range(3):
                m = masks[dr][delta]
                parts.append(jnp.sum(m if q == 2 else m * surface[q], axis=0, keepdims=True))
            rows.append(jnp.concatenate(parts, axis=1))
    rows.append(jnp.zeros((7, 768), F32))
    wide = jnp.concatenate(rows, axis=0)
    out_ref[...] = lax.dot_general(wide, spread_matrix(), NT, precision=HIGH, preferred_element_type=F32)


def dia_kernel(e_ref, mask_ref, trow_ref, col_ref, w_ref, cur_ref, out_ref, E, F1, F2, OH, forced_ref):
    CH = 432
    tail = jnp.zeros((KP - KC, 256), BF16)
    E[KC:, :] = tail
    F1[KC:, :] = tail
    F2[KC:, :] = tail
    hi, lo = split(e_ref[...])
    E[:KC, :128] = hi
    E[:KC, 128:] = lo

    def gather(i, _):
        rows = pl.ds(pl.multiple_of(i * CH, 16), CH)
        lanes = lax.broadcasted_iota(jnp.int32, (CH, KP), 1).astype(F32)
        e = e_ref[rows, :]
        cols = col_ref[rows, :]
        for m in range(4):
            OH[m * CH : (m + 1) * CH, :] = jnp.where(lanes == cols[:, m : m + 1], 1.0, 0.0).astype(BF16)
        p = jnp.dot(OH[...], E[...], preferred_element_type=F32)
        p = p[:, :128] + p[:, 128:]
        g = [p[m * CH : (m + 1) * CH] for m in range(4)]
        s = cols[:, 4:5]
        ee = e * e
        e2 = 2.0 * e
        a = s * (ee * (g[0] + g[1]) - e2 * g[0] * g[1])
        b = s * (ee * (g[2] + g[3]) - e2 * g[2] * g[3])
        forced_ref[rows, :] = e - (a + b)
        ah, al = split(a)
        bh, bl = split(b)
        F1[rows, :128] = ah
        F1[rows, 128:] = al
        F2[rows, :128] = bh
        F2[rows, 128:] = bl
        return 0

    lax.fori_loop(0, KC // CH, gather, 0)

    def scatter(i, _):
        rows = pl.ds(pl.multiple_of(i * CH, 16), CH)
        b = lax.broadcasted_iota(jnp.int32, (CH, KP), 0) + i * CH

        def onehot(m):
            return jnp.where(b == trow_ref[m : m + 1, :], 1.0, 0.0)

        p = jnp.dot((onehot(0) + onehot(1)).astype(BF16), F1[...], preferred_element_type=F32)
        p = p + jnp.dot((onehot(2) + onehot(3)).astype(BF16), F2[...], preferred_element_type=F32)
        forced_ref[rows, :] = mask_ref[...] * (forced_ref[rows, :] + 0.5 * (p[:, :128] + p[:, 128:]))
        return 0

    lax.fori_loop(0, KC // CH, scatter, 0)
    forced_ref[KC:, :] = jnp.zeros((KP - KC, 128), F32)
    drift = jnp.dot(w_ref[...], forced_ref[...], precision=HIGH, preferred_element_type=F32)
    extra = jnp.concatenate([drift[0:2], cur_ref[0:2, :], jnp.zeros((1, 128), F32)], axis=0)
    for d in range(128):
        out_ref[d, 0:SHARE, :] = forced_ref[d * SHARE : (d + 1) * SHARE, :]
        out_ref[d, SHARE:16, :] = extra


def build_maps(map_ref, CT, M, MF):
    def step(s, _):
        row = map_ref[pl.ds(s, 1), :]
        n = ((row >> 13) << 7) | (row & 127)
        rl = (row >> 7) & 63
        col = pl.ds(pl.multiple_of(s * 128, 128), 128)
        CT[:, col] = jnp.where(lax.broadcasted_iota(jnp.int32, (256, 128), 0) == n, 1.0, 0.0).astype(BF16)
        mf = jnp.where(lax.broadcasted_iota(jnp.int32, (64, 128), 0) == rl, 1.0, 0.0)
        MF[:, col] = mf
        M[:, col] = mf.astype(BF16)
        return 0

    lax.fori_loop(0, 128, step, 0)


def substep(f, cx, cy, first_lane, last_lane):
    ox = jnp.maximum(cx, 0.0) * f
    ix = jnp.minimum(cx, 0.0) * f
    oy = jnp.maximum(cy, 0.0) * f
    iy = jnp.minimum(cy, 0.0) * f
    rows = f.shape[0]
    nx = jnp.where(last_lane, 0.0, pltpu.roll(ix, 127, 1))
    px = jnp.where(first_lane, 0.0, pltpu.roll(ox, 1, 1))
    ny = pltpu.roll(iy, rows - 1, 0)
    py = pltpu.roll(oy, 1, 0)
    return f - (ox - ix + nx - px) - (oy - iy + ny - py)


S = 8
R = SHARE * 64


def grid_kernel(arr_ref, map_ref, speed_ref, out_ref, drift_ref, CT, M, MF, LH, acc, dacc, T, G, cur, edge, halo, send_sem, recv_sem):
    grp = lax.axis_index("grp")
    dev = lax.axis_index("dev")
    barrier = pltpu.get_barrier_semaphore()
    pl.semaphore_signal(barrier, inc=1, device_id=(1 - grp, dev), device_id_type=MESH)
    build_maps(map_ref, CT, M, MF)
    acc[...] = jnp.zeros_like(acc)
    dacc[...] = jnp.zeros_like(dacc)
    zero_row = jnp.zeros((1, 128), F32)

    def forward(i, _):
        drift_rows = []
        for j in range(S):
            cols = pl.ds(pl.multiple_of(i * (S * 128) + j * 128, 128), 128)
            c = slice(j * 128, (j + 1) * 128)
            for k in range(SHARE):
                x = jnp.broadcast_to(arr_ref[pl.ds(i * S + j, 1), k : k + 1, :].reshape(1, 128), (16, 128))
                hi, lo = split(x)
                for q in range(4):
                    m = M[q * 16 : (q + 1) * 16, cols]
                    r = k * 64 + q * 16
                    LH[r : r + 16, c] = m * hi
                    LH[R + r : R + r + 16, c] = m * lo
            row = map_ref[pl.ds(i * S + j, 1), :] >> 7
            pieces = []
            for q in range(2):
                x = arr_ref[pl.ds(i * S + j, 1), SHARE + q : SHARE + q + 1, :].reshape(1, 128)
                for dr in range(3):
                    pieces.append(jnp.where(row == dev + (dr - 1), x, zero_row))
            pieces += [zero_row, zero_row]
            piece = jnp.concatenate(pieces, axis=0)
            hi = piece.astype(BF16).astype(F32)
            drift_rows.append(jnp.concatenate([hi, piece - hi], axis=0).astype(BF16))
        c = CT[:, pl.ds(pl.multiple_of(i * (S * 128), 128), S * 128)]
        acc[...] += lax.dot_general(LH[:R], c, NT, preferred_element_type=F32) + lax.dot_general(
            LH[R:], c, NT, preferred_element_type=F32
        )
        dacc[...] += lax.dot_general(jnp.concatenate(drift_rows, axis=1), c, NT, preferred_element_type=F32)
        return 0

    lax.fori_loop(0, 128 // S, forward, 0)
    drift = dacc[0:8] + dacc[8:16]
    rowid = lax.broadcasted_iota(jnp.int32, (8, 128), 0)
    wave_row = dev + lax.rem(rowid, 3) - 1
    drift_ref[...] = jnp.where(wave_row >= 64, drift[:, 128:], drift[:, :128])

    top = grp == 0
    for k in range(SHARE):
        low = acc[k * 64 : (k + 1) * 64, 0:128]
        high = acc[k * 64 : (k + 1) * 64, 128:256]
        G[k, 8:72, :] = low
        G[k, 72:136, :] = high
        edge[0, k : k + 1, :] = jnp.where(top, high[63:64], low[0:1])
        edge[1, k : k + 1, :] = jnp.where(top, high[62:63], low[1:2])
    for q in range(2):
        for s in range(128):
            cur[q, 8 + s : 9 + s, :] = arr_ref[s : s + 1, 13 + q : 14 + q, :].reshape(1, 128)
        edge[0, SHARE + q : SHARE + q + 1, :] = jnp.where(top, cur[q, 135:136, :], cur[q, 8:9, :])
        edge[1, SHARE + q : SHARE + q + 1, :] = jnp.where(top, cur[q, 134:135, :], cur[q, 9:10, :])
    for r in range(2):
        edge[r, 13:16, :] = jnp.zeros((3, 128), F32)
    pl.semaphore_wait(barrier, 1)
    copy = pltpu.make_async_remote_copy(
        src_ref=edge, dst_ref=halo, send_sem=send_sem, recv_sem=recv_sem, device_id=(1 - grp, dev), device_id_type=MESH
    )
    copy.start()
    copy.wait()

    below_on = jnp.where(top, 1.0, 0.0)
    above_on = 1.0 - below_on
    blank = jnp.zeros((6, 128), F32)

    def pad(dst, k, index):
        h0 = halo[0, k : k + 1, :]
        h1 = halo[1, k : k + 1, :]
        dst[index, 0:8, :] = jnp.concatenate([blank, h1, h0], axis=0) * above_on
        dst[index, 136:144, :] = jnp.concatenate([h0, h1, blank], axis=0) * below_on

    for k in range(SHARE):
        pad(G, k, k)
    for q in range(2):
        pad(cur, SHARE + q, q)
    lane = lax.broadcasted_iota(jnp.int32, (144, 128), 1)
    line = lax.broadcasted_iota(jnp.int32, (144, 128), 0)
    first_lane, last_lane = lane == 0, lane == 127
    keep = jnp.where(line < 8, above_on, jnp.where(line >= 136, below_on, 1.0))

    def propagate(k, _):
        cx = cur[0] + speed_ref[0, k]
        cy = cur[1] + speed_ref[1, k]
        f = substep(G[k], cx, cy, first_lane, last_lane) * keep
        f = substep(f, cx, cy, first_lane, last_lane)
        hi, lo = split(f[8:136])
        r = pl.multiple_of(k * 64, 64)
        for h in range(2):
            LH[pl.ds(r, 64), h * 128 : (h + 1) * 128] = hi[h * 64 : (h + 1) * 64]
            LH[pl.ds(R + r, 64), h * 128 : (h + 1) * 128] = lo[h * 64 : (h + 1) * 64]
        return 0

    lax.fori_loop(0, SHARE, propagate, 0)

    def backward(i, _):
        c = CT[:, pl.ds(pl.multiple_of(i * (S * 128), 128), S * 128)]
        T[...] = jnp.dot(LH[:R, 0:256], c, preferred_element_type=F32) + jnp.dot(
            LH[R:, 0:256], c, preferred_element_type=F32
        )
        for j in range(S):
            m = MF[:, pl.ds(pl.multiple_of(i * (S * 128) + j * 128, 128), 128)]
            for k in range(SHARE):
                r = jnp.sum(T[k * 64 : (k + 1) * 64, j * 128 : (j + 1) * 128] * m, axis=0, keepdims=True)
                out_ref[pl.ds(i * S + j, 1), k : k + 1, :] = r.reshape(1, 1, 128)
            out_ref[pl.ds(i * S + j, 1), SHARE:16, :] = jnp.zeros((1, 16 - SHARE, 128), F32)
        return 0

    lax.fori_loop(0, 128 // S, backward, 0)


def cells_kernel(drift_ref, cp_ref, out_ref):
    masks = couple_masks(cp_ref[...], lax.axis_index("dev"))
    wide = jnp.dot(drift_ref[...], spread_matrix(), precision=HIGH, preferred_element_type=F32)
    for q in range(2):
        total = jnp.zeros((8, 256), F32)
        for dr in range(3):
            for delta in range(3):
                total = total + masks[dr][delta] * wide[q * 3 + dr : q * 3 + dr + 1, delta * 256 : (delta + 1) * 256]
        out_ref[q * 8 : (q + 1) * 8, :] = total


def ocean_kernel(u_ref, v_ref, uh_ref, vh_ref, d_ref, dh_ref, mix_ref, prof_ref, ou_ref, ov_ref, A, B):
    grp = lax.axis_index("grp")
    dev = lax.axis_index("dev")
    start = (grp * 128 + dev) * 8
    line = lax.broadcasted_iota(jnp.int32, (24, 256), 0)
    lane = lax.broadcasted_iota(jnp.int32, (24, 256), 1)
    world = start + line - 8
    keep = jnp.where((world >= 0) & (world < 2048), 1.0, 0.0)
    f = 0.5 + world.astype(F32) / 2048.0
    first_lane, last_lane = lane == 0, lane == 255
    blank = jnp.zeros((6, 256), F32)

    def drift_block(q):
        return jnp.concatenate(
            [blank, dh_ref[0, q], d_ref[q * 8 : (q + 1) * 8, :], dh_ref[1, q], blank], axis=0
        )

    us, vs = drift_block(0), drift_block(1)

    def load(z, _):
        A[0, z] = jnp.concatenate([blank, uh_ref[0, z], u_ref[z], uh_ref[1, z], blank], axis=0)
        A[1, z] = jnp.concatenate([blank, vh_ref[0, z], v_ref[z], vh_ref[1, z], blank], axis=0)
        return 0

    lax.fori_loop(0, NZ, load, 0)

    def lap(a):
        r = jnp.where(last_lane, 0.0, pltpu.roll(a, 255, 1)) + jnp.where(first_lane, 0.0, pltpu.roll(a, 1, 1))
        return r + pltpu.roll(a, 1, 0) + pltpu.roll(a, 23, 0) - 4.0 * a

    def step(src, emit):
        def level(z, carry):
            pu, pv = carry
            u, v = src[0, z], src[1, z]
            last = z == NZ - 1
            zn = jnp.minimum(z + 1, NZ - 1)
            m0 = mix_ref[0, z]
            m1 = jnp.where(last, 0.0, mix_ref[0, zn])
            nu, nv = src[0, zn], src[1, zn]
            p = prof_ref[0, z]
            wu = m1 * (nu - u) - m0 * (u - pu)
            wv = m1 * (nv - v) - m0 * (v - pv)
            emit(z, u + 0.2 * (0.2 * lap(u) + wu + f * (v + p * vs)), v + 0.2 * (0.2 * lap(v) + wv - f * (u + p * us)))
            return u, v

        zero = jnp.zeros((24, 256), F32)
        lax.fori_loop(0, NZ, level, (zero, zero))

    def emit1(z, u, v):
        B[0, z] = u * keep
        B[1, z] = v * keep

    def emit2(z, u, v):
        ou_ref[z] = u[8:16]
        ov_ref[z] = v[8:16]

    step(A, emit1)
    step(B, emit2)


def neighbours(x, axis):
    n = lax.axis_size(axis)
    up = [(i, i + 1) for i in range(n - 1)]
    return lambda last, first: (lax.ppermute(last, axis, up), lax.ppermute(first, axis, [(b, a) for a, b in up]))


def params(**kw):
    return pltpu.CompilerParams(vmem_limit_bytes=VMEM_LIMIT, **kw)


def body(spectra, sea_mask, card_map, dia_table, dia_coef, speed, stokes_weight, couple_point, ocean_u, ocean_v, mixing):
    group = lax.axis_index("grp")
    device = lax.axis_index("dev")
    sds = jax.ShapeDtypeStruct
    both = ("grp", "dev")
    swap = neighbours(None, both)
    uh = jnp.stack(swap(ocean_u[:, 6:8], ocean_u[:, 0:2]))
    vh = jnp.stack(swap(ocean_v[:, 6:8], ocean_v[:, 0:2]))
    part = pl.pallas_call(partial_kernel, out_shape=sds((16, 128), F32), name="partials")(
        couple_point, ocean_u[0], ocean_v[0]
    )
    before, after = neighbours(None, "dev")(part[6:9], part[0:3])
    totals = part[3:6] + before + after
    cur = 0.3 * totals[:2] / (totals[2] + 1.0)
    cur = jnp.pad(cur, ((0, 6), (0, 0)))
    cosine, sine = direction_cosines(jnp.arange(KC, dtype=jnp.int32))
    weights = jnp.pad(jnp.stack([stokes_weight * cosine, stokes_weight * sine]), ((0, 6), (0, KP - KC)))
    trow = jnp.pad(dia_table, ((0, 4), (0, KP - KC)), constant_values=-1)
    col = jnp.concatenate([dia_table.T.astype(F32), dia_coef[:, None], jnp.zeros((KC, 3), F32)], axis=1)
    mask = sea_mask.astype(F32)[None, :]
    payload = pl.pallas_call(
        dia_kernel,
        out_shape=sds((128, 16, 128), F32),
        scratch_shapes=[pltpu.VMEM((KP, 256), BF16)] * 3 + [pltpu.VMEM((4 * 432, KP), BF16), pltpu.VMEM((KP, 128), F32)],
        compiler_params=params(),
        name="sources",
    )(spectra, mask, trow, col, weights, cur)
    arrived = lax.all_to_all(payload, "dev", split_axis=0, concat_axis=0, tiled=True)
    map2d = lax.dynamic_slice_in_dim(card_map, group * 16384, 16384, 0).reshape(128, 128)
    speeds = jnp.pad(jnp.stack([speed * cosine, speed * sine]), ((0, 0), (0, KP - KC)))
    speeds = jnp.pad(lax.dynamic_slice_in_dim(speeds, device * SHARE, SHARE, 1), ((0, 0), (0, 16 - SHARE)))
    vmem = pl.BlockSpec(memory_space=pltpu.VMEM)
    smem = pl.BlockSpec(memory_space=pltpu.SMEM)
    leaving, drift = pl.pallas_call(
        grid_kernel,
        out_shape=(sds((128, 16, 128), F32), sds((8, 128), F32)),
        in_specs=[vmem, vmem, smem],
        out_specs=(vmem, vmem),
        scratch_shapes=[
            pltpu.VMEM((256, 16384), BF16),
            pltpu.VMEM((64, 16384), BF16),
            pltpu.VMEM((64, 16384), F32),
            pltpu.VMEM((2 * R, S * 128), BF16),
            pltpu.VMEM((R, 256), F32),
            pltpu.VMEM((16, 256), F32),
            pltpu.VMEM((R, S * 128), F32),
            pltpu.VMEM((SHARE, 144, 128), F32),
            pltpu.VMEM((2, 144, 128), F32),
            pltpu.VMEM((2, 16, 128), F32),
            pltpu.VMEM((2, 16, 128), F32),
            pltpu.SemaphoreType.DMA,
            pltpu.SemaphoreType.DMA,
        ],
        compiler_params=params(collective_id=0, has_side_effects=True),
        name="grid",
    )(arrived, map2d, speeds)
    returned = lax.all_to_all(leaving, "dev", split_axis=0, concat_axis=0, tiled=True)
    new_spectra = returned[:, :SHARE].reshape(KP, 128)[:KC] * mask
    cells = pl.pallas_call(cells_kernel, out_shape=sds((16, 256), F32), name="cells")(drift, couple_point)
    cells3 = cells.reshape(2, 8, 256)
    dh = jnp.stack(swap(cells3[:, 6:8], cells3[:, 0:2]))
    profile = jnp.exp(-3.0 * (jnp.arange(NZ, dtype=jnp.int32).astype(F32) + 0.5) / NZ)[None, :]
    new_u, new_v = pl.pallas_call(
        ocean_kernel,
        out_shape=(sds((NZ, 8, 256), F32), sds((NZ, 8, 256), F32)),
        in_specs=[vmem] * 6 + [smem, smem],
        out_specs=(vmem, vmem),
        scratch_shapes=[pltpu.VMEM((2, NZ, 24, 256), F32)] * 2,
        compiler_params=params(),
        name="ocean",
    )(ocean_u, ocean_v, uh, vh, cells, dh, mixing[None, :], profile)
    return (new_spectra, new_u, new_v)


def solution(mesh):
    both = ("grp", "dev")
    in_specs = (P(None, both), P(both), P(), P(), P(), P(), P(), P(both, None), P(None, both, None), P(None, both, None), P())
    out_specs = (P(None, both), P(None, both, None), P(None, both, None))
    return jax.shard_map(body, mesh=mesh, in_specs=in_specs, out_specs=out_specs, check_vma=False)
```

time: 1080 us -> 189 us (0.17)
  blocking collectives: 588 us -> 0 us
  local copies, waits for them, and re-layouts: 236 us -> 10.9 us
  starting transfers between devices: 166 us -> 59 us
  Pallas kernels: 0 us -> 71.2 us
  other arithmetic: 68.7 us -> 5.68 us
  waiting for transfers between devices: 18 us -> 40.4 us
    all_gather x2 -> x0, blocking collectives: 588 us -> none  [the longest x1 300 us: body(): lax.all_gather(drift, 'dev', axis=1, tiled=True)]
    ppermute x8, starting transfers between devices: 147 us -> 33.2 us  [the longest x4 21.9 us: neighbours(): lax.ppermute(first, axis, [(b, a) for a, b in up])]
    scatter x2 -> x0, local copies, waits for them, and re-layouts: 105 us -> none  [the longest x1 60.3 us: body(): inverse = jnp.zeros((group_points,), jnp.int32).at[group_map].set(jnp.ara...]
    gather x9 -> x0, local copies, waits for them, and re-layouts: 94.8 us -> none  [the longest x1 58.2 us: body(): leaving = field.reshape(share, group_points)[:, group_map]]
    pallas_call x0 -> x5, Pallas kernels: none -> 71.2 us  [the longest x1 46.3 us: body(): pl.pallas_call(grid_kernel, out_shape=(sds((128, 16, 128), F32), sds((8,...]
    scatter-add x5 -> x0, other arithmetic: 48.1 us -> none  [the longest x2 18.3 us: source_terms(): total = total.at[table[2]].add(second).at[table[3]].add(second)]
    all_to_all x2, waiting for transfers between devices: 0.01 us -> 25.9 us  [the longest x1 25.9 us: body(): lax.all_to_all(payload, 'dev', split_axis=0, concat_axis=0, tiled=True)]
    all_to_all x5 -> x0, local copies, waits for them, and re-layouts: 12.3 us -> none  [the longest x2 6.17 us: body(): lax.all_to_all(leaving, 'dev', split_axis=1, concat_axis=0, tiled=True)]
  transfers between devices with their start and end apart: 10 -> 10, of which waited for: 4 -> 3; matrix products, arithmetic and copies ran while one was open for 28% -> 4% of each run, Pallas kernels for 0% -> 6%
where the time goes in v1:
time: 189 us; the launch traced here: 188 us
  Pallas kernels  71.2 us (38%)
  starting transfers between devices  59 us (31%)
  waiting for transfers between devices  40.4 us (21%)
  local copies, waits for them, and re-layouts  10.9 us (6%)
  other arithmetic  5.68 us (3%)
    pallas_call x1, Pallas kernels, body(): pl.pallas_call(grid_kernel, out_shape=(sds((128, 16, 128), F32), sds((8,...  46.3 us
    all_to_all x1, waiting for transfers between devices, body(): lax.all_to_all(payload, 'dev', split_axis=0, concat_axis=0, tiled=True)  25.9 us
    ppermute x4, starting transfers between devices, neighbours(): lax.ppermute(first, axis, [(b, a) for a, b in up])  21.9 us
    all_to_all x1, starting transfers between devices, body(): lax.all_to_all(payload, 'dev', split_axis=0, concat_axis=0, tiled=True)  19.5 us
    ppermute x4, waiting for transfers between devices, neighbours(): lax.ppermute(last, axis, up)  14.4 us
    pallas_call x1, Pallas kernels, body(): pl.pallas_call(dia_kernel, out_shape=sds((128, 16, 128), F32), scratch_sh...  11.3 us
    ppermute x4, starting transfers between devices, neighbours(): lax.ppermute(last, axis, up)  11.3 us
    pallas_call x1, Pallas kernels, body(): pl.pallas_call(ocean_kernel, out_shape=(sds((NZ, 8, 256), F32), sds((NZ,...  10.2 us
  transfers between devices with their start and end apart: 10, of which 3 were waited for; matrix products, arithmetic and copies ran while one was open for 4% of the time, Pallas kernels for 6%

profile of v1, /device:TPU:1, one launch (start us, length us, event | category | flops | bytes accessed | tf_op | source)
XLA Modules:
  0.0 188.1 jit_solution(5416608574517796024)
XLA Ops:
  0.6 0.0 copy-start
  0.6 1.3 slice_bitcast_fusion.1.u_ref
  2.0 1.3 slice_bitcast_fusion.v_ref
  3.3 1.8 partials.1
  5.1 0.8 fusion.19
  5.9 1.3 collective-permute-start.1
  7.2 4.6 %collective-permute-start = (f32[3,128]{1,0:T(4,128)S(1)}, f32[3,128]{1,0:T(4,128)S(1)}, u32[]{:S(2)}, u32[]{:S(2)}) collective-permute-start(f32[3,128]{1,0:T(4,128)S(1)} %get-tuple-element.19), channel_id=1, source_target_pairs={{0,1},{1,2},{2,3},{3,4},{4,5},{5,6},{6,7},{7,8},{8,9},{9,10},{10,1... | collective-permute-start | bytes 4616 | tf_op jit(solution)/shard_map/ppermute | solution.py:342
  11.7 0.0 copy-done.7
  11.8 0.0 copy-done.4
  11.8 0.0 copy-start.5
  11.8 0.7 copy-done.5
  12.5 0.1 fusion.8
  12.6 0.1 pad.37.clone
  12.7 0.6 select_maximum_fusion.w_ref
  13.3 0.1 maximum_maximum_fusion
  13.4 0.6 copy-done.8
  13.9 0.5 fusion.20
  14.4 0.6 pad.20.trow_ref
  15.1 1.1 copy.17.col_ref
  16.2 0.0 collective-permute-done.1
  16.2 0.0 collective-permute-done
  16.2 0.7 fusion.12
  16.9 0.6 pad.22.cur_ref
  17.5 11.3 %sources.1 = f32[128,16,128]{2,1,0:T(8,128)} custom-call(f32[1296,128]{1,0:T(8,128)} %e_ref.1, f32[1,128]{1,0:T(1,128)} %get-tuple-element.24.mask_ref, s32[8,1408]{1,0:T(8,128)} %pad.20.trow_ref, f32[1296,8]{1,0:T(8,128)} %copy.17.col_ref, f32[8,1408]{1,0:T(8,128)} %select_maximum_fusion.w_ref, f32[8,128]{1,0:T(8,128)} %pad.22.cur_ref), custom_call_target="tpu_custom_call" | custom-call | tf_op jit(solution)/shard_map/sources/pallas_call | solution.py:369
  28.8 19.5 %all-to-all-start = ((f32[128,16,128]{2,1,0:T(8,128)}), f32[128,16,128]{2,1,0:T(8,128)S(1)}, u32[]{:S(2)}, u32[]{:S(2)}) async-start(f32[128,16,128]{2,1,0:T(8,128)} %sources.1), calls=%async_computation | async-start | bytes 2097152 | tf_op jit(solution)/shard_map/all_to_all | solution.py:376
  48.3 0.0 copy-start.6
  48.3 0.7 copy-done.6
  49.0 0.1 fusion.9
  49.1 0.1 fusion.14
  49.2 0.6 pad.24.speed_ref
  49.8 0.0 copy-done
  49.8 0.6 dynamic-slice_bitcast_fusion.map_ref
  50.4 25.9 %all-to-all-done.arr_ref = f32[128,16,128]{2,1,0:T(8,128)S(1)} async-done(((f32[128,16,128]{2,1,0:T(8,128)}), f32[128,16,128]{2,1,0:T(8,128)S(1)}, u32[]{:S(2)}, u32[]{:S(2)}) %all-to-all-start) | async-done | bytes 1048608 | tf_op jit(solution)/shard_map/all_to_all | solution.py:376
  76.3 1.0 copy-done.1
  77.3 46.3 %grid.1 = (f32[128,16,128]{2,1,0:T(8,128)}, f32[8,128]{1,0:T(8,128)}) custom-call(f32[128,16,128]{2,1,0:T(8,128)} %copy-done.1, s32[128,128]{1,0:T(8,128)} %dynamic-slice_bitcast_fusion.map_ref, f32[2,16]{1,0:T(2,128)} %pad.24.speed_ref), custom_call_target="tpu_custom_call" | custom-call | tf_op jit(solution)/shard_map/grid/pallas_call | solution.py:382
  123.6 0.0 copy-start.2
  123.6 6.3 %all-to-all-start.1 = ((f32[128,16,128]{2,1,0:T(8,128)}), f32[128,16,128]{2,1,0:T(8,128)S(1)}, u32[]{:S(2)}, u32[]{:S(2)}) async-start(f32[128,16,128]{2,1,0:T(8,128)} %get-tuple-element.7), calls=%async_computation.1 | async-start | bytes 2097152 | tf_op jit(solution)/shard_map/all_to_all | solution.py:405
  129.9 0.0 copy-done.2
  129.9 0.0 copy-start.3
  129.9 0.1 fusion.17
  130.0 9.1 %collective-permute-start.3 = (f32[40,2,256]{2,1,0:T(2,128)S(1)}, f32[40,2,256]{2,1,0:T(2,128)S(1)}, u32[]{:S(2)}, u32[]{:S(2)}) collective-permute-start(f32[40,2,256]{2,1,0:T(2,128)S(1)} %get-tuple-element.14), channel_id=1, source_target_pairs={{1,0},{2,1},{3,2},{4,3},{5,4},{6,5},{7,6},{8,7},{9,8},{10,9},{11,1... | collective-permute-start | bytes 245768 | tf_op jit(solution)/shard_map/ppermute | solution.py:342
  139.1 1.9 %collective-permute-start.2 = (f32[40,2,256]{2,1,0:T(2,128)S(1)}, f32[40,2,256]{2,1,0:T(2,128)S(1)}, u32[]{:S(2)}, u32[]{:S(2)}) collective-permute-start(f32[40,2,256]{2,1,0:T(2,128)S(1)} %get-tuple-element.13), channel_id=1, source_target_pairs={{0,1},{1,2},{2,3},{3,4},{4,5},{5,6},{6,7},{7,8},{8,9},{9,10},{10,1... | collective-permute-start | bytes 245768 | tf_op jit(solution)/shard_map/ppermute | solution.py:342
  141.1 0.0 copy-done.3
  141.1 0.1 fusion.16
  141.1 9.1 %collective-permute-start.5 = (f32[40,2,256]{2,1,0:T(2,128)S(1)}, f32[40,2,256]{2,1,0:T(2,128)S(1)}, u32[]{:S(2)}, u32[]{:S(2)}) collective-permute-start(f32[40,2,256]{2,1,0:T(2,128)S(1)} %get-tuple-element.12), channel_id=1, source_target_pairs={{1,0},{2,1},{3,2},{4,3},{5,4},{6,5},{7,6},{8,7},{9,8},{10,9},{11,1... | collective-permute-start | bytes 245768 | tf_op jit(solution)/shard_map/ppermute | solution.py:342
  150.2 1.9 %collective-permute-start.4 = (f32[40,2,256]{2,1,0:T(2,128)S(1)}, f32[40,2,256]{2,1,0:T(2,128)S(1)}, u32[]{:S(2)}, u32[]{:S(2)}) collective-permute-start(f32[40,2,256]{2,1,0:T(2,128)S(1)} %get-tuple-element.11), channel_id=1, source_target_pairs={{0,1},{1,2},{2,3},{3,4},{4,5},{5,6},{6,7},{7,8},{8,9},{9,10},{10,1... | collective-permute-start | bytes 245768 | tf_op jit(solution)/shard_map/ppermute | solution.py:342
  152.1 0.6 multiply_exponential_fusion.prof_ref
  152.7 0.0 collective-permute-done.3
  152.7 7.7 %collective-permute-done.2 = f32[40,2,256]{2,1,0:T(2,128)S(1)} collective-permute-done((f32[40,2,256]{2,1,0:T(2,128)S(1)}, f32[40,2,256]{2,1,0:T(2,128)S(1)}, u32[]{:S(2)}, u32[]{:S(2)}) %collective-permute-start.2) | collective-permute-done | bytes 81952 | tf_op jit(solution)/shard_map/ppermute | solution.py:342
  160.4 0.7 pad_maximum_fusion.uh_ref
  161.2 1.6 cells.1.d_ref
  162.8 0.8 fusion.18
  163.6 2.4 %collective-permute-start.7 = (f32[2,2,256]{2,1,0:T(2,128)S(1)}, f32[2,2,256]{2,1,0:T(2,128)S(1)}, u32[]{:S(2)}, u32[]{:S(2)}) collective-permute-start(f32[2,2,256]{2,1,0:T(2,128)S(1)} %get-tuple-element.16), channel_id=1, source_target_pairs={{1,0},{2,1},{3,2},{4,3},{5,4},{6,5},{7,6},{8,7},{9,8},{10,9},{11,1... | collective-permute-start | bytes 12296 | tf_op jit(solution)/shard_map/ppermute | solution.py:342
  166.0 2.9 %collective-permute-start.6 = (f32[2,2,256]{2,1,0:T(2,128)S(1)}, f32[2,2,256]{2,1,0:T(2,128)S(1)}, u32[]{:S(2)}, u32[]{:S(2)}) collective-permute-start(f32[2,2,256]{2,1,0:T(2,128)S(1)} %get-tuple-element.15), channel_id=1, source_target_pairs={{0,1},{1,2},{2,3},{3,4},{4,5},{5,6},{6,7},{7,8},{8,9},{9,10},{10,1... | collective-permute-start | bytes 12296 | tf_op jit(solution)/shard_map/ppermute | solution.py:342
  168.9 0.0 collective-permute-done.5
  168.9 0.0 collective-permute-done.4
  168.9 0.7 pad_maximum_fusion.1.vh_ref
  169.6 0.0 collective-permute-done.7
  169.6 6.7 %collective-permute-done.6 = f32[2,2,256]{2,1,0:T(2,128)S(1)} collective-permute-done((f32[2,2,256]{2,1,0:T(2,128)S(1)}, f32[2,2,256]{2,1,0:T(2,128)S(1)}, u32[]{:S(2)}, u32[]{:S(2)}) %collective-permute-start.6) | collective-permute-done | bytes 4128 | tf_op jit(solution)/shard_map/ppermute | solution.py:342
  176.4 0.6 pad_maximum_fusion.2.dh_ref
  177.0 10.2 %ocean.1 = (f32[40,8,256]{2,1,0:T(8,128)}, f32[40,8,256]{2,1,0:T(8,128)}) custom-call(f32[40,8,256]{2,1,0:T(8,128)} %u_ref.1, f32[40,8,256]{2,1,0:T(8,128)} %v_ref.1, f32[2,40,2,256]{3,2,1,0:T(2,128)} %pad_maximum_fusion.uh_ref, f32[2,40,2,256]{3,2,1,0:T(2,128)} %pad_maximum_fusion.1.vh_ref, f32[16,256]{1,0:T(8,128)} %cells.1.d_ref, ...), custom_call_target="tpu_custom_call" | custom-call | tf_op jit(solution)/shard_map/ocean/pallas_call | solution.py:411
  187.1 0.0 all-to-all-done.1
  187.1 0.1 reshape.33
  187.2 0.9 slice_multiply_fusion
  (13 shorter events, 0.1 us)
Async XLA Ops:
  0.6 49.1 %copy-start = (s32[32768]{0:T(1024)S(1)}, s32[32768]{0:T(1024)}, u32[]{:S(2)}) copy-start(s32[32768]{0:T(1024)} %param.13) | copy-start | bytes 393220
  3.3 8.5 %copy-start.4 = (s32[4,1296]{1,0:T(4,128)S(1)}, s32[4,1296]{1,0:T(4,128)}, u32[]{:S(2)}) copy-start(s32[4,1296]{1,0:T(4,128)} %param.14) | copy-start | bytes 62212
  5.1 6.6 %copy-start.7 = (f32[1296]{0:T(1024)S(1)}, f32[1296]{0:T(1024)}, u32[]{:S(2)}) copy-start(f32[1296]{0:T(1024)} %param.15) | copy-start | bytes 15556
  5.9 10.3 %collective-permute-start.1 = (f32[3,128]{1,0:T(4,128)S(1)}, f32[3,128]{1,0:T(4,128)S(1)}, u32[]{:S(2)}, u32[]{:S(2)}) collective-permute-start(f32[3,128]{1,0:T(4,128)S(1)} %get-tuple-element.20), channel_id=1, source_target_pairs={{1,0},{2,1},{3,2},{4,3},{5,4},{6,5},{7,6},{8,7},{9,8},{10,9},{11,1... | collective-permute-start | bytes 4616 | tf_op jit(solution)/shard_map/ppermute | solution.py:342
  7.2 9.0 %collective-permute-start = (f32[3,128]{1,0:T(4,128)S(1)}, f32[3,128]{1,0:T(4,128)S(1)}, u32[]{:S(2)}, u32[]{:S(2)}) collective-permute-start(f32[3,128]{1,0:T(4,128)S(1)} %get-tuple-element.19), channel_id=1, source_target_pairs={{0,1},{1,2},{2,3},{3,4},{4,5},{5,6},{6,7},{7,8},{8,9},{9,10},{10,1... | collective-permute-start | bytes 4616 | tf_op jit(solution)/shard_map/ppermute | solution.py:342
  11.8 0.7 copy-start.5
  13.3 0.7 copy-start.8
  28.8 47.5 %all-to-all-start = ((f32[128,16,128]{2,1,0:T(8,128)}), f32[128,16,128]{2,1,0:T(8,128)S(1)}, u32[]{:S(2)}, u32[]{:S(2)}) async-start(f32[128,16,128]{2,1,0:T(8,128)} %sources.1), calls=%async_computation | async-start | bytes 2097152 | tf_op jit(solution)/shard_map/all_to_all | solution.py:376
  48.3 0.7 copy-start.6
  76.3 1.0 copy-start.1
  123.6 6.4 %copy-start.2 = (f32[40,8,256]{2,1,0:T(8,128)S(1)}, f32[40,8,256]{2,1,0:T(8,128)}, u32[]{:S(2)}) copy-start(f32[40,8,256]{2,1,0:T(8,128)} %u_ref.1) | copy-start | bytes 983044
  123.6 63.6 %all-to-all-start.1 = ((f32[128,16,128]{2,1,0:T(8,128)}), f32[128,16,128]{2,1,0:T(8,128)S(1)}, u32[]{:S(2)}, u32[]{:S(2)}) async-start(f32[128,16,128]{2,1,0:T(8,128)} %get-tuple-element.7), calls=%async_computation.1 | async-start | bytes 2097152 | tf_op jit(solution)/shard_map/all_to_all | solution.py:405
  129.9 11.1 %copy-start.3 = (f32[40,8,256]{2,1,0:T(8,128)S(1)}, f32[40,8,256]{2,1,0:T(8,128)}, u32[]{:S(2)}) copy-start(f32[40,8,256]{2,1,0:T(8,128)} %v_ref.1) | copy-start | bytes 983044
  130.0 22.7 %collective-permute-start.3 = (f32[40,2,256]{2,1,0:T(2,128)S(1)}, f32[40,2,256]{2,1,0:T(2,128)S(1)}, u32[]{:S(2)}, u32[]{:S(2)}) collective-permute-start(f32[40,2,256]{2,1,0:T(2,128)S(1)} %get-tuple-element.14), channel_id=1, source_target_pairs={{1,0},{2,1},{3,2},{4,3},{5,4},{6,5},{7,6},{8,7},{9,8},{10,9},{11,1... | collective-permute-start | bytes 245768 | tf_op jit(solution)/shard_map/ppermute | solution.py:342
  139.1 21.3 %collective-permute-start.2 = (f32[40,2,256]{2,1,0:T(2,128)S(1)}, f32[40,2,256]{2,1,0:T(2,128)S(1)}, u32[]{:S(2)}, u32[]{:S(2)}) collective-permute-start(f32[40,2,256]{2,1,0:T(2,128)S(1)} %get-tuple-element.13), channel_id=1, source_target_pairs={{0,1},{1,2},{2,3},{3,4},{4,5},{5,6},{6,7},{7,8},{8,9},{9,10},{10,1... | collective-permute-start | bytes 245768 | tf_op jit(solution)/shard_map/ppermute | solution.py:342
  141.1 27.8 %collective-permute-start.5 = (f32[40,2,256]{2,1,0:T(2,128)S(1)}, f32[40,2,256]{2,1,0:T(2,128)S(1)}, u32[]{:S(2)}, u32[]{:S(2)}) collective-permute-start(f32[40,2,256]{2,1,0:T(2,128)S(1)} %get-tuple-element.12), channel_id=1, source_target_pairs={{1,0},{2,1},{3,2},{4,3},{5,4},{6,5},{7,6},{8,7},{9,8},{10,9},{11,1... | collective-permute-start | bytes 245768 | tf_op jit(solution)/shard_map/ppermute | solution.py:342
  150.2 18.7 %collective-permute-start.4 = (f32[40,2,256]{2,1,0:T(2,128)S(1)}, f32[40,2,256]{2,1,0:T(2,128)S(1)}, u32[]{:S(2)}, u32[]{:S(2)}) collective-permute-start(f32[40,2,256]{2,1,0:T(2,128)S(1)} %get-tuple-element.11), channel_id=1, source_target_pairs={{0,1},{1,2},{2,3},{3,4},{4,5},{5,6},{6,7},{7,8},{8,9},{9,10},{10,1... | collective-permute-start | bytes 245768 | tf_op jit(solution)/shard_map/ppermute | solution.py:342
  163.6 6.0 %collective-permute-start.7 = (f32[2,2,256]{2,1,0:T(2,128)S(1)}, f32[2,2,256]{2,1,0:T(2,128)S(1)}, u32[]{:S(2)}, u32[]{:S(2)}) collective-permute-start(f32[2,2,256]{2,1,0:T(2,128)S(1)} %get-tuple-element.16), channel_id=1, source_target_pairs={{1,0},{2,1},{3,2},{4,3},{5,4},{6,5},{7,6},{8,7},{9,8},{10,9},{11,1... | collective-permute-start | bytes 12296 | tf_op jit(solution)/shard_map/ppermute | solution.py:342
  166.0 10.4 %collective-permute-start.6 = (f32[2,2,256]{2,1,0:T(2,128)S(1)}, f32[2,2,256]{2,1,0:T(2,128)S(1)}, u32[]{:S(2)}, u32[]{:S(2)}) collective-permute-start(f32[2,2,256]{2,1,0:T(2,128)S(1)} %get-tuple-element.15), channel_id=1, source_target_pairs={{0,1},{1,2},{2,3},{3,4},{4,5},{5,6},{6,7},{7,8},{8,9},{9,10},{10,1... | collective-permute-start | bytes 12296 | tf_op jit(solution)/shard_map/ppermute | solution.py:342

commit v2 on v1

v2 whole, which is shorter than its diff:
```python
import jax
import jax.numpy as jnp
from jax import lax
from jax.experimental import pallas as pl
from jax.experimental.pallas import tpu as pltpu
from jax.sharding import PartitionSpec as P

ND = 36
NZ = 40
KC = 1296
KP = 1408
SHARE = 11
F32, BF16 = jnp.float32, jnp.bfloat16
NT = (((1,), (1,)), ((), ()))
HIGH = lax.Precision.HIGHEST
MESH = pl.DeviceIdType.MESH
VMEM_LIMIT = 56 << 20


def direction_cosines(index):
    theta = ((index % ND).astype(jnp.float32) + 0.5) * (2.0 * jnp.pi / ND)
    return (jnp.cos(theta), jnp.sin(theta))


def split(x):
    hi = x.astype(BF16)
    return hi, (x - hi.astype(F32)).astype(BF16)


def spread_matrix():
    wide = lax.broadcasted_iota(jnp.int32, (128, 768), 1)
    target = ((wide & 255) >> 1) + (wide >> 8) - 1
    return jnp.where(lax.broadcasted_iota(jnp.int32, (128, 768), 0) == target, 1.0, 0.0)


def couple_masks(cp, dev):
    row = (cp >> 7) - dev
    col = (cp & 127) - (lax.broadcasted_iota(jnp.int32, (8, 256), 1) >> 1)
    valid = cp >= 0
    return [
        [jnp.where(valid & (row == dr - 1) & (col == delta - 1), 1.0, 0.0) for delta in range(3)]
        for dr in range(3)
    ]


def build_maps(map_ref, CT, M, MF):
    def step(s, _):
        row = map_ref[pl.ds(s, 1), :]
        n = ((row >> 13) << 7) | (row & 127)
        rl = (row >> 7) & 63
        col = pl.ds(pl.multiple_of(s * 128, 128), 128)
        CT[:, col] = jnp.where(lax.broadcasted_iota(jnp.int32, (256, 128), 0) == n, 1.0, 0.0).astype(BF16)
        mf = jnp.where(lax.broadcasted_iota(jnp.int32, (64, 128), 0) == rl, 1.0, 0.0)
        MF[:, col] = mf
        M[:, col] = mf.astype(BF16)
        return 0

    lax.fori_loop(0, 128, step, 0)


def substep(f, cx, cy, first_lane, last_lane):
    ox = jnp.maximum(cx, 0.0) * f
    ix = jnp.minimum(cx, 0.0) * f
    oy = jnp.maximum(cy, 0.0) * f
    iy = jnp.minimum(cy, 0.0) * f
    rows = f.shape[0]
    nx = jnp.where(last_lane, 0.0, pltpu.roll(ix, 127, 1))
    px = jnp.where(first_lane, 0.0, pltpu.roll(ox, 1, 1))
    ny = pltpu.roll(iy, rows - 1, 0)
    py = pltpu.roll(oy, 1, 0)
    return f - (ox - ix + nx - px) - (oy - iy + ny - py)


S = 8
R = SHARE * 64
ROWS = SHARE + 2
CH = 432


def chunk_offset(i):
    return jnp.where(i % 2 == 1, (i + 1) // 2, 16 - i // 2)


def wait_for(ref, sem):
    pltpu.make_async_copy(ref, ref, sem).wait()


def step_kernel(
    e_ref, mask_ref, trow_ref, col_ref, w_ref, map_ref, speed_ref, cp_ref, u_ref, v_ref, mix_ref, prof_ref,
    ret, ou_ref, ov_ref,
    E, F1, F2, OH, forced_ref, payload, arr, outb, CT, M, MF, LH, acc, dacc, T, G, cur, edge, halo,
    part, pin, cb, curb, ostage, ohalo, B,
    o_send, o_recv, p_send, p_recv, c_send, c_recv, a_send, a_recv, h_send, h_recv, r_send, r_recv,
):
    grp = lax.axis_index("grp")
    dev = lax.axis_index("dev")
    q16 = dev // 8
    linear = grp * 128 + dev
    has_up = linear > 0
    has_down = linear < 255
    up = linear + 255
    up_id = ((up // 128) % 2, up % 128)
    down = linear + 1
    down_id = ((down // 128) % 2, down % 128)

    barrier = pltpu.get_barrier_semaphore()

    def greet(i, _):
        pl.semaphore_signal(barrier, inc=1, device_id=(grp, (dev + i) % 128), device_id_type=MESH)
        return 0

    lax.fori_loop(1, 128, greet, 0)
    pl.semaphore_signal(barrier, inc=1, device_id=(1 - grp, dev), device_id_type=MESH)
    crosses_down = (grp == 0) & (dev == 127)
    crosses_up = (grp == 1) & (dev == 0)

    @pl.when(crosses_down)
    def _():
        pl.semaphore_signal(barrier, inc=1, device_id=down_id, device_id_type=MESH)

    @pl.when(crosses_up)
    def _():
        pl.semaphore_signal(barrier, inc=1, device_id=up_id, device_id_type=MESH)

    masks = couple_masks(cp_ref[...], dev)
    surface = [u_ref[0], v_ref[0]]
    rows = []
    for dr in range(3):
        for q in range(3):
            pieces = []
            for delta in range(3):
                m = masks[dr][delta]
                pieces.append(jnp.sum(m if q == 2 else m * surface[q], axis=0, keepdims=True))
            rows.append(jnp.concatenate(pieces, axis=1))
        rows.append(jnp.zeros((5, 768), F32))
    sums = lax.dot_general(
        jnp.concatenate(rows, axis=0), spread_matrix(), NT, precision=HIGH, preferred_element_type=F32
    )
    for dr in range(3):
        part[dr] = sums[dr * 8 : (dr + 1) * 8]

    def stage_ocean(slot, a, b):
        def level(z, _):
            for side, line in ((0, 0), (1, 7)):
                ostage[slot, side, 0, pl.ds(z, 1), :] = a(z)[line : line + 1]
                ostage[slot, side, 1, pl.ds(z, 1), :] = b(z)[line : line + 1]
            return 0

        lax.fori_loop(0, NZ, level, 0)

    stage_ocean(0, lambda z: u_ref[z], lambda z: v_ref[z])
    build_maps(map_ref, CT, M, MF)

    pl.semaphore_wait(barrier, 128 + jnp.where(crosses_down | crosses_up, 1, 0))

    def ocean_copy(slot, side):
        return pltpu.make_async_remote_copy(
            src_ref=ostage.at[slot, side],
            dst_ref=ohalo.at[slot, 1 - side],
            send_sem=o_send.at[slot, side],
            recv_sem=o_recv.at[slot, 1 - side],
            device_id=up_id if side == 0 else down_id,
            device_id_type=MESH,
        )

    def ocean_start(slot):
        for side, there in ((0, has_up), (1, has_down)):
            @pl.when(there)
            def _(side=side):
                ocean_copy(slot, side).start()

    def ocean_wait(slot):
        for side, there in ((0, has_up), (1, has_down)):
            @pl.when(there)
            def _(side=side):
                wait_for(ostage.at[slot, side], o_send.at[slot, side])
                wait_for(ohalo.at[slot, side], o_recv.at[slot, side])

    def part_copy(side):
        return pltpu.make_async_remote_copy(
            src_ref=part.at[2 * side],
            dst_ref=pin.at[1 - side],
            send_sem=p_send.at[side],
            recv_sem=p_recv.at[1 - side],
            device_id=(grp, (dev + 127 + 2 * side) % 128),
            device_id_type=MESH,
        )

    for side, there in ((0, dev > 0), (1, dev < 127)):
        @pl.when(there)
        def _(side=side):
            part_copy(side).start()

    ocean_start(0)

    tail = jnp.zeros((KP - KC, 256), BF16)
    E[KC:, :] = tail
    F1[KC:, :] = tail
    F2[KC:, :] = tail
    hi, lo = split(e_ref[...])
    E[:KC, :128] = hi
    E[:KC, 128:] = lo

    def gather(i, _):
        rows = pl.ds(pl.multiple_of(i * CH, 16), CH)
        lanes = lax.broadcasted_iota(jnp.int32, (CH, KP), 1).astype(F32)
        e = e_ref[rows, :]
        cols = col_ref[rows, :]
        for m in range(4):
            OH[m * CH : (m + 1) * CH, :] = jnp.where(lanes == cols[:, m : m + 1], 1.0, 0.0).astype(BF16)
        p = jnp.dot(OH[...], E[...], preferred_element_type=F32)
        p = p[:, :128] + p[:, 128:]
        g = [p[m * CH : (m + 1) * CH] for m in range(4)]
        s = cols[:, 4:5]
        ee = e * e
        e2 = 2.0 * e
        a = s * (ee * (g[0] + g[1]) - e2 * g[0] * g[1])
        b = s * (ee * (g[2] + g[3]) - e2 * g[2] * g[3])
        forced_ref[rows, :] = e - (a + b)
        ah, al = split(a)
        bh, bl = split(b)
        F1[rows, :128] = ah
        F1[rows, 128:] = al
        F2[rows, :128] = bh
        F2[rows, 128:] = bl
        return 0

    lax.fori_loop(0, KC // CH, gather, 0)

    for side, there in ((0, dev > 0), (1, dev < 127)):
        @pl.when(there)
        def _(side=side):
            wait_for(part.at[2 * side], p_send.at[side])
            wait_for(pin.at[side], p_recv.at[side])

    total = part[1] + jnp.where(dev > 0, pin[0], 0.0) + jnp.where(dev < 127, pin[1], 0.0)
    speeds = 0.3 * total[0:2] / (total[2:3] + 1.0)
    for q in range(2):
        cb[q] = speeds[q : q + 1]
        curb[dev, q] = speeds[q : q + 1]

    def tell(i, _):
        pltpu.make_async_remote_copy(
            src_ref=cb,
            dst_ref=curb.at[dev],
            send_sem=c_send,
            recv_sem=c_recv,
            device_id=(grp, (dev + i) % 128),
            device_id_type=MESH,
        ).start()
        return 0

    lax.fori_loop(1, 128, tell, 0)

    def scatter(i, _):
        rows = pl.ds(pl.multiple_of(i * CH, 16), CH)
        b = lax.broadcasted_iota(jnp.int32, (CH, KP), 0) + i * CH

        def onehot(m):
            return jnp.where(b == trow_ref[m : m + 1, :], 1.0, 0.0)

        p = jnp.dot((onehot(0) + onehot(1)).astype(BF16), F1[...], preferred_element_type=F32)
        p = p + jnp.dot((onehot(2) + onehot(3)).astype(BF16), F2[...], preferred_element_type=F32)
        forced_ref[rows, :] = mask_ref[...] * (forced_ref[rows, :] + 0.5 * (p[:, :128] + p[:, 128:]))
        return 0

    lax.fori_loop(0, KC // CH, scatter, 0)
    forced_ref[KC:, :] = jnp.zeros((KP - KC, 128), F32)
    drift_own = jnp.dot(w_ref[...], forced_ref[...], precision=HIGH, preferred_element_type=F32)

    def fill(d, _):
        for k in range(SHARE):
            payload[d, k] = forced_ref[pl.ds(d * SHARE + k, 1), :]
        for q in range(2):
            payload[d, SHARE + q] = drift_own[q : q + 1]
        return 0

    lax.fori_loop(0, 128, fill, 0)

    pltpu.make_async_copy(payload.at[dev], arr.at[dev], a_recv.at[q16]).start()

    def send(n, _):
        dest = ((q16 + 16 - chunk_offset(n // 8)) % 16) * 8 + (dev + n) % 8
        pltpu.make_async_remote_copy(
            src_ref=payload.at[dest],
            dst_ref=arr.at[dev],
            send_sem=a_send,
            recv_sem=a_recv.at[q16],
            device_id=(grp, dest),
            device_id_type=MESH,
        ).start()
        return 0

    lax.fori_loop(1, 128, send, 0)

    wait_for(curb.at[pl.ds(0, 127)], c_send)
    wait_for(curb.at[pl.ds(0, 127)], c_recv)

    def place(s, _):
        for q in range(2):
            cur[q, pl.ds(8 + s, 1), :] = curb[s, q]
        return 0

    lax.fori_loop(0, 128, place, 0)
    acc[...] = jnp.zeros_like(acc)
    dacc[...] = jnp.zeros_like(dacc)
    zero_row = jnp.zeros((1, 128), F32)

    def forward(i, _):
        chunk = (q16 + chunk_offset(i)) % 16
        wait_for(arr.at[pl.ds(chunk * S, S)], a_recv.at[chunk])
        drift_rows = []
        for j in range(S):
            s = chunk * S + j
            cols = pl.ds(pl.multiple_of(s * 128, 128), 128)
            c = slice(j * 128, (j + 1) * 128)
            for k in range(SHARE):
                x = jnp.broadcast_to(arr[s, k], (16, 128))
                hi, lo = split(x)
                for q in range(4):
                    m = M[q * 16 : (q + 1) * 16, cols]
                    r = k * 64 + q * 16
                    LH[r : r + 16, c] = m * hi
                    LH[R + r : R + r + 16, c] = m * lo
            row = map_ref[pl.ds(s, 1), :] >> 7
            pieces = []
            for q in range(2):
                x = arr[s, SHARE + q]
                for dr in range(3):
                    pieces.append(jnp.where(row == dev + (dr - 1), x, zero_row))
            pieces += [zero_row, zero_row]
            piece = jnp.concatenate(pieces, axis=0)
            hi = piece.astype(BF16).astype(F32)
            drift_rows.append(jnp.concatenate([hi, piece - hi], axis=0).astype(BF16))
        c = CT[:, pl.ds(pl.multiple_of(chunk * (S * 128), 128), S * 128)]
        acc[...] += lax.dot_general(LH[:R], c, NT, preferred_element_type=F32) + lax.dot_general(
            LH[R:], c, NT, preferred_element_type=F32
        )
        dacc[...] += lax.dot_general(jnp.concatenate(drift_rows, axis=1), c, NT, preferred_element_type=F32)
        return 0

    lax.fori_loop(0, 128 // S, forward, 0)

    top = grp == 0
    for k in range(SHARE):
        low = acc[k * 64 : (k + 1) * 64, 0:128]
        high = acc[k * 64 : (k + 1) * 64, 128:256]
        G[k, 8:72, :] = low
        G[k, 72:136, :] = high
        edge[0, k : k + 1, :] = jnp.where(top, high[63:64], low[0:1])
        edge[1, k : k + 1, :] = jnp.where(top, high[62:63], low[1:2])
    for q in range(2):
        edge[0, SHARE + q : SHARE + q + 1, :] = jnp.where(top, cur[q, 135:136, :], cur[q, 8:9, :])
        edge[1, SHARE + q : SHARE + q + 1, :] = jnp.where(top, cur[q, 134:135, :], cur[q, 9:10, :])
    for r in range(2):
        edge[r, 13:16, :] = jnp.zeros((3, 128), F32)
    exchange = pltpu.make_async_remote_copy(
        src_ref=edge, dst_ref=halo, send_sem=h_send, recv_sem=h_recv, device_id=(1 - grp, dev), device_id_type=MESH
    )
    exchange.start()

    drift = dacc[0:8] + dacc[8:16]
    wave_row = dev + lax.rem(lax.broadcasted_iota(jnp.int32, (8, 128), 0), 3) - 1
    drift = jnp.where(wave_row >= 64, drift[:, 128:], drift[:, :128])
    wide = jnp.dot(drift, spread_matrix(), precision=HIGH, preferred_element_type=F32)
    masks = couple_masks(cp_ref[...], dev)
    cells = []
    for q in range(2):
        sum_q = jnp.zeros((8, 256), F32)
        for dr in range(3):
            for delta in range(3):
                sum_q = sum_q + masks[dr][delta] * wide[q * 3 + dr : q * 3 + dr + 1, delta * 256 : (delta + 1) * 256]
        cells.append(sum_q)
    us, vs = cells

    oline = lax.broadcasted_iota(jnp.int32, (8, 256), 0)
    olane = lax.broadcasted_iota(jnp.int32, (8, 256), 1)
    coriolis = 0.5 + (linear * 8 + oline).astype(F32) / 2048.0
    fvs, fus = coriolis * vs, coriolis * us

    def ocean_step(slot, source, emit):
        def lap(a, z, q):
            above = jnp.where(has_up, ohalo[slot, 0, q, pl.ds(z, 1), :], 0.0)
            below = jnp.where(has_down, ohalo[slot, 1, q, pl.ds(z, 1), :], 0.0)
            r = jnp.where(olane == 255, 0.0, pltpu.roll(a, 255, 1)) + jnp.where(olane == 0, 0.0, pltpu.roll(a, 1, 1))
            r = r + jnp.where(oline == 0, above, pltpu.roll(a, 1, 0)) + jnp.where(oline == 7, below, pltpu.roll(a, 7, 0))
            return r - 4.0 * a

        def level(z, carry):
            pu, pv = carry
            u, v = source(0, z), source(1, z)
            zn = jnp.minimum(z + 1, NZ - 1)
            m0 = mix_ref[0, z]
            m1 = jnp.where(z == NZ - 1, 0.0, mix_ref[0, zn])
            nu, nv = source(0, zn), source(1, zn)
            p = prof_ref[0, z]
            wu = m1 * (nu - u) - m0 * (u - pu)
            wv = m1 * (nv - v) - m0 * (v - pv)
            emit(
                z,
                u + 0.2 * (0.2 * lap(u, z, 0) + wu + coriolis * v + p * fvs),
                v + 0.2 * (0.2 * lap(v, z, 1) + wv - coriolis * u - p * fus),
            )
            return u, v

        zero = jnp.zeros((8, 256), F32)
        lax.fori_loop(0, NZ, level, (zero, zero))

    def emit1(z, u, v):
        B[0, z] = u
        B[1, z] = v

    def emit2(z, u, v):
        ou_ref[z] = u
        ov_ref[z] = v

    ocean_wait(0)
    ocean_step(0, lambda q, z: (u_ref, v_ref)[q][z], emit1)
    stage_ocean(1, lambda z: B[0, z], lambda z: B[1, z])
    ocean_start(1)

    exchange.wait()
    below_on = jnp.where(top, 1.0, 0.0)
    above_on = 1.0 - below_on
    blank = jnp.zeros((6, 128), F32)

    def pad(dst, k, index):
        h0 = halo[0, k : k + 1, :]
        h1 = halo[1, k : k + 1, :]
        dst[index, 0:8, :] = jnp.concatenate([blank, h1, h0], axis=0) * above_on
        dst[index, 136:144, :] = jnp.concatenate([h0, h1, blank], axis=0) * below_on

    for k in range(SHARE):
        pad(G, k, k)
    for q in range(2):
        pad(cur, SHARE + q, q)
    lane = lax.broadcasted_iota(jnp.int32, (144, 128), 1)
    line = lax.broadcasted_iota(jnp.int32, (144, 128), 0)
    first_lane, last_lane = lane == 0, lane == 127
    keep = jnp.where(line < 8, above_on, jnp.where(line >= 136, below_on, 1.0))

    def propagate(k, _):
        cx = cur[0] + speed_ref[0, k]
        cy = cur[1] + speed_ref[1, k]
        f = substep(G[k], cx, cy, first_lane, last_lane) * keep
        f = substep(f, cx, cy, first_lane, last_lane)
        hi, lo = split(f[8:136])
        r = pl.multiple_of(k * 64, 64)
        for h in range(2):
            LH[pl.ds(r, 64), h * 128 : (h + 1) * 128] = hi[h * 64 : (h + 1) * 64]
            LH[pl.ds(R + r, 64), h * 128 : (h + 1) * 128] = lo[h * 64 : (h + 1) * 64]
        return 0

    lax.fori_loop(0, SHARE, propagate, 0)

    def backward(t, _):
        i = 15 - t
        chunk = (q16 + 16 - chunk_offset(i)) % 16
        c = CT[:, pl.ds(pl.multiple_of(chunk * (S * 128), 128), S * 128)]
        T[...] = jnp.dot(LH[:R, 0:256], c, preferred_element_type=F32) + jnp.dot(
            LH[R:, 0:256], c, preferred_element_type=F32
        )
        for j in range(S):
            s = chunk * S + j
            m = MF[:, pl.ds(pl.multiple_of(s * 128, 128), 128)]
            for k in range(SHARE):
                outb[s, k] = jnp.sum(T[k * 64 : (k + 1) * 64, j * 128 : (j + 1) * 128] * m, axis=0, keepdims=True)

        def post(j, _):
            s = chunk * S + j

            @pl.when(s != dev)
            def _():
                pltpu.make_async_remote_copy(
                    src_ref=outb.at[s],
                    dst_ref=ret.at[pl.ds(dev * SHARE, SHARE)],
                    send_sem=r_send,
                    recv_sem=r_recv,
                    device_id=(grp, s),
                    device_id_type=MESH,
                ).start()

            return 0

        lax.fori_loop(0, S, post, 0)
        return 0

    lax.fori_loop(0, 128 // S, backward, 0)
    for k in range(SHARE):
        ret[dev * SHARE + k] = outb[dev, k]

    ocean_wait(1)
    ocean_step(1, lambda q, z: B[q, z], emit2)

    wait_for(payload.at[pl.ds(0, 127)], a_send)
    wait_for(outb.at[pl.ds(0, 127)], r_send)
    wait_for(ret.at[pl.ds(0, 127 * SHARE)], r_recv)


def body(spectra, sea_mask, card_map, dia_table, dia_coef, speed, stokes_weight, couple_point, ocean_u, ocean_v, mixing):
    group = lax.axis_index("grp")
    device = lax.axis_index("dev")
    sds = jax.ShapeDtypeStruct
    cosine, sine = direction_cosines(jnp.arange(KC, dtype=jnp.int32))
    weights = jnp.pad(jnp.stack([stokes_weight * cosine, stokes_weight * sine]), ((0, 6), (0, KP - KC)))
    trow = jnp.pad(dia_table, ((0, 4), (0, KP - KC)), constant_values=-1)
    col = jnp.concatenate([dia_table.T.astype(F32), dia_coef[:, None], jnp.zeros((KC, 3), F32)], axis=1)
    mask = sea_mask.astype(F32)[None, :]
    map2d = lax.dynamic_slice_in_dim(card_map, group * 16384, 16384, 0).reshape(128, 128)
    speeds = jnp.pad(jnp.stack([speed * cosine, speed * sine]), ((0, 0), (0, KP - KC)))
    speeds = jnp.pad(lax.dynamic_slice_in_dim(speeds, device * SHARE, SHARE, 1), ((0, 0), (0, 16 - SHARE)))
    profile = jnp.exp(-3.0 * (jnp.arange(NZ, dtype=jnp.int32).astype(F32) + 0.5) / NZ)[None, :]
    vmem = pl.BlockSpec(memory_space=pltpu.VMEM)
    smem = pl.BlockSpec(memory_space=pltpu.SMEM)
    dma = pltpu.SemaphoreType.DMA
    scratch = [
        pltpu.VMEM((KP, 256), BF16),
        pltpu.VMEM((KP, 256), BF16),
        pltpu.VMEM((KP, 256), BF16),
        pltpu.VMEM((4 * CH, KP), BF16),
        pltpu.VMEM((KP, 128), F32),
        pltpu.VMEM((128, ROWS, 1, 128), F32),
        pltpu.VMEM((128, ROWS, 1, 128), F32),
        pltpu.VMEM((128, SHARE, 1, 128), F32),
        pltpu.VMEM((256, 16384), BF16),
        pltpu.VMEM((64, 16384), BF16),
        pltpu.VMEM((64, 16384), F32),
        pltpu.VMEM((2 * R, S * 128), BF16),
        pltpu.VMEM((R, 256), F32),
        pltpu.VMEM((16, 256), F32),
        pltpu.VMEM((R, S * 128), F32),
        pltpu.VMEM((SHARE, 144, 128), F32),
        pltpu.VMEM((2, 144, 128), F32),
        pltpu.VMEM((2, 16, 128), F32),
        pltpu.VMEM((2, 16, 128), F32),
        pltpu.VMEM((3, 8, 128), F32),
        pltpu.VMEM((2, 8, 128), F32),
        pltpu.VMEM((2, 1, 128), F32),
        pltpu.VMEM((128, 2, 1, 128), F32),
        pltpu.VMEM((2, 2, 2, NZ, 256), F32),
        pltpu.VMEM((2, 2, 2, NZ, 256), F32),
        pltpu.VMEM((2, NZ, 8, 256), F32),
        dma((2, 2)), dma((2, 2)), dma((2,)), dma((2,)), dma, dma, dma, dma((16,)), dma, dma, dma, dma,
    ]
    ret, new_u, new_v = pl.pallas_call(
        step_kernel,
        out_shape=(sds((KP, 1, 128), F32), sds((NZ, 8, 256), F32), sds((NZ, 8, 256), F32)),
        in_specs=[vmem] * 6 + [smem] + [vmem] * 3 + [smem] * 2,
        out_specs=(vmem, vmem, vmem),
        scratch_shapes=scratch,
        compiler_params=pltpu.CompilerParams(
            vmem_limit_bytes=VMEM_LIMIT, collective_id=0, has_side_effects=True
        ),
        name="step",
    )(spectra, mask, trow, col, weights, map2d, speeds, couple_point, ocean_u, ocean_v, mixing[None, :], profile)
    new_spectra = ret.reshape(KP, 128)[:KC] * mask
    return (new_spectra, new_u, new_v)


def solution(mesh):
    both = ("grp", "dev")
    in_specs = (P(None, both), P(both), P(), P(), P(), P(), P(), P(both, None), P(None, both, None), P(None, both, None), P())
    out_specs = (P(None, both), P(None, both, None), P(None, both, None))
    return jax.shard_map(body, mesh=mesh, in_specs=in_specs, out_specs=out_specs, check_vma=False)
```

time: 189 us -> 93.6 us (0.50)
  starting transfers between devices: 59 us -> 0 us
  waiting for transfers between devices: 40.4 us -> 0 us
  Pallas kernels: 71.2 us -> 80.8 us
  local copies, waits for them, and re-layouts: 10.9 us -> 7.53 us
  other arithmetic: 5.68 us -> 2.89 us
    ppermute x8 -> x0, starting transfers between devices: 33.2 us -> none  [the longest x4 21.9 us: neighbours(): lax.ppermute(first, axis, [(b, a) for a, b in up])]
    all_to_all x2 -> x0, waiting for transfers between devices: 25.9 us -> none  [the longest x1 25.9 us: body(): lax.all_to_all(payload, 'dev', split_axis=0, concat_axis=0, tiled=True)]
    all_to_all x2 -> x0, starting transfers between devices: 25.8 us -> none  [the longest x1 19.5 us: body(): lax.all_to_all(payload, 'dev', split_axis=0, concat_axis=0, tiled=True)]
    ppermute x8 -> x0, waiting for transfers between devices: 14.4 us -> none  [the longest x4 14.4 us: neighbours(): lax.ppermute(last, axis, up)]
    pallas_call x5 -> x1, Pallas kernels: 71.2 us -> 80.8 us  [body(): pl.pallas_call(step_kernel, out_shape=(sds((KP, 1, 128), F32), sds((NZ, 8...]
    squeeze x2 -> x0, local copies, waits for them, and re-layouts: 2.63 us -> none  [the longest x1 1.33 us: body(): ocean_u[0]]
    another operation x3 -> x0, other arithmetic: 2.07 us -> none  [the longest x1 0.74 us: body(): uh = jnp.stack(swap(ocean_u[:, 6:8], ocean_u[:, 0:2]))]
  transfers between devices with their start and end apart: 10 -> 0, of which waited for: 3 -> 0; matrix products, arithmetic and copies ran while one was open for 4% -> 0% of each run, Pallas kernels for 6% -> 0%
where the time goes in v2:
time: 93.6 us; the launch traced here: 92 us
  Pallas kernels  80.8 us (86%)
  local copies, waits for them, and re-layouts  7.53 us (8%)
  other arithmetic  2.89 us (3%)
    pallas_call x1, Pallas kernels, body(): pl.pallas_call(step_kernel, out_shape=(sds((KP, 1, 128), F32), sds((NZ, 8...  80.8 us
    unnamed x18, local copies, waits for them, and re-layouts  3.38 us

profile of v2, /device:TPU:1, one launch (start us, length us, event | category | flops | bytes accessed | tf_op | source)
XLA Modules:
  0.0 92.0 jit_solution(5157781373968457687)
XLA Ops:
  0.6 0.0 copy-start
  0.7 0.0 copy-start.6
  0.7 0.1 pad.26.clone
  0.7 0.0 copy-start.7
  0.7 0.6 multiply_exponential_fusion.prof_ref
  1.4 0.0 copy-done.7
  1.4 0.5 fusion.15
  1.9 0.0 copy-start.4
  1.9 0.0 copy-done.6
  1.9 0.7 copy-done.4
  2.6 0.1 fusion.9
  2.7 0.0 copy-start.5
  2.7 0.1 fusion.13
  2.8 0.6 pad.19.speed_ref
  3.4 0.0 copy-done.5
  3.4 0.0 copy-start.3
  3.4 0.1 fusion.8
  3.5 0.6 copy-done.3
  4.1 0.1 maximum_maximum_fusion
  4.2 0.6 select_maximum_fusion.w_ref
  4.8 0.6 pad.16.trow_ref
  5.4 0.0 copy-done
  5.5 0.6 dynamic-slice_bitcast_fusion.map_ref
  6.1 1.1 %copy.17.col_ref = f32[1296,8]{1,0:T(8,128)} copy(f32[1296,8]{0,1:T(8,128)S(1)} %maximum_maximum_fusion) | data formatting | bytes 82944 | tf_op jit(solution)/shard_map/concatenate | solution.py:507
  7.2 80.8 %step.1 = (f32[1408,1,128]{2,1,0:T(1,128)}, f32[40,8,256]{2,1,0:T(8,128)}, f32[40,8,256]{2,1,0:T(8,128)}) custom-call(f32[1296,128]{1,0:T(8,128)} %e_ref.1, f32[1,128]{1,0:T(1,128)} %get-tuple-element.14.mask_ref, s32[8,1408]{1,0:T(8,128)} %pad.16.trow_ref, f32[1296,8]{1,0:T(8,128)} %copy.17.col_ref, f32[8,1408]{1,0:T(8,128)} %select_maximum_fusion.w_ref, ...), custom_call_target="tpu_custom_call" | custom-call | tf_op jit(solution)/shard_map/step/pallas_call | solution.py:545
  88.0 1.1 %slice.6 = f32[1296,1,128]{2,1,0:T(1,128)S(1)} slice(f32[1408,1,128]{2,1,0:T(1,128)} %get-tuple-element.6), slice={[0:1296], [0:1], [0:128]} | slice | bytes 1327104 | tf_op jit(solution)/shard_map/slice | solution.py:556
  89.1 0.0 copy-start.2
  89.2 0.9 broadcast_multiply_fusion
  90.0 0.1 copy-done.2
  90.2 0.0 copy-start.1
  90.2 0.7 copy.20
  90.9 0.4 copy-done.1
  91.3 0.7 copy.21
  (7 shorter events, 0.0 us)
Async XLA Ops:
  0.6 4.8 %copy-start = (s32[32768]{0:T(1024)S(1)}, s32[32768]{0:T(1024)}, u32[]{:S(2)}) copy-start(s32[32768]{0:T(1024)} %param.13) | copy-start | bytes 393220
  0.7 1.2 %copy-start.6 = (f32[1296]{0:T(1024)S(1)}, f32[1296]{0:T(1024)}, u32[]{:S(2)}) copy-start(f32[1296]{0:T(1024)} %param.15) | copy-start | bytes 15556
  0.7 0.7 copy-start.7
  1.9 0.7 copy-start.4
  2.7 0.7 copy-start.5
  3.4 0.7 copy-start.3
  89.1 1.0 %copy-start.2 = (f32[40,8,256]{2,1,0:T(8,128)S(1)}, f32[40,8,256]{2,1,0:T(8,128)}, u32[]{:S(2)}) copy-start(f32[40,8,256]{2,1,0:T(8,128)} %get-tuple-element.19) | copy-start | bytes 983044
  90.2 1.1 %copy-start.1 = (f32[40,8,256]{2,1,0:T(8,128)S(1)}, f32[40,8,256]{2,1,0:T(8,128)}, u32[]{:S(2)}) copy-start(f32[40,8,256]{2,1,0:T(8,128)} %get-tuple-element.20) | copy-start | bytes 983044

commit v3 on v2

v3 whole, which is shorter than its diff:
```python
import jax
import jax.numpy as jnp
import numpy as np
from jax import lax
from jax.experimental import pallas as pl
from jax.experimental.pallas import tpu as pltpu
from jax.sharding import PartitionSpec as P

ND = 36
NZ = 40
KC = 1296
KP = 1408
FIRST, SECOND = 5, 6
SHARE = FIRST + SECOND
F32, BF16 = jnp.float32, jnp.bfloat16
NT = (((1,), (1,)), ((), ()))
HIGH = lax.Precision.HIGHEST
MESH = pl.DeviceIdType.MESH
VMEM_LIMIT = 56 << 20


def direction_table():
    theta = (np.arange(ND) + 0.5) * (2.0 * np.pi / ND)
    return np.stack([np.cos(theta), np.sin(theta)]).astype(np.float32)


def split(x):
    hi = x.astype(BF16)
    return hi, (x - hi.astype(F32)).astype(BF16)


def spread_matrix():
    wide = lax.broadcasted_iota(jnp.int32, (128, 768), 1)
    target = ((wide & 255) >> 1) + (wide >> 8) - 1
    return jnp.where(lax.broadcasted_iota(jnp.int32, (128, 768), 0) == target, 1.0, 0.0)


def couple_masks(cp, dev):
    row = (cp >> 7) - dev
    col = (cp & 127) - (lax.broadcasted_iota(jnp.int32, (8, 256), 1) >> 1)
    valid = cp >= 0
    return [
        [jnp.where(valid & (row == dr - 1) & (col == delta - 1), 1.0, 0.0) for delta in range(3)]
        for dr in range(3)
    ]


def build_maps(map_ref, base, CT, M, MF):
    def step(s, _):
        row = map_ref[pl.ds(base + s, 1), :]
        n = ((row >> 13) << 7) | (row & 127)
        rl = (row >> 7) & 63
        col = pl.ds(pl.multiple_of(s * 128, 128), 128)
        CT[:, col] = jnp.where(lax.broadcasted_iota(jnp.int32, (256, 128), 0) == n, 1.0, 0.0).astype(BF16)
        mf = jnp.where(lax.broadcasted_iota(jnp.int32, (64, 128), 0) == rl, 1.0, 0.0)
        MF[:, col] = mf
        M[:, col] = mf.astype(BF16)
        return 0

    lax.fori_loop(0, 128, step, 0)


def substep(f, cx, cy, first_lane, last_lane):
    ox = jnp.maximum(cx, 0.0) * f
    ix = jnp.minimum(cx, 0.0) * f
    oy = jnp.maximum(cy, 0.0) * f
    iy = jnp.minimum(cy, 0.0) * f
    rows = f.shape[0]
    nx = jnp.where(last_lane, 0.0, pltpu.roll(ix, 127, 1))
    px = jnp.where(first_lane, 0.0, pltpu.roll(ox, 1, 1))
    ny = pltpu.roll(iy, rows - 1, 0)
    py = pltpu.roll(oy, 1, 0)
    return f - (ox - ix + nx - px) - (oy - iy + ny - py)


S = 8
ROWS = 10
CH = 432


def chunk_offset(i):
    return jnp.where((i & 1) == 1, (i + 1) >> 1, 16 - (i >> 1))


def wait_for(ref, sem):
    pltpu.make_async_copy(ref, ref, sem).wait()


def step_kernel(
    e_ref, mask_ref, table_ref, coef_ref, stokes_ref, trig_ref, map_ref, speed_ref, dirs_ref, cp_ref, u_ref, v_ref,
    mix_ref, prof_ref,
    ret, ret_last, ou_ref, ov_ref,
    E, F1, F2, OH, forced_ref, trow_ref, col_ref, pay1, pay2, arr1, arr2, out1, out2, CT, M, MF, LH, FF1, FF2, acc, dacc, T,
    G, cur, edge, halo, part, pin, ostage, ohalo, B,
    o_send, o_recv, p_send, p_recv, a1_send, a1_recv, a2_send, a2_recv, a3_send,
    h_send, h_recv, r_send, r_recv,
):
    grp = lax.axis_index("grp")
    dev = lax.axis_index("dev")
    q16 = dev >> 3
    owner = (dev & 7) == 0
    linear = grp * 128 + dev
    has_up = linear > 0
    has_down = linear < 255
    up = linear + 255
    up_id = ((up // 128) % 2, up % 128)
    down = linear + 1
    down_id = ((down // 128) % 2, down % 128)

    barrier = pltpu.get_barrier_semaphore()

    def greet(i, _):
        pl.semaphore_signal(barrier, inc=1, device_id=(grp, (dev + i) & 127), device_id_type=MESH)
        return 0

    lax.fori_loop(1, 128, greet, 0)
    pl.semaphore_signal(barrier, inc=1, device_id=(1 - grp, dev), device_id_type=MESH)
    crosses_down = (grp == 0) & (dev == 127)
    crosses_up = (grp == 1) & (dev == 0)

    @pl.when(crosses_down)
    def _():
        pl.semaphore_signal(barrier, inc=1, device_id=down_id, device_id_type=MESH)

    @pl.when(crosses_up)
    def _():
        pl.semaphore_signal(barrier, inc=1, device_id=up_id, device_id_type=MESH)

    masks = couple_masks(cp_ref[...], dev)
    surface = [u_ref[0], v_ref[0]]
    rows = []
    for dr in range(3):
        for q in range(3):
            pieces = []
            for delta in range(3):
                m = masks[dr][delta]
                pieces.append(jnp.sum(m if q == 2 else m * surface[q], axis=0, keepdims=True))
            rows.append(jnp.concatenate(pieces, axis=1))
        rows.append(jnp.zeros((5, 768), F32))
    sums = lax.dot_general(
        jnp.concatenate(rows, axis=0), spread_matrix(), NT, precision=HIGH, preferred_element_type=F32
    )
    for dr in range(3):
        part[dr] = sums[dr * 8 : (dr + 1) * 8]

    def stage_ocean(slot, a, b):
        def level(z, _):
            for side, line in ((0, 0), (1, 7)):
                ostage[slot, side, 0, pl.ds(z, 1), :] = a(z)[line : line + 1]
                ostage[slot, side, 1, pl.ds(z, 1), :] = b(z)[line : line + 1]
            return 0

        lax.fori_loop(0, NZ, level, 0)

    stage_ocean(0, lambda z: u_ref[z], lambda z: v_ref[z])
    build_maps(map_ref, grp * 128, CT, M, MF)

    trow_ref[...] = jnp.full((8, KP), -1, jnp.int32)
    trow_ref[0:4, :KC] = table_ref[...]
    OH_rows = trow_ref[...].astype(F32)
    line8 = lax.broadcasted_iota(jnp.int32, (8, KP), 0)
    wide_coef = jnp.concatenate([coef_ref[...], jnp.zeros((1, KP - KC), F32)], axis=1)
    col_ref[...] = jnp.transpose(jnp.where(line8 < 4, OH_rows, wide_coef))
    tail = jnp.zeros((KP - KC, 256), BF16)
    E[KC:, :] = tail
    F1[KC:, :] = tail
    F2[KC:, :] = tail
    hi, lo = split(e_ref[...])
    E[:KC, :128] = hi
    E[:KC, 128:] = lo

    def gather(i, _):
        rows = pl.ds(pl.multiple_of(i * CH, 16), CH)
        lanes = lax.broadcasted_iota(jnp.int32, (CH, KP), 1).astype(F32)
        e = e_ref[rows, :]
        cols = col_ref[rows, :]
        for m in range(4):
            OH[m * CH : (m + 1) * CH, :] = jnp.where(lanes == cols[:, m : m + 1], 1.0, 0.0).astype(BF16)
        p = jnp.dot(OH[...], E[...], preferred_element_type=F32)
        p = p[:, :128] + p[:, 128:]
        g = [p[m * CH : (m + 1) * CH] for m in range(4)]
        s = cols[:, 4:5]
        ee = e * e
        e2 = 2.0 * e
        a = s * (ee * (g[0] + g[1]) - e2 * g[0] * g[1])
        b = s * (ee * (g[2] + g[3]) - e2 * g[2] * g[3])
        forced_ref[rows, :] = e - (a + b)
        ah, al = split(a)
        bh, bl = split(b)
        F1[rows, :128] = ah
        F1[rows, 128:] = al
        F2[rows, :128] = bh
        F2[rows, 128:] = bl
        return 0

    lax.fori_loop(0, KC // CH, gather, 0)

    mask = mask_ref[...].astype(F32)

    def scatter(first, count):
        rows = slice(first, first + count)
        b = lax.broadcasted_iota(jnp.int32, (count, KP), 0) + first

        def onehot(m):
            return jnp.where(b == trow_ref[m : m + 1, :], 1.0, 0.0)

        p = jnp.dot((onehot(0) + onehot(1)).astype(BF16), F1[...], preferred_element_type=F32)
        p = p + jnp.dot((onehot(2) + onehot(3)).astype(BF16), F2[...], preferred_element_type=F32)
        forced_ref[rows, :] = mask * (forced_ref[rows, :] + 0.5 * (p[:, :128] + p[:, 128:]))

    def destination(n):
        return (((q16 - chunk_offset(n >> 3)) & 15) << 3) | ((dev + n) & 7)

    scatter(0, FIRST * 128)

    scatter(FIRST * 128, KC - FIRST * 128)
    forced_ref[KC:, :] = jnp.zeros((KP - KC, 128), F32)
    weights = trig_ref[...] * jnp.concatenate([stokes_ref[...], jnp.zeros((1, KP - KC), F32)], axis=1)
    drift_own = jnp.dot(weights, forced_ref[...], precision=HIGH, preferred_element_type=F32)

    def ocean_copy(slot, side):
        return pltpu.make_async_remote_copy(
            src_ref=ostage.at[slot, side],
            dst_ref=ohalo.at[slot, 1 - side],
            send_sem=o_send.at[slot, side],
            recv_sem=o_recv.at[slot, 1 - side],
            device_id=up_id if side == 0 else down_id,
            device_id_type=MESH,
        )

    def ocean_start(slot):
        for side, there in ((0, has_up), (1, has_down)):
            @pl.when(there)
            def _(side=side):
                ocean_copy(slot, side).start()

    def ocean_wait(slot):
        for side, there in ((0, has_up), (1, has_down)):
            @pl.when(there)
            def _(side=side):
                wait_for(ostage.at[slot, side], o_send.at[slot, side])
                wait_for(ohalo.at[slot, side], o_recv.at[slot, side])

    def part_copy(side):
        return pltpu.make_async_remote_copy(
            src_ref=part.at[2 * side],
            dst_ref=pin.at[1 - side],
            send_sem=p_send.at[side],
            recv_sem=p_recv.at[1 - side],
            device_id=(grp, (dev + 127 + 2 * side) & 127),
            device_id_type=MESH,
        )

    pl.semaphore_wait(barrier, 128 + jnp.where(crosses_down | crosses_up, 1, 0))

    for side, there in ((0, dev > 0), (1, dev < 127)):
        @pl.when(there)
        def _(side=side):
            part_copy(side).start()

    def fill1(t, _):
        for r in range(4):
            d = t * 4 + r
            for k in range(FIRST):
                pay1[d, k] = forced_ref[pl.ds(k * 128 + d, 1), :]
        return 0

    lax.fori_loop(0, 32, fill1, 0)
    pltpu.make_async_copy(pay1.at[dev], arr1.at[dev], a1_recv.at[q16]).start()

    def send1(n, _):
        dest = destination(n)
        pltpu.make_async_remote_copy(
            src_ref=pay1.at[dest],
            dst_ref=arr1.at[dev],
            send_sem=a1_send,
            recv_sem=a1_recv.at[q16],
            device_id=(grp, dest),
            device_id_type=MESH,
        ).start()
        return 0

    lax.fori_loop(1, 128, send1, 0)
    ocean_start(0)

    for side, there in ((0, dev > 0), (1, dev < 127)):
        @pl.when(there)
        def _(side=side):
            wait_for(part.at[2 * side], p_send.at[side])
            wait_for(pin.at[side], p_recv.at[side])

    total = part[1] + jnp.where(dev > 0, pin[0], 0.0) + jnp.where(dev < 127, pin[1], 0.0)
    speeds = 0.3 * total[0:2] / (total[2:3] + 1.0)

    def fill2(t, _):
        for r in range(8):
            d = t * 8 + r
            for k in range(5):
                pay2[d, k] = forced_ref[pl.ds((FIRST + k) * 128 + d, 1), :]
            for q in range(2):
                pay2[d, 5 + q] = drift_own[q : q + 1]
                pay2[d, 7 + q] = speeds[q : q + 1]
        pay2[t * 8, 9] = forced_ref[pl.ds(1280 + t, 1), :]
        return 0

    lax.fori_loop(0, 16, fill2, 0)

    @pl.when(owner)
    def _():
        pltpu.make_async_copy(pay2.at[dev], arr2.at[dev], a2_recv.at[q16]).start()

    @pl.when(jnp.logical_not(owner))
    def _():
        pltpu.make_async_copy(pay2.at[dev, pl.ds(0, 9)], arr2.at[dev, pl.ds(0, 9)], a2_recv.at[q16]).start()

    def send2(n, _):
        dest = destination(n)

        @pl.when((dest & 7) == 0)
        def _():
            pltpu.make_async_remote_copy(
                src_ref=pay2.at[dest],
                dst_ref=arr2.at[dev],
                send_sem=a3_send,
                recv_sem=a2_recv.at[q16],
                device_id=(grp, dest),
                device_id_type=MESH,
            ).start()

        @pl.when((dest & 7) != 0)
        def _():
            pltpu.make_async_remote_copy(
                src_ref=pay2.at[dest, pl.ds(0, 9)],
                dst_ref=arr2.at[dev, pl.ds(0, 9)],
                send_sem=a2_send,
                recv_sem=a2_recv.at[q16],
                device_id=(grp, dest),
                device_id_type=MESH,
            ).start()

        return 0

    lax.fori_loop(1, 128, send2, 0)

    zero_row = jnp.zeros((1, 128), F32)
    top = grp == 0

    def forward(count, arrived, target, extra):
        R = count * 64
        target[...] = jnp.zeros_like(target)

        def chunk_step(i, _):
            chunk = (q16 + chunk_offset(i)) & 15
            if extra:
                @pl.when(owner)
                def _():
                    wait_for(arr2.at[pl.ds(chunk * S, S)], a2_recv.at[chunk])

                @pl.when(jnp.logical_not(owner))
                def _():
                    wait_for(arr2.at[pl.ds(chunk * S, S), pl.ds(0, 9)], a2_recv.at[chunk])
            else:
                wait_for(arr1.at[pl.ds(chunk * S, S)], a1_recv.at[chunk])
            for j in range(S):
                s = chunk * S + j
                cols = pl.ds(pl.multiple_of(s * 128, 128), 128)
                c = slice(j * 128, (j + 1) * 128)
                for k in range(count):
                    slot = 9 if k == 5 else k
                    x = jnp.broadcast_to(arrived[s, slot], (16, 128))
                    hi, lo = split(x)
                    for q in range(4):
                        m = M[q * 16 : (q + 1) * 16, cols]
                        r = k * 64 + q * 16
                        LH[r : r + 16, c] = m * hi
                        LH[R + r : R + r + 16, c] = m * lo
                if extra:
                    row = map_ref[pl.ds(grp * 128 + s, 1), :] >> 7
                    pieces = []
                    for q in range(2):
                        cur[q, pl.ds(8 + s, 1), :] = arrived[s, 7 + q]
                        x = arrived[s, 5 + q]
                        for dr in range(3):
                            pieces.append(jnp.where(row == dev + (dr - 1), x, zero_row))
                    pieces += [zero_row, zero_row]
                    piece = jnp.concatenate(pieces, axis=0)
                    hi = piece.astype(BF16).astype(F32)
                    LH[2 * R : 2 * R + 16, c] = jnp.concatenate([hi, piece - hi], axis=0).astype(BF16)
            c = CT[:, pl.ds(pl.multiple_of(chunk * (S * 128), 128), S * 128)]
            d = lax.dot_general(LH[: 2 * R + (16 if extra else 0)], c, NT, preferred_element_type=F32)
            target[:R] += d[:R] + d[R : 2 * R]
            if extra:
                dacc[...] += d[2 * R :]
            return 0

        lax.fori_loop(0, 128 // S, chunk_step, 0)

    def boundary(part, first, count):
        for k in range(count):
            low = acc[k * 64 : (k + 1) * 64, 0:128]
            high = acc[k * 64 : (k + 1) * 64, 128:256]
            G[first + k, 8:72, :] = low
            G[first + k, 72:136, :] = high
            edge[part, 0, k : k + 1, :] = jnp.where(top, high[63:64], low[0:1])
            edge[part, 1, k : k + 1, :] = jnp.where(top, high[62:63], low[1:2])
        for r in range(2):
            if part == 0:
                edge[part, r, count:8, :] = jnp.zeros((8 - count, 128), F32)
            else:
                for q in range(2):
                    edge[part, r, 6 + q : 7 + q, :] = jnp.where(
                        top, cur[q, 135 - r : 136 - r, :], cur[q, 8 + r : 9 + r, :]
                    )
        exchange(part).start()

    def exchange(part):
        return pltpu.make_async_remote_copy(
            src_ref=edge.at[part],
            dst_ref=halo.at[part],
            send_sem=h_send.at[part],
            recv_sem=h_recv.at[part],
            device_id=(1 - grp, dev),
            device_id_type=MESH,
        )

    below_on = jnp.where(top, 1.0, 0.0)
    above_on = 1.0 - below_on
    blank = jnp.zeros((6, 128), F32)

    def pad(dst, index, part, k):
        h0 = halo[part, 0, k : k + 1, :]
        h1 = halo[part, 1, k : k + 1, :]
        dst[index, 0:8, :] = jnp.concatenate([blank, h1, h0], axis=0) * above_on
        dst[index, 136:144, :] = jnp.concatenate([h0, h1, blank], axis=0) * below_on

    lane = lax.broadcasted_iota(jnp.int32, (144, 128), 1)
    line = lax.broadcasted_iota(jnp.int32, (144, 128), 0)
    first_lane, last_lane = lane == 0, lane == 127
    keep = jnp.where(line < 8, above_on, jnp.where(line >= 136, below_on, 1.0))

    def propagate(part, first, count, FF):
        for k in range(count):
            pad(G, first + k, part, k)

        def one(k, _):
            comp = jnp.where(first + k == 10, 1280 + q16, (first + k) * 128 + dev)
            way = lax.rem(comp, ND)
            pace = speed_ref[comp]
            cx = cur[0] + pace * dirs_ref[0, way]
            cy = cur[1] + pace * dirs_ref[1, way]
            f = substep(G[first + k], cx, cy, first_lane, last_lane) * keep
            f = substep(f, cx, cy, first_lane, last_lane)
            hi, lo = split(f[8:136])
            r = pl.multiple_of(k * 64, 64)
            for h in range(2):
                FF[pl.ds(r, 64), h * 128 : (h + 1) * 128] = hi[h * 64 : (h + 1) * 64]
                FF[pl.ds(count * 64 + r, 64), h * 128 : (h + 1) * 128] = lo[h * 64 : (h + 1) * 64]
            return 0

        lax.fori_loop(0, count, one, 0)

    def backward(part, first, count, FF, out):
        R = count * 64

        def chunk_step(t, _):
            chunk = (q16 - chunk_offset(15 - t)) & 15
            c = CT[:, pl.ds(pl.multiple_of(chunk * (S * 128), 128), S * 128)]
            T[:R] = jnp.dot(FF[:R], c, preferred_element_type=F32) + jnp.dot(FF[R:], c, preferred_element_type=F32)
            for j in range(S):
                s = chunk * S + j
                m = MF[:, pl.ds(pl.multiple_of(s * 128, 128), 128)]
                for k in range(count):
                    out[s, k] = jnp.sum(T[k * 64 : (k + 1) * 64, j * 128 : (j + 1) * 128] * m, axis=0, keepdims=True)

            def post(j, _):
                s = chunk * S + j

                @pl.when(s != dev)
                def _():
                    pltpu.make_async_remote_copy(
                        src_ref=out.at[s, pl.ds(0, 5)],
                        dst_ref=ret.at[pl.ds(first, 5), dev],
                        send_sem=r_send.at[part],
                        recv_sem=r_recv.at[part],
                        device_id=(grp, s),
                        device_id_type=MESH,
                    ).start()

                if part == 1:
                    @pl.when((s != dev) & owner)
                    def _():
                        pltpu.make_async_remote_copy(
                            src_ref=out.at[s, 5],
                            dst_ref=ret_last.at[q16],
                            send_sem=r_send.at[2],
                            recv_sem=r_recv.at[2],
                            device_id=(grp, s),
                            device_id_type=MESH,
                        ).start()

                return 0

            lax.fori_loop(0, S, post, 0)
            return 0

        lax.fori_loop(0, 128 // S, chunk_step, 0)
        for k in range(5):
            ret[first + k, dev] = out[dev, k]

    dacc[...] = jnp.zeros_like(dacc)
    forward(FIRST, arr1, acc, False)
    boundary(0, 0, FIRST)
    forward(SECOND, arr2, acc, True)
    boundary(1, FIRST, SECOND)
    drift = dacc[0:8] + dacc[8:16]
    wave_row = dev + lax.rem(lax.broadcasted_iota(jnp.int32, (8, 128), 0), 3) - 1
    drift = jnp.where(wave_row >= 64, drift[:, 128:], drift[:, :128])
    wide = jnp.dot(drift, spread_matrix(), precision=HIGH, preferred_element_type=F32)
    masks = couple_masks(cp_ref[...], dev)
    cells = []
    for q in range(2):
        sum_q = jnp.zeros((8, 256), F32)
        for dr in range(3):
            for delta in range(3):
                sum_q = sum_q + masks[dr][delta] * wide[q * 3 + dr : q * 3 + dr + 1, delta * 256 : (delta + 1) * 256]
        cells.append(sum_q)
    us, vs = cells

    oline = lax.broadcasted_iota(jnp.int32, (8, 256), 0)
    olane = lax.broadcasted_iota(jnp.int32, (8, 256), 1)
    coriolis = 0.5 + (linear * 8 + oline).astype(F32) / 2048.0
    fvs, fus = coriolis * vs, coriolis * us

    def ocean_step(slot, source, emit):
        def lap(a, z, q):
            above = jnp.where(has_up, ohalo[slot, 0, q, pl.ds(z, 1), :], 0.0)
            below = jnp.where(has_down, ohalo[slot, 1, q, pl.ds(z, 1), :], 0.0)
            r = jnp.where(olane == 255, 0.0, pltpu.roll(a, 255, 1)) + jnp.where(olane == 0, 0.0, pltpu.roll(a, 1, 1))
            r = r + jnp.where(oline == 0, above, pltpu.roll(a, 1, 0)) + jnp.where(oline == 7, below, pltpu.roll(a, 7, 0))
            return r - 4.0 * a

        def level(z, carry):
            pu, pv = carry
            u, v = source(0, z), source(1, z)
            zn = jnp.minimum(z + 1, NZ - 1)
            m0 = mix_ref[z]
            m1 = jnp.where(z == NZ - 1, 0.0, mix_ref[zn])
            nu, nv = source(0, zn), source(1, zn)
            p = prof_ref[z]
            wu = m1 * (nu - u) - m0 * (u - pu)
            wv = m1 * (nv - v) - m0 * (v - pv)
            emit(
                z,
                u + 0.2 * (0.2 * lap(u, z, 0) + wu + coriolis * v + p * fvs),
                v + 0.2 * (0.2 * lap(v, z, 1) + wv - coriolis * u - p * fus),
            )
            return u, v

        zero = jnp.zeros((8, 256), F32)
        lax.fori_loop(0, NZ, level, (zero, zero))

    def emit1(z, u, v):
        B[0, z] = u
        B[1, z] = v

    def emit2(z, u, v):
        ou_ref[z] = u
        ov_ref[z] = v

    ocean_wait(0)
    ocean_step(0, lambda q, z: (u_ref, v_ref)[q][z], emit1)
    stage_ocean(1, lambda z: B[0, z], lambda z: B[1, z])
    ocean_start(1)

    exchange(0).wait()
    exchange(1).wait()
    for q in range(2):
        pad(cur, q, 1, 6 + q)
    propagate(0, 0, FIRST, FF1)
    backward(0, 0, FIRST, FF1, out1)
    propagate(1, FIRST, SECOND, FF2)
    backward(1, FIRST, SECOND, FF2, out2)

    @pl.when(owner)
    def _():
        ret_last[q16] = out2[dev, 5]

    ocean_wait(1)
    ocean_step(1, lambda q, z: B[q, z], emit2)

    wait_for(pay1.at[pl.ds(0, 127)], a1_send)

    @pl.when(owner)
    def _():
        wait_for(pay2.at[pl.ds(0, 112), pl.ds(0, 9)], a2_send)
        wait_for(pay2.at[pl.ds(0, 15)], a3_send)
        wait_for(out2.at[pl.ds(0, 127), 5], r_send.at[2])
        wait_for(ret_last.at[pl.ds(0, 15)], r_recv.at[2])

    @pl.when(jnp.logical_not(owner))
    def _():
        wait_for(pay2.at[pl.ds(0, 111), pl.ds(0, 9)], a2_send)
        wait_for(pay2.at[pl.ds(0, 16)], a3_send)
        wait_for(ret_last.at[pl.ds(0, 16)], r_recv.at[2])

    wait_for(out1.at[pl.ds(0, 127)], r_send.at[0])
    wait_for(out2.at[pl.ds(0, 127), pl.ds(0, 5)], r_send.at[1])
    wait_for(ret.at[pl.ds(0, 5), pl.ds(0, 127)], r_recv.at[0])
    wait_for(ret.at[pl.ds(0, 5), pl.ds(0, 127)], r_recv.at[1])


def body(spectra, sea_mask, card_map, dia_table, dia_coef, speed, stokes_weight, couple_point, ocean_u, ocean_v, mixing):
    sds = jax.ShapeDtypeStruct
    dirs = direction_table()
    trig = np.zeros((8, KP), np.float32)
    trig[:2, :KC] = np.tile(dirs, (1, KC // ND))
    profile = np.exp(-3.0 * (np.arange(NZ) + 0.5) / NZ).astype(np.float32)
    vmem = pl.BlockSpec(memory_space=pltpu.VMEM)
    smem = pl.BlockSpec(memory_space=pltpu.SMEM)
    dma = pltpu.SemaphoreType.DMA
    scratch = [
        pltpu.VMEM((KP, 256), BF16),
        pltpu.VMEM((KP, 256), BF16),
        pltpu.VMEM((KP, 256), BF16),
        pltpu.VMEM((4 * CH, KP), BF16),
        pltpu.VMEM((KP, 128), F32),
        pltpu.VMEM((8, KP), jnp.int32),
        pltpu.VMEM((KP, 8), F32),
        pltpu.VMEM((128, FIRST, 1, 128), F32),
        pltpu.VMEM((128, ROWS, 1, 128), F32),
        pltpu.VMEM((128, FIRST, 1, 128), F32),
        pltpu.VMEM((128, ROWS, 1, 128), F32),
        pltpu.VMEM((128, FIRST, 1, 128), F32),
        pltpu.VMEM((128, SECOND, 1, 128), F32),
        pltpu.VMEM((256, 16384), BF16),
        pltpu.VMEM((64, 16384), BF16),
        pltpu.VMEM((64, 16384), F32),
        pltpu.VMEM((128 * SECOND + 16, S * 128), BF16),
        pltpu.VMEM((128 * FIRST, 256), BF16),
        pltpu.VMEM((128 * SECOND, 256), BF16),
        pltpu.VMEM((64 * SECOND, 256), F32),
        pltpu.VMEM((16, 256), F32),
        pltpu.VMEM((64 * SECOND, S * 128), F32),
        pltpu.VMEM((SHARE, 144, 128), F32),
        pltpu.VMEM((2, 144, 128), F32),
        pltpu.VMEM((2, 2, 8, 128), F32),
        pltpu.VMEM((2, 2, 8, 128), F32),
        pltpu.VMEM((3, 8, 128), F32),
        pltpu.VMEM((2, 8, 128), F32),
        pltpu.VMEM((2, 2, 2, NZ, 256), F32),
        pltpu.VMEM((2, 2, 2, NZ, 256), F32),
        pltpu.VMEM((2, NZ, 8, 256), F32),
        dma((2, 2)), dma((2, 2)), dma((2,)), dma((2,)),
        dma, dma((16,)), dma, dma((16,)), dma, dma((2,)), dma((2,)), dma((3,)), dma((3,)),
    ]
    ret, ret_last, new_u, new_v = pl.pallas_call(
        step_kernel,
        out_shape=(
            sds((10, 128, 1, 128), F32), sds((16, 1, 128), F32), sds((NZ, 8, 256), F32), sds((NZ, 8, 256), F32)
        ),
        in_specs=[vmem] * 7 + [smem] * 2 + [vmem] * 3 + [smem] * 2,
        out_specs=(vmem,) * 4,
        scratch_shapes=scratch,
        compiler_params=pltpu.CompilerParams(
            vmem_limit_bytes=VMEM_LIMIT, collective_id=0, has_side_effects=True
        ),
        name="step",
    )(
        spectra, sea_mask.reshape(1, 128), dia_table, dia_coef.reshape(1, KC), stokes_weight.reshape(1, KC),
        jnp.asarray(trig), card_map.reshape(256, 128), speed, jnp.asarray(dirs), couple_point, ocean_u, ocean_v,
        mixing, jnp.asarray(profile),
    )
    new_spectra = jnp.concatenate([ret.reshape(1280, 128), ret_last.reshape(16, 128)]) * sea_mask.astype(F32)
    return (new_spectra, new_u, new_v)


def solution(mesh):
    both = ("grp", "dev")
    in_specs = (P(None, both), P(both), P(), P(), P(), P(), P(), P(both, None), P(None, both, None), P(None, both, None), P())
    out_specs = (P(None, both), P(None, both, None), P(None, both, None))
    return jax.shard_map(body, mesh=mesh, in_specs=in_specs, out_specs=out_specs, check_vma=False)
```

time: 93.6 us -> 93.9 us (level)
  the two profiles are of different devices: /device:TPU:1 before, /device:TPU:8 now
where the time goes in v3:
time: 93.9 us; the launch traced here: 93.6 us
  Pallas kernels  85.9 us (91%)
  local copies, waits for them, and re-layouts  5.06 us (5%)
  other arithmetic  2.02 us (2%)
    pallas_call x1, Pallas kernels, body(): pl.pallas_call(step_kernel, out_shape=(sds((10, 128, 1, 128), F32), sds((...  85.9 us
    unnamed x12, local copies, waits for them, and re-layouts  3.16 us
    mul x1, other arithmetic, body(): jnp.concatenate([ret.reshape(1280, 128), ret_last.reshape(16, 128)])  2.02 us

profile of v3, /device:TPU:8, one launch (start us, length us, event | category | flops | bytes accessed | tf_op | source)
XLA Modules:
  0.0 93.6 jit_solution(1009883841315938153)
XLA Ops:
  0.6 0.0 copy-start.4
  0.6 0.6 copy-done.4
  1.3 0.0 copy-start.3
  1.3 1.3 %reshape.26.coef_ref = f32[1,1296]{1,0:T(1,128)} reshape(f32[1296]{0:T(1024)} %param.18) | data formatting | bytes 10368 | tf_op jit(solution)/shard_map/reshape | solution.py:669
  2.6 0.0 copy-done.3
  2.6 0.6 reshape.27.stokes_ref
  3.2 85.9 %step.1 = (f32[10,128,1,128]{3,2,1,0:T(1,128)}, f32[16,1,128]{2,1,0:T(1,128)}, f32[40,8,256]{2,1,0:T(8,128)}, f32[40,8,256]{2,1,0:T(8,128)}) custom-call(f32[1296,128]{1,0:T(8,128)} %e_ref.1, s32[1,128]{1,0:T(1,128)} %bitcast.7, s32[4,1296]{1,0:T(4,128)} %table_ref.1, f32[1,1296]{1,0:T(1,128)} %reshape.26.coef_ref, f32[1,1296]{1,0:T(1,128)} %reshape.27.stokes_ref, ...), custom_call_target="tpu_custom_call" | custom-call | tf_op jit(solution)/shard_map/step/pallas_call | solution.py:656
  89.1 0.0 copy-start.2
  89.1 0.7 copy-done.2
  89.8 0.0 copy-start.1
  89.8 2.0 %maximum_multiply_fusion = f32[1296,128]{1,0:T(8,128)} fusion(f32[16,128]{1,0:T(8,128)S(1)} %bitcast.6, f32[1280,128]{1,0:T(8,128)} %bitcast.4, f32[128]{0:T(128)S(1)} %convert_element_type.3), kind=kLoop, calls=%fused_computation | loop fusion | flops 331776 | bytes 1327616 | tf_op jit(solution)/shard_map/mul | solution.py:673
  91.8 0.0 copy-done.1
  91.8 0.0 copy-start
  91.8 0.7 copy.19
  92.5 0.4 copy-done
  92.9 0.7 copy.20
  (1 shorter events, 0.0 us)
Async XLA Ops:
  0.6 0.7 copy-start.4
  1.3 1.3 %copy-start.3 = (f32[1296]{0:T(1024)S(1)}, f32[1296]{0:T(1024)}, u32[]{:S(2)}) copy-start(f32[1296]{0:T(1024)} %param.20) | copy-start | bytes 15556
  89.1 0.7 copy-start.2
  89.8 2.0 %copy-start.1 = (f32[40,8,256]{2,1,0:T(8,128)S(1)}, f32[40,8,256]{2,1,0:T(8,128)}, u32[]{:S(2)}) copy-start(f32[40,8,256]{2,1,0:T(8,128)} %get-tuple-element.15) | copy-start | bytes 983044
  91.8 1.1 %copy-start = (f32[40,8,256]{2,1,0:T(8,128)S(1)}, f32[40,8,256]{2,1,0:T(8,128)}, u32[]{:S(2)}) copy-start(f32[40,8,256]{2,1,0:T(8,128)} %get-tuple-element.16) | copy-start | bytes 983044

commit v4 on v3

v4 whole, which is shorter than its diff:
```python
import jax
import jax.numpy as jnp
import numpy as np
from jax import lax
from jax.experimental import pallas as pl
from jax.experimental.pallas import tpu as pltpu
from jax.sharding import PartitionSpec as P

ND = 36
NZ = 40
KC = 1296
KP = 1408
SHARE = 11
F32, BF16 = jnp.float32, jnp.bfloat16
NT = (((1,), (1,)), ((), ()))
HIGH = lax.Precision.HIGHEST
MESH = pl.DeviceIdType.MESH
VMEM_LIMIT = 56 << 20


def direction_table():
    theta = (np.arange(ND) + 0.5) * (2.0 * np.pi / ND)
    return np.stack([np.cos(theta), np.sin(theta)]).astype(np.float32)


def split(x):
    hi = x.astype(BF16)
    return hi, (x - hi.astype(F32)).astype(BF16)


def spread_matrix():
    wide = lax.broadcasted_iota(jnp.int32, (128, 768), 1)
    target = ((wide & 255) >> 1) + (wide >> 8) - 1
    return jnp.where(lax.broadcasted_iota(jnp.int32, (128, 768), 0) == target, 1.0, 0.0)


def couple_masks(cp, dev):
    row = (cp >> 7) - dev
    col = (cp & 127) - (lax.broadcasted_iota(jnp.int32, (8, 256), 1) >> 1)
    valid = cp >= 0
    return [
        [jnp.where(valid & (row == dr - 1) & (col == delta - 1), 1.0, 0.0) for delta in range(3)]
        for dr in range(3)
    ]


def build_maps(map_ref, base, CT, M, MF):
    def step(s, _):
        row = map_ref[pl.ds(base + s, 1), :]
        n = ((row >> 13) << 7) | (row & 127)
        rl = (row >> 7) & 63
        col = pl.ds(pl.multiple_of(s * 128, 128), 128)
        CT[:, col] = jnp.where(lax.broadcasted_iota(jnp.int32, (256, 128), 0) == n, 1.0, 0.0).astype(BF16)
        mf = jnp.where(lax.broadcasted_iota(jnp.int32, (64, 128), 0) == rl, 1.0, 0.0)
        MF[:, col] = mf
        M[:, col] = mf.astype(BF16)
        return 0

    lax.fori_loop(0, 128, step, 0)


def substep(f, cx, cy, first_lane, last_lane):
    ox = jnp.maximum(cx, 0.0) * f
    ix = jnp.minimum(cx, 0.0) * f
    oy = jnp.maximum(cy, 0.0) * f
    iy = jnp.minimum(cy, 0.0) * f
    rows = f.shape[0]
    nx = jnp.where(last_lane, 0.0, pltpu.roll(ix, 127, 1))
    px = jnp.where(first_lane, 0.0, pltpu.roll(ox, 1, 1))
    ny = pltpu.roll(iy, rows - 1, 0)
    py = pltpu.roll(oy, 1, 0)
    return f - (ox - ix + nx - px) - (oy - iy + ny - py)


S = 8
ROWS = 15
R = SHARE * 64
ONEHOT = 8
RB = ONEHOT * 64
CH = 432


def chunk_offset(i):
    return jnp.where((i & 1) == 1, (i + 1) >> 1, 16 - (i >> 1))


def start_of(dev):
    return dev * 10 + ((dev + 7) >> 3)


def wait_for(ref, sem):
    pltpu.make_async_copy(ref, ref, sem).wait()


def step_kernel(
    e_ref, mask_ref, table_ref, coef_ref, stokes_ref, trig_ref, map_ref, speed_ref, dirs_ref, cp_ref, u_ref, v_ref,
    mix_ref, prof_ref,
    ret, ou_ref, ov_ref,
    E, F1, F2, OH, forced_ref, trow_ref, col_ref, pay, arr, out, CT, M, MF, LH, FF, acc, dacc, T,
    G, cur, edge, halo, part, pin, ostage, ohalo, B,
    o_send, o_recv, p_send, p_recv, a_send, a_recv, b_send,
    h_send, h_recv, r_send, r_recv,
):
    grp = lax.axis_index("grp")
    dev = lax.axis_index("dev")
    q16 = dev >> 3
    owner = (dev & 7) == 0
    first = start_of(dev)
    linear = grp * 128 + dev
    has_up = linear > 0
    has_down = linear < 255
    up = linear + 255
    up_id = ((up // 128) % 2, up % 128)
    down = linear + 1
    down_id = ((down // 128) % 2, down % 128)

    barrier = pltpu.get_barrier_semaphore()

    def greet(i, _):
        pl.semaphore_signal(barrier, inc=1, device_id=(grp, (dev + i) & 127), device_id_type=MESH)
        return 0

    lax.fori_loop(1, 128, greet, 0)
    pl.semaphore_signal(barrier, inc=1, device_id=(1 - grp, dev), device_id_type=MESH)
    crosses_down = (grp == 0) & (dev == 127)
    crosses_up = (grp == 1) & (dev == 0)

    @pl.when(crosses_down)
    def _():
        pl.semaphore_signal(barrier, inc=1, device_id=down_id, device_id_type=MESH)

    @pl.when(crosses_up)
    def _():
        pl.semaphore_signal(barrier, inc=1, device_id=up_id, device_id_type=MESH)

    masks = couple_masks(cp_ref[...], dev)
    surface = [u_ref[0], v_ref[0]]
    rows = []
    for dr in range(3):
        for q in range(3):
            pieces = []
            for delta in range(3):
                m = masks[dr][delta]
                pieces.append(jnp.sum(m if q == 2 else m * surface[q], axis=0, keepdims=True))
            rows.append(jnp.concatenate(pieces, axis=1))
        rows.append(jnp.zeros((5, 768), F32))
    sums = lax.dot_general(
        jnp.concatenate(rows, axis=0), spread_matrix(), NT, precision=HIGH, preferred_element_type=F32
    )
    for dr in range(3):
        part[dr] = sums[dr * 8 : (dr + 1) * 8]

    def stage_ocean(slot, a, b):
        def level(z, _):
            for side, line in ((0, 0), (1, 7)):
                ostage[slot, side, 0, pl.ds(z, 1), :] = a(z)[line : line + 1]
                ostage[slot, side, 1, pl.ds(z, 1), :] = b(z)[line : line + 1]
            return 0

        lax.fori_loop(0, NZ, level, 0, unroll=8)

    stage_ocean(0, lambda z: u_ref[z], lambda z: v_ref[z])
    build_maps(map_ref, grp * 128, CT, M, MF)

    trow_ref[...] = jnp.full((8, KP), -1, jnp.int32)
    trow_ref[0:4, :KC] = table_ref[...]
    OH_rows = trow_ref[...].astype(F32)
    line8 = lax.broadcasted_iota(jnp.int32, (8, KP), 0)
    wide_coef = jnp.concatenate([coef_ref[...].reshape(1, KC), jnp.zeros((1, KP - KC), F32)], axis=1)
    col_ref[...] = jnp.transpose(jnp.where(line8 < 4, OH_rows, wide_coef))
    tail = jnp.zeros((KP - KC, 256), BF16)
    E[KC:, :] = tail
    F1[KC:, :] = tail
    F2[KC:, :] = tail
    hi, lo = split(e_ref[...])
    E[:KC, :128] = hi
    E[:KC, 128:] = lo

    def gather(i, _):
        rows = pl.ds(pl.multiple_of(i * CH, 16), CH)
        lanes = lax.broadcasted_iota(jnp.int32, (CH, KP), 1).astype(F32)
        e = e_ref[rows, :]
        cols = col_ref[rows, :]
        for m in range(4):
            OH[m * CH : (m + 1) * CH, :] = jnp.where(lanes == cols[:, m : m + 1], 1.0, 0.0).astype(BF16)
        p = jnp.dot(OH[...], E[...], preferred_element_type=F32)
        p = p[:, :128] + p[:, 128:]
        g = [p[m * CH : (m + 1) * CH] for m in range(4)]
        s = cols[:, 4:5]
        ee = e * e
        e2 = 2.0 * e
        a = s * (ee * (g[0] + g[1]) - e2 * g[0] * g[1])
        b = s * (ee * (g[2] + g[3]) - e2 * g[2] * g[3])
        forced_ref[rows, :] = e - (a + b)
        ah, al = split(a)
        bh, bl = split(b)
        F1[rows, :128] = ah
        F1[rows, 128:] = al
        F2[rows, :128] = bh
        F2[rows, 128:] = bl
        return 0

    lax.fori_loop(0, KC // CH, gather, 0)

    mask = mask_ref[...].astype(F32)

    def scatter(i, _):
        rows = pl.ds(pl.multiple_of(i * CH, 16), CH)
        b = lax.broadcasted_iota(jnp.int32, (CH, KP), 0) + i * CH

        def onehot(m):
            return jnp.where(b == trow_ref[m : m + 1, :], 1.0, 0.0)

        p = jnp.dot((onehot(0) + onehot(1)).astype(BF16), F1[...], preferred_element_type=F32)
        p = p + jnp.dot((onehot(2) + onehot(3)).astype(BF16), F2[...], preferred_element_type=F32)
        forced_ref[rows, :] = mask * (forced_ref[rows, :] + 0.5 * (p[:, :128] + p[:, 128:]))
        return 0

    lax.fori_loop(0, KC // CH, scatter, 0)

    def destination(n):
        return (((q16 - chunk_offset(n >> 3)) & 15) << 3) | ((dev + n) & 7)

    forced_ref[KC:, :] = jnp.zeros((KP - KC, 128), F32)
    weights = trig_ref[...] * jnp.concatenate([stokes_ref[...].reshape(1, KC), jnp.zeros((1, KP - KC), F32)], axis=1)
    drift_own = jnp.dot(weights, forced_ref[...], precision=HIGH, preferred_element_type=F32)

    def ocean_copy(slot, side):
        return pltpu.make_async_remote_copy(
            src_ref=ostage.at[slot, side],
            dst_ref=ohalo.at[slot, 1 - side],
            send_sem=o_send.at[slot, side],
            recv_sem=o_recv.at[slot, 1 - side],
            device_id=up_id if side == 0 else down_id,
            device_id_type=MESH,
        )

    def ocean_start(slot):
        for side, there in ((0, has_up), (1, has_down)):
            @pl.when(there)
            def _(side=side):
                ocean_copy(slot, side).start()

    def ocean_wait(slot):
        for side, there in ((0, has_up), (1, has_down)):
            @pl.when(there)
            def _(side=side):
                wait_for(ostage.at[slot, side], o_send.at[slot, side])
                wait_for(ohalo.at[slot, side], o_recv.at[slot, side])

    def part_copy(side):
        return pltpu.make_async_remote_copy(
            src_ref=part.at[2 * side],
            dst_ref=pin.at[1 - side],
            send_sem=p_send.at[side],
            recv_sem=p_recv.at[1 - side],
            device_id=(grp, (dev + 127 + 2 * side) & 127),
            device_id_type=MESH,
        )

    def fill(t, _):
        for r in range(4):
            d = t * 4 + r
            base = start_of(d)
            for k in range(10):
                pay[d, k] = forced_ref[pl.ds(base + k, 1), :]
            for q in range(2):
                pay[d, 10 + q] = drift_own[q : q + 1]
            pay[d, 14] = forced_ref[pl.ds(base + 10, 1), :]
        return 0

    lax.fori_loop(0, 32, fill, 0)

    pl.semaphore_wait(barrier, 128 + jnp.where(crosses_down | crosses_up, 1, 0))

    for side, there in ((0, dev > 0), (1, dev < 127)):
        @pl.when(there)
        def _(side=side):
            part_copy(side).start()

    for side, there in ((0, dev > 0), (1, dev < 127)):
        @pl.when(there)
        def _(side=side):
            wait_for(part.at[2 * side], p_send.at[side])
            wait_for(pin.at[side], p_recv.at[side])

    total = part[1] + jnp.where(dev > 0, pin[0], 0.0) + jnp.where(dev < 127, pin[1], 0.0)
    speeds = 0.3 * total[0:2] / (total[2:3] + 1.0)

    def fill_currents(t, _):
        for r in range(8):
            for q in range(2):
                pay[t * 8 + r, 12 + q] = speeds[q : q + 1]
        return 0

    lax.fori_loop(0, 16, fill_currents, 0)

    @pl.when(owner)
    def _():
        pltpu.make_async_copy(pay.at[dev], arr.at[dev], a_recv.at[q16]).start()

    @pl.when(jnp.logical_not(owner))
    def _():
        pltpu.make_async_copy(pay.at[dev, pl.ds(0, 14)], arr.at[dev, pl.ds(0, 14)], a_recv.at[q16]).start()

    def send(n, _):
        dest = destination(n)

        @pl.when((dest & 7) == 0)
        def _():
            pltpu.make_async_remote_copy(
                src_ref=pay.at[dest],
                dst_ref=arr.at[dev],
                send_sem=b_send,
                recv_sem=a_recv.at[q16],
                device_id=(grp, dest),
                device_id_type=MESH,
            ).start()

        @pl.when((dest & 7) != 0)
        def _():
            pltpu.make_async_remote_copy(
                src_ref=pay.at[dest, pl.ds(0, 14)],
                dst_ref=arr.at[dev, pl.ds(0, 14)],
                send_sem=a_send,
                recv_sem=a_recv.at[q16],
                device_id=(grp, dest),
                device_id_type=MESH,
            ).start()

        return 0

    lax.fori_loop(1, 128, send, 0)
    ocean_start(0)

    zero_row = jnp.zeros((1, 128), F32)
    top = grp == 0

    acc[...] = jnp.zeros_like(acc)
    dacc[...] = jnp.zeros_like(dacc)

    def forward(i, _):
        chunk = (q16 + chunk_offset(i)) & 15

        @pl.when(owner)
        def _():
            wait_for(arr.at[pl.ds(chunk * S, S)], a_recv.at[chunk])

        @pl.when(jnp.logical_not(owner))
        def _():
            wait_for(arr.at[pl.ds(chunk * S, S), pl.ds(0, 14)], a_recv.at[chunk])

        for j in range(S):
            s = chunk * S + j
            cols = pl.ds(pl.multiple_of(s * 128, 128), 128)
            c = slice(j * 128, (j + 1) * 128)
            for k in range(SHARE):
                x = jnp.broadcast_to(arr[s, 14 if k == 10 else k], (16, 128))
                hi, lo = split(x)
                for q in range(4):
                    m = M[q * 16 : (q + 1) * 16, cols]
                    r = k * 64 + q * 16
                    LH[r : r + 16, c] = m * hi
                    LH[R + r : R + r + 16, c] = m * lo
            row = map_ref[pl.ds(grp * 128 + s, 1), :] >> 7
            pieces = []
            for q in range(2):
                cur[q, pl.ds(8 + s, 1), :] = arr[s, 12 + q]
                x = arr[s, 10 + q]
                for dr in range(3):
                    pieces.append(jnp.where(row == dev + (dr - 1), x, zero_row))
            pieces += [zero_row, zero_row]
            piece = jnp.concatenate(pieces, axis=0)
            hi = piece.astype(BF16).astype(F32)
            LH[2 * R : 2 * R + 16, c] = jnp.concatenate([hi, piece - hi], axis=0).astype(BF16)
        c = CT[:, pl.ds(pl.multiple_of(chunk * (S * 128), 128), S * 128)]
        d = lax.dot_general(LH[...], c, NT, preferred_element_type=F32)
        acc[...] += d[:R] + d[R : 2 * R]
        dacc[...] += d[2 * R :]
        return 0

    lax.fori_loop(0, 128 // S, forward, 0)

    for k in range(SHARE):
        low = acc[k * 64 : (k + 1) * 64, 0:128]
        high = acc[k * 64 : (k + 1) * 64, 128:256]
        G[k, 8:72, :] = low
        G[k, 72:136, :] = high
        edge[0, k : k + 1, :] = jnp.where(top, high[63:64], low[0:1])
        edge[1, k : k + 1, :] = jnp.where(top, high[62:63], low[1:2])
    for r in range(2):
        for q in range(2):
            edge[r, SHARE + q : SHARE + q + 1, :] = jnp.where(
                top, cur[q, 135 - r : 136 - r, :], cur[q, 8 + r : 9 + r, :]
            )
        edge[r, 13:16, :] = jnp.zeros((3, 128), F32)
    exchange = pltpu.make_async_remote_copy(
        src_ref=edge, dst_ref=halo, send_sem=h_send, recv_sem=h_recv, device_id=(1 - grp, dev), device_id_type=MESH
    )
    exchange.start()

    below_on = jnp.where(top, 1.0, 0.0)
    above_on = 1.0 - below_on
    blank = jnp.zeros((6, 128), F32)

    def pad(dst, index, k):
        h0 = halo[0, k : k + 1, :]
        h1 = halo[1, k : k + 1, :]
        dst[index, 0:8, :] = jnp.concatenate([blank, h1, h0], axis=0) * above_on
        dst[index, 136:144, :] = jnp.concatenate([h0, h1, blank], axis=0) * below_on

    lane = lax.broadcasted_iota(jnp.int32, (144, 128), 1)
    line = lax.broadcasted_iota(jnp.int32, (144, 128), 0)
    first_lane, last_lane = lane == 0, lane == 127
    keep = jnp.where(line < 8, above_on, jnp.where(line >= 136, below_on, 1.0))

    def propagate(k, _):
        comp = jnp.minimum(first + k, KC - 1)
        way = lax.rem(comp, ND)
        pace = speed_ref[comp]
        cx = cur[0] + pace * dirs_ref[0, way]
        cy = cur[1] + pace * dirs_ref[1, way]
        f = substep(G[k], cx, cy, first_lane, last_lane) * keep
        f = substep(f, cx, cy, first_lane, last_lane)
        G[k] = f
        return 0

    def backward(t, _):
        chunk = (q16 - chunk_offset(15 - t)) & 15
        c = CT[:, pl.ds(pl.multiple_of(chunk * (S * 128), 128), S * 128)]
        T[...] = jnp.dot(FF[:RB], c, preferred_element_type=F32) + jnp.dot(FF[RB:], c, preferred_element_type=F32)
        where = map_ref[pl.ds(pl.multiple_of(grp * 128 + chunk * S, 8), S), :]
        row, col = where >> 7, where & 127
        taken = [jnp.zeros((S, 128), F32) for _ in range(SHARE - ONEHOT)]
        for r in range(128):
            hit = row == r
            for k in range(SHARE - ONEHOT):
                x = jnp.broadcast_to(G[ONEHOT + k, 8 + r : 9 + r, :], (S, 128))
                y = jnp.take_along_axis(x, col, axis=1, mode="promise_in_bounds")
                taken[k] = jnp.where(hit, y, taken[k])
        for j in range(S):
            s = chunk * S + j
            for k in range(SHARE - ONEHOT):
                out[s, ONEHOT + k] = taken[k][j : j + 1]
            m = MF[:, pl.ds(pl.multiple_of(s * 128, 128), 128)]
            for k in range(ONEHOT):
                out[s, k] = jnp.sum(T[k * 64 : (k + 1) * 64, j * 128 : (j + 1) * 128] * m, axis=0, keepdims=True)

        def post(j, _):
            s = chunk * S + j

            @pl.when((s != dev) & owner)
            def _():
                pltpu.make_async_remote_copy(
                    src_ref=out.at[s],
                    dst_ref=ret.at[pl.ds(first, 11)],
                    send_sem=r_send,
                    recv_sem=r_recv,
                    device_id=(grp, s),
                    device_id_type=MESH,
                ).start()

            @pl.when((s != dev) & jnp.logical_not(owner))
            def _():
                pltpu.make_async_remote_copy(
                    src_ref=out.at[s, pl.ds(0, 10)],
                    dst_ref=ret.at[pl.ds(first, 10)],
                    send_sem=r_send,
                    recv_sem=r_recv,
                    device_id=(grp, s),
                    device_id_type=MESH,
                ).start()

            return 0

        lax.fori_loop(0, S, post, 0)
        return 0

    drift = dacc[0:8] + dacc[8:16]
    wave_row = dev + lax.rem(lax.broadcasted_iota(jnp.int32, (8, 128), 0), 3) - 1
    drift = jnp.where(wave_row >= 64, drift[:, 128:], drift[:, :128])
    wide = jnp.dot(drift, spread_matrix(), precision=HIGH, preferred_element_type=F32)
    masks = couple_masks(cp_ref[...], dev)
    cells = []
    for q in range(2):
        sum_q = jnp.zeros((8, 256), F32)
        for dr in range(3):
            for delta in range(3):
                sum_q = sum_q + masks[dr][delta] * wide[q * 3 + dr : q * 3 + dr + 1, delta * 256 : (delta + 1) * 256]
        cells.append(sum_q)
    us, vs = cells

    oline = lax.broadcasted_iota(jnp.int32, (8, 256), 0)
    olane = lax.broadcasted_iota(jnp.int32, (8, 256), 1)
    coriolis = 0.5 + (linear * 8 + oline).astype(F32) / 2048.0
    fvs, fus = coriolis * vs, coriolis * us

    def ocean_step(slot, source, emit):
        def lap(a, z, q):
            above = jnp.where(has_up, ohalo[slot, 0, q, pl.ds(z, 1), :], 0.0)
            below = jnp.where(has_down, ohalo[slot, 1, q, pl.ds(z, 1), :], 0.0)
            r = jnp.where(olane == 255, 0.0, pltpu.roll(a, 255, 1)) + jnp.where(olane == 0, 0.0, pltpu.roll(a, 1, 1))
            r = r + jnp.where(oline == 0, above, pltpu.roll(a, 1, 0)) + jnp.where(oline == 7, below, pltpu.roll(a, 7, 0))
            return r - 4.0 * a

        def level(z, carry):
            pu, pv = carry
            u, v = source(0, z), source(1, z)
            zn = jnp.minimum(z + 1, NZ - 1)
            m0 = mix_ref[z]
            m1 = jnp.where(z == NZ - 1, 0.0, mix_ref[zn])
            nu, nv = source(0, zn), source(1, zn)
            p = prof_ref[z]
            wu = m1 * (nu - u) - m0 * (u - pu)
            wv = m1 * (nv - v) - m0 * (v - pv)
            emit(
                z,
                u + 0.2 * (0.2 * lap(u, z, 0) + wu + coriolis * v + p * fvs),
                v + 0.2 * (0.2 * lap(v, z, 1) + wv - coriolis * u - p * fus),
            )
            return u, v

        zero = jnp.zeros((8, 256), F32)
        lax.fori_loop(0, NZ, level, (zero, zero), unroll=8)

    def emit1(z, u, v):
        B[0, z] = u
        B[1, z] = v

    def emit2(z, u, v):
        ou_ref[z] = u
        ov_ref[z] = v

    ocean_wait(0)
    ocean_step(0, lambda q, z: (u_ref, v_ref)[q][z], emit1)
    stage_ocean(1, lambda z: B[0, z], lambda z: B[1, z])
    ocean_start(1)

    exchange.wait()
    for k in range(SHARE):
        pad(G, k, k)
    for q in range(2):
        pad(cur, q, SHARE + q)
    lax.fori_loop(0, SHARE, propagate, 0)
    for k in range(ONEHOT):
        for h in range(2):
            hi, lo = split(G[k, 8 + h * 64 : 72 + h * 64, :])
            FF[k * 64 : (k + 1) * 64, h * 128 : (h + 1) * 128] = hi
            FF[RB + k * 64 : RB + (k + 1) * 64, h * 128 : (h + 1) * 128] = lo
    lax.fori_loop(0, 128 // S, backward, 0)
    for k in range(10):
        ret[first + k] = out[dev, k]

    @pl.when(owner)
    def _():
        ret[first + 10] = out[dev, 10]

    ocean_wait(1)
    ocean_step(1, lambda q, z: B[q, z], emit2)

    @pl.when(owner)
    def _():
        wait_for(pay.at[pl.ds(0, 112), pl.ds(0, 14)], a_send)
        wait_for(pay.at[pl.ds(0, 15)], b_send)
        wait_for(out.at[pl.ds(0, 127)], r_send)
        wait_for(ret.at[pl.ds(0, KC - 11)], r_recv)

    @pl.when(jnp.logical_not(owner))
    def _():
        wait_for(pay.at[pl.ds(0, 111), pl.ds(0, 14)], a_send)
        wait_for(pay.at[pl.ds(0, 16)], b_send)
        wait_for(out.at[pl.ds(0, 127), pl.ds(0, 10)], r_send)
        wait_for(ret.at[pl.ds(0, KC - 10)], r_recv)


def body(spectra, sea_mask, card_map, dia_table, dia_coef, speed, stokes_weight, couple_point, ocean_u, ocean_v, mixing):
    sds = jax.ShapeDtypeStruct
    dirs = direction_table()
    trig = np.zeros((8, KP), np.float32)
    trig[:2, :KC] = np.tile(dirs, (1, KC // ND))
    profile = np.exp(-3.0 * (np.arange(NZ) + 0.5) / NZ).astype(np.float32)
    vmem = pl.BlockSpec(memory_space=pltpu.VMEM)
    smem = pl.BlockSpec(memory_space=pltpu.SMEM)
    dma = pltpu.SemaphoreType.DMA
    scratch = [
        pltpu.VMEM((KP, 256), BF16),
        pltpu.VMEM((KP, 256), BF16),
        pltpu.VMEM((KP, 256), BF16),
        pltpu.VMEM((4 * CH, KP), BF16),
        pltpu.VMEM((KP, 128), F32),
        pltpu.VMEM((8, KP), jnp.int32),
        pltpu.VMEM((KP, 8), F32),
        pltpu.VMEM((128, ROWS, 1, 128), F32),
        pltpu.VMEM((128, ROWS, 1, 128), F32),
        pltpu.VMEM((128, SHARE, 1, 128), F32),
        pltpu.VMEM((256, 16384), BF16),
        pltpu.VMEM((64, 16384), BF16),
        pltpu.VMEM((64, 16384), F32),
        pltpu.VMEM((2 * R + 16, S * 128), BF16),
        pltpu.VMEM((2 * RB, 256), BF16),
        pltpu.VMEM((R, 256), F32),
        pltpu.VMEM((16, 256), F32),
        pltpu.VMEM((RB, S * 128), F32),
        pltpu.VMEM((SHARE, 144, 128), F32),
        pltpu.VMEM((2, 144, 128), F32),
        pltpu.VMEM((2, 16, 128), F32),
        pltpu.VMEM((2, 16, 128), F32),
        pltpu.VMEM((3, 8, 128), F32),
        pltpu.VMEM((2, 8, 128), F32),
        pltpu.VMEM((2, 2, 2, NZ, 256), F32),
        pltpu.VMEM((2, 2, 2, NZ, 256), F32),
        pltpu.VMEM((2, NZ, 8, 256), F32),
        dma((2, 2)), dma((2, 2)), dma((2,)), dma((2,)), dma, dma((16,)), dma, dma, dma, dma, dma,
    ]
    ret, new_u, new_v = pl.pallas_call(
        step_kernel,
        out_shape=(sds((KC, 1, 128), F32), sds((NZ, 8, 256), F32), sds((NZ, 8, 256), F32)),
        in_specs=[vmem] * 7 + [smem] * 2 + [vmem] * 3 + [smem] * 2,
        out_specs=(vmem,) * 3,
        scratch_shapes=scratch,
        compiler_params=pltpu.CompilerParams(
            vmem_limit_bytes=VMEM_LIMIT, collective_id=0, has_side_effects=True
        ),
        name="step",
    )(
        spectra, sea_mask.reshape(1, 128), dia_table, dia_coef, stokes_weight,
        jnp.asarray(trig), card_map.reshape(256, 128), speed, jnp.asarray(dirs), couple_point, ocean_u, ocean_v,
        mixing, jnp.asarray(profile),
    )
    new_spectra = ret.reshape(KC, 128) * sea_mask.astype(F32)
    return (new_spectra, new_u, new_v)


def solution(mesh):
    both = ("grp", "dev")
    in_specs = (P(None, both), P(both), P(), P(), P(), P(), P(), P(both, None), P(None, both, None), P(None, both, None), P())
    out_specs = (P(None, both), P(None, both, None), P(None, both, None))
    return jax.shard_map(body, mesh=mesh, in_specs=in_specs, out_specs=out_specs, check_vma=False)
```

time: 93.9 us -> 86.2 us (0.918)
  the two profiles are of different devices: /device:TPU:8 before, /device:TPU:1 now
where the time goes in v4:
time: 86.2 us; the launch traced here: 86 us
  Pallas kernels  80.8 us (94%)
  local copies, waits for them, and re-layouts  2.47 us (3%)
  other arithmetic  2.02 us (2%)
    pallas_call x1, Pallas kernels, body(): pl.pallas_call(step_kernel, out_shape=(sds((KC, 1, 128), F32), sds((NZ, 8...  80.8 us
    unnamed x8, local copies, waits for them, and re-layouts  2.47 us
    mul x1, other arithmetic, body(): new_spectra = ret.reshape(KC, 128) * sea_mask.astype(F32)  2.02 us

profile of v4, /device:TPU:1, one launch (start us, length us, event | category | flops | bytes accessed | tf_op | source)
XLA Modules:
  0.0 86.0 jit_solution(18000499342672589163)
XLA Ops:
  0.6 0.0 copy-start.2
  0.6 0.6 copy-done.2
  1.3 80.8 %step.1 = (f32[1296,1,128]{2,1,0:T(1,128)}, f32[40,8,256]{2,1,0:T(8,128)}, f32[40,8,256]{2,1,0:T(8,128)}) custom-call(f32[1296,128]{1,0:T(8,128)} %e_ref.1, s32[1,128]{1,0:T(1,128)} %bitcast.5, s32[4,1296]{1,0:T(4,128)} %table_ref.1, f32[1296]{0:T(1024)} %coef_ref.1, f32[1296]{0:T(1024)} %stokes_ref.1, f32[8,1408]{1,0:T(8,128)} %constant.6.clone.trig_ref, ...), custom_call_target="tpu_custom_call" | custom-call | tf_op jit(solution)/shard_map/step/pallas_call | solution.py:615
  82.1 0.0 copy-start.1
  82.1 2.0 %broadcast_multiply_fusion = f32[1296,128]{1,0:T(8,128)} fusion(f32[1296,128]{1,0:T(8,128)} %bitcast.3, f32[128]{0:T(128)S(1)} %convert_element_type.3), kind=kLoop, calls=%fused_computation | loop fusion | flops 165888 | bytes 1327616 | tf_op jit(solution)/shard_map/mul | solution.py:630
  84.2 0.0 copy-done.1
  84.2 0.0 copy-start
  84.2 0.7 copy.19
  84.9 0.4 copy-done
  85.3 0.7 copy.20
  (1 shorter events, 0.0 us)
Async XLA Ops:
  0.6 0.7 copy-start.2
  82.1 2.0 %copy-start.1 = (f32[40,8,256]{2,1,0:T(8,128)S(1)}, f32[40,8,256]{2,1,0:T(8,128)}, u32[]{:S(2)}) copy-start(f32[40,8,256]{2,1,0:T(8,128)} %get-tuple-element.13) | copy-start | bytes 983044
  84.2 1.1 %copy-start = (f32[40,8,256]{2,1,0:T(8,128)S(1)}, f32[40,8,256]{2,1,0:T(8,128)}, u32[]{:S(2)}) copy-start(f32[40,8,256]{2,1,0:T(8,128)} %get-tuple-element.14) | copy-start | bytes 983044

commit v5 on v4

--- a/solution.py
+++ b/solution.py
@@ -73,7 +73,7 @@
 
 
 S = 8
-ROWS = 15
+HEAD, TAIL = 7, 4
 R = SHARE * 64
 ONEHOT = 8
 RB = ONEHOT * 64
@@ -96,9 +96,9 @@
     e_ref, mask_ref, table_ref, coef_ref, stokes_ref, trig_ref, map_ref, speed_ref, dirs_ref, cp_ref, u_ref, v_ref,
     mix_ref, prof_ref,
     ret, ou_ref, ov_ref,
-    E, F1, F2, OH, forced_ref, trow_ref, col_ref, pay, arr, out, CT, M, MF, LH, FF, acc, dacc, T,
-    G, cur, edge, halo, part, pin, ostage, ohalo, B,
-    o_send, o_recv, p_send, p_recv, a_send, a_recv, b_send,
+    E, F1, F2, OH, forced_ref, trow_ref, col_ref, pay1, pay2, arr1, arr2, out, CT, M, MF, LH, FF, acc, dacc, T,
+    G, H, cur, edge, halo, part, pin, ostage, ohalo, B,
+    o_send, o_recv, p_send, p_recv, a1_send, a1_recv, a2_send, a2_recv, b_send,
     h_send, h_recv, r_send, r_recv,
 ):
     grp = lax.axis_index("grp")
@@ -262,11 +262,13 @@
         for r in range(4):
             d = t * 4 + r
             base = start_of(d)
-            for k in range(10):
-                pay[d, k] = forced_ref[pl.ds(base + k, 1), :]
+            for k in range(HEAD):
+                pay1[d, k] = forced_ref[pl.ds(base + k, 1), :]
+            for k in range(3):
+                pay2[d, k] = forced_ref[pl.ds(base + HEAD + k, 1), :]
             for q in range(2):
-                pay[d, 10 + q] = drift_own[q : q + 1]
-            pay[d, 14] = forced_ref[pl.ds(base + 10, 1), :]
+                pay2[d, 3 + q] = drift_own[q : q + 1]
+            pay2[d, 7] = forced_ref[pl.ds(base + 10, 1), :]
         return 0
 
     lax.fori_loop(0, 32, fill, 0)
@@ -277,6 +279,22 @@
         @pl.when(there)
         def _(side=side):
             part_copy(side).start()
+
+    pltpu.make_async_copy(pay1.at[dev], arr1.at[dev], a1_recv.at[q16]).start()
+
+    def send1(n, _):
+        dest = destination(n)
+        pltpu.make_async_remote_copy(
+            src_ref=pay1.at[dest],
+            dst_ref=arr1.at[dev],
+            send_sem=a1_send,
+            recv_sem=a1_recv.at[q16],
+            device_id=(grp, dest),
+            device_id_type=MESH,
+        ).start()
+        return 0
+
+    lax.fori_loop(1, 128, send1, 0)
 
     for side, there in ((0, dev > 0), (1, dev < 127)):
         @pl.when(there)
@@ -290,29 +308,29 @@
     def fill_currents(t, _):
         for r in range(8):
             for q in range(2):
-                pay[t * 8 + r, 12 + q] = speeds[q : q + 1]
+                pay2[t * 8 + r, 5 + q] = speeds[q : q + 1]
         return 0
 
     lax.fori_loop(0, 16, fill_currents, 0)
 
     @pl.when(owner)
     def _():
-        pltpu.make_async_copy(pay.at[dev], arr.at[dev], a_recv.at[q16]).start()
+        pltpu.make_async_copy(pay2.at[dev], arr2.at[dev], a2_recv.at[q16]).start()
 
     @pl.when(jnp.logical_not(owner))
     def _():
-        pltpu.make_async_copy(pay.at[dev, pl.ds(0, 14)], arr.at[dev, pl.ds(0, 14)], a_recv.at[q16]).start()
-
-    def send(n, _):
+        pltpu.make_async_copy(pay2.at[dev, pl.ds(0, 7)], arr2.at[dev, pl.ds(0, 7)], a2_recv.at[q16]).start()
+
+    def send2(n, _):
         dest = destination(n)
 
         @pl.when((dest & 7) == 0)
         def _():
             pltpu.make_async_remote_copy(
-                src_ref=pay.at[dest],
-                dst_ref=arr.at[dev],
+                src_ref=pay2.at[dest],
+                dst_ref=arr2.at[dev],
                 send_sem=b_send,
-                recv_sem=a_recv.at[q16],
+                recv_sem=a2_recv.at[q16],
                 device_id=(grp, dest),
                 device_id_type=MESH,
             ).start()
@@ -320,66 +338,74 @@
         @pl.when((dest & 7) != 0)
         def _():
             pltpu.make_async_remote_copy(
-                src_ref=pay.at[dest, pl.ds(0, 14)],
-                dst_ref=arr.at[dev, pl.ds(0, 14)],
-                send_sem=a_send,
-                recv_sem=a_recv.at[q16],
+                src_ref=pay2.at[dest, pl.ds(0, 7)],
+                dst_ref=arr2.at[dev, pl.ds(0, 7)],
+                send_sem=a2_send,
+                recv_sem=a2_recv.at[q16],
                 device_id=(grp, dest),
                 device_id_type=MESH,
             ).start()
 
         return 0
 
-    lax.fori_loop(1, 128, send, 0)
-    ocean_start(0)
-
+    lax.fori_loop(1, 128, send2, 0)
     zero_row = jnp.zeros((1, 128), F32)
     top = grp == 0
 
     acc[...] = jnp.zeros_like(acc)
     dacc[...] = jnp.zeros_like(dacc)
 
-    def forward(i, _):
-        chunk = (q16 + chunk_offset(i)) & 15
-
-        @pl.when(owner)
-        def _():
-            wait_for(arr.at[pl.ds(chunk * S, S)], a_recv.at[chunk])
-
-        @pl.when(jnp.logical_not(owner))
-        def _():
-            wait_for(arr.at[pl.ds(chunk * S, S), pl.ds(0, 14)], a_recv.at[chunk])
-
-        for j in range(S):
-            s = chunk * S + j
-            cols = pl.ds(pl.multiple_of(s * 128, 128), 128)
-            c = slice(j * 128, (j + 1) * 128)
-            for k in range(SHARE):
-                x = jnp.broadcast_to(arr[s, 14 if k == 10 else k], (16, 128))
-                hi, lo = split(x)
-                for q in range(4):
-                    m = M[q * 16 : (q + 1) * 16, cols]
-                    r = k * 64 + q * 16
-                    LH[r : r + 16, c] = m * hi
-                    LH[R + r : R + r + 16, c] = m * lo
-            row = map_ref[pl.ds(grp * 128 + s, 1), :] >> 7
-            pieces = []
-            for q in range(2):
-                cur[q, pl.ds(8 + s, 1), :] = arr[s, 12 + q]
-                x = arr[s, 10 + q]
-                for dr in range(3):
-                    pieces.append(jnp.where(row == dev + (dr - 1), x, zero_row))
-            pieces += [zero_row, zero_row]
-            piece = jnp.concatenate(pieces, axis=0)
-            hi = piece.astype(BF16).astype(F32)
-            LH[2 * R : 2 * R + 16, c] = jnp.concatenate([hi, piece - hi], axis=0).astype(BF16)
-        c = CT[:, pl.ds(pl.multiple_of(chunk * (S * 128), 128), S * 128)]
-        d = lax.dot_general(LH[...], c, NT, preferred_element_type=F32)
-        acc[...] += d[:R] + d[R : 2 * R]
-        dacc[...] += d[2 * R :]
-        return 0
-
-    lax.fori_loop(0, 128 // S, forward, 0)
+    def forward(low, count, last):
+        n = count * 64
+
+        def chunk_step(i, _):
+            chunk = (q16 + chunk_offset(i)) & 15
+            if last:
+                @pl.when(owner)
+                def _():
+                    wait_for(arr2.at[pl.ds(chunk * S, S)], a2_recv.at[chunk])
+
+                @pl.when(jnp.logical_not(owner))
+                def _():
+                    wait_for(arr2.at[pl.ds(chunk * S, S), pl.ds(0, 7)], a2_recv.at[chunk])
+            else:
+                wait_for(arr1.at[pl.ds(chunk * S, S)], a1_recv.at[chunk])
+
+            for j in range(S):
+                s = chunk * S + j
+                cols = pl.ds(pl.multiple_of(s * 128, 128), 128)
+                c = slice(j * 128, (j + 1) * 128)
+                for k in range(count):
+                    x = (arr2[s, 7 if k == 3 else k]) if last else arr1[s, k]
+                    hi, lo = split(jnp.broadcast_to(x, (16, 128)))
+                    for q in range(4):
+                        m = M[q * 16 : (q + 1) * 16, cols]
+                        r = k * 64 + q * 16
+                        LH[r : r + 16, c] = m * hi
+                        LH[n + r : n + r + 16, c] = m * lo
+                if last:
+                    row = map_ref[pl.ds(grp * 128 + s, 1), :] >> 7
+                    pieces = []
+                    for q in range(2):
+                        cur[q, pl.ds(8 + s, 1), :] = arr2[s, 5 + q]
+                        x = arr2[s, 3 + q]
+                        for dr in range(3):
+                            pieces.append(jnp.where(row == dev + (dr - 1), x, zero_row))
+                    pieces += [zero_row, zero_row]
+                    piece = jnp.concatenate(pieces, axis=0)
+                    hi = piece.astype(BF16).astype(F32)
+                    LH[2 * n : 2 * n + 16, c] = jnp.concatenate([hi, piece - hi], axis=0).astype(BF16)
+            c = CT[:, pl.ds(pl.multiple_of(chunk * (S * 128), 128), S * 128)]
+            d = lax.dot_general(LH[: 2 * n + (16 if last else 0)], c, NT, preferred_element_type=F32)
+            acc[low : low + n] += d[:n] + d[n : 2 * n]
+            if last:
+                dacc[...] += d[2 * n :]
+            return 0
+
+        lax.fori_loop(0, 128 // S, chunk_step, 0)
+
+    forward(0, HEAD, False)
+    forward(HEAD * 64, TAIL, True)
 
     for k in range(SHARE):
         low = acc[k * 64 : (k + 1) * 64, 0:128]
@@ -398,6 +424,7 @@
         src_ref=edge, dst_ref=halo, send_sem=h_send, recv_sem=h_recv, device_id=(1 - grp, dev), device_id_type=MESH
     )
     exchange.start()
+    ocean_start(0)
 
     below_on = jnp.where(top, 1.0, 0.0)
     above_on = 1.0 - below_on
@@ -414,15 +441,19 @@
     first_lane, last_lane = lane == 0, lane == 127
     keep = jnp.where(line < 8, above_on, jnp.where(line >= 136, below_on, 1.0))
 
-    def propagate(k, _):
+    def pace_of(k):
         comp = jnp.minimum(first + k, KC - 1)
         way = lax.rem(comp, ND)
         pace = speed_ref[comp]
-        cx = cur[0] + pace * dirs_ref[0, way]
-        cy = cur[1] + pace * dirs_ref[1, way]
+        return pace * dirs_ref[0, way], pace * dirs_ref[1, way]
+
+    def propagate(k, _):
+        pace_x, pace_y = pace_of(k)
+        cx = cur[0] + pace_x
+        cy = cur[1] + pace_y
         f = substep(G[k], cx, cy, first_lane, last_lane) * keep
         f = substep(f, cx, cy, first_lane, last_lane)
-        G[k] = f
+        H[k] = f[8:136]
         return 0
 
     def backward(t, _):
@@ -435,7 +466,7 @@
         for r in range(128):
             hit = row == r
             for k in range(SHARE - ONEHOT):
-                x = jnp.broadcast_to(G[ONEHOT + k, 8 + r : 9 + r, :], (S, 128))
+                x = jnp.broadcast_to(H[ONEHOT + k, r : r + 1, :], (S, 128))
                 y = jnp.take_along_axis(x, col, axis=1, mode="promise_in_bounds")
                 taken[k] = jnp.where(hit, y, taken[k])
         for j in range(S):
@@ -475,6 +506,38 @@
 
         lax.fori_loop(0, S, post, 0)
         return 0
+
+    none = jnp.zeros((8, 128), F32)
+    for k in range(SHARE):
+        G[k, 0:8, :] = none
+        G[k, 136:144, :] = none
+    for q in range(2):
+        cur[q, 0:8, :] = none
+        cur[q, 136:144, :] = none
+
+    lax.fori_loop(0, SHARE, propagate, 0)
+    exchange.wait()
+    for k in range(SHARE):
+        pad(G, k, k)
+    for q in range(2):
+        pad(cur, q, SHARE + q)
+    strip = pl.multiple_of(jnp.where(top, 112, 0), 8)
+    strip_lane = lax.broadcasted_iota(jnp.int32, (32, 128), 1)
+    strip_line = lax.broadcasted_iota(jnp.int32, (32, 128), 0) + strip
+    strip_keep = jnp.where(strip_line < 8, above_on, jnp.where(strip_line >= 136, below_on, 1.0))
+    strip_u, strip_v = cur[0, pl.ds(strip, 32), :], cur[1, pl.ds(strip, 32), :]
+    for k in range(SHARE):
+        pace_x, pace_y = pace_of(k)
+        cx, cy = strip_u + pace_x, strip_v + pace_y
+        f = substep(G[k, pl.ds(strip, 32), :], cx, cy, strip_lane == 0, strip_lane == 127) * strip_keep
+        f = substep(f, cx, cy, strip_lane == 0, strip_lane == 127)
+        H[k, pl.ds(pl.multiple_of(jnp.where(top, 120, 0), 8), 8), :] = jnp.where(top, f[16:24], f[8:16])
+    for k in range(ONEHOT):
+        for h in range(2):
+            hi, lo = split(H[k, h * 64 : 64 + h * 64, :])
+            FF[k * 64 : (k + 1) * 64, h * 128 : (h + 1) * 128] = hi
+            FF[RB + k * 64 : RB + (k + 1) * 64, h * 128 : (h + 1) * 128] = lo
+    lax.fori_loop(0, 5, backward, 0)
 
     drift = dacc[0:8] + dacc[8:16]
     wave_row = dev + lax.rem(lax.broadcasted_iota(jnp.int32, (8, 128), 0), 3) - 1
@@ -536,18 +599,7 @@
     stage_ocean(1, lambda z: B[0, z], lambda z: B[1, z])
     ocean_start(1)
 
-    exchange.wait()
-    for k in range(SHARE):
-        pad(G, k, k)
-    for q in range(2):
-        pad(cur, q, SHARE + q)
-    lax.fori_loop(0, SHARE, propagate, 0)
-    for k in range(ONEHOT):
-        for h in range(2):
-            hi, lo = split(G[k, 8 + h * 64 : 72 + h * 64, :])
-            FF[k * 64 : (k + 1) * 64, h * 128 : (h + 1) * 128] = hi
-            FF[RB + k * 64 : RB + (k + 1) * 64, h * 128 : (h + 1) * 128] = lo
-    lax.fori_loop(0, 128 // S, backward, 0)
+    lax.fori_loop(5, 128 // S, backward, 0)
     for k in range(10):
         ret[first + k] = out[dev, k]
 
@@ -558,19 +610,30 @@
     ocean_wait(1)
     ocean_step(1, lambda q, z: B[q, z], emit2)
 
+    wait_for(pay1.at[pl.ds(0, 127)], a1_send)
+
     @pl.when(owner)
     def _():
-        wait_for(pay.at[pl.ds(0, 112), pl.ds(0, 14)], a_send)
-        wait_for(pay.at[pl.ds(0, 15)], b_send)
+        wait_for(pay2.at[pl.ds(0, 112), pl.ds(0, 7)], a2_send)
+        wait_for(pay2.at[pl.ds(0, 15)], b_send)
         wait_for(out.at[pl.ds(0, 127)], r_send)
         wait_for(ret.at[pl.ds(0, KC - 11)], r_recv)
 
     @pl.when(jnp.logical_not(owner))
     def _():
-        wait_for(pay.at[pl.ds(0, 111), pl.ds(0, 14)], a_send)
-        wait_for(pay.at[pl.ds(0, 16)], b_send)
+        wait_for(pay2.at[pl.ds(0, 111), pl.ds(0, 7)], a2_send)
+        wait_for(pay2.at[pl.ds(0, 16)], b_send)
         wait_for(out.at[pl.ds(0, 127), pl.ds(0, 10)], r_send)
         wait_for(ret.at[pl.ds(0, KC - 10)], r_recv)
+
+
+def finish_kernel(r_ref, mask_ref, u_ref, v_ref, o_ref, ou_ref, ov_ref, sem):
+    copies = [pltpu.make_async_copy(u_ref, ou_ref, sem.at[0]), pltpu.make_async_copy(v_ref, ov_ref, sem.at[1])]
+    for copy in copies:
+        copy.start()
+    o_ref[...] = r_ref[...] * mask_ref[...].astype(F32)
+    for copy in copies:
+        copy.wait()
 
 
 def body(spectra, sea_mask, card_map, dia_table, dia_coef, speed, stokes_weight, couple_point, ocean_u, ocean_v, mixing):
@@ -590,18 +653,21 @@
         pltpu.VMEM((KP, 128), F32),
         pltpu.VMEM((8, KP), jnp.int32),
         pltpu.VMEM((KP, 8), F32),
-        pltpu.VMEM((128, ROWS, 1, 128), F32),
-        pltpu.VMEM((128, ROWS, 1, 128), F32),
+        pltpu.VMEM((128, HEAD, 1, 128), F32),
+        pltpu.VMEM((128, 8, 1, 128), F32),
+        pltpu.VMEM((128, HEAD, 1, 128), F32),
+        pltpu.VMEM((128, 8, 1, 128), F32),
         pltpu.VMEM((128, SHARE, 1, 128), F32),
         pltpu.VMEM((256, 16384), BF16),
         pltpu.VMEM((64, 16384), BF16),
         pltpu.VMEM((64, 16384), F32),
-        pltpu.VMEM((2 * R + 16, S * 128), BF16),
+        pltpu.VMEM((128 * HEAD, S * 128), BF16),
         pltpu.VMEM((2 * RB, 256), BF16),
         pltpu.VMEM((R, 256), F32),
         pltpu.VMEM((16, 256), F32),
         pltpu.VMEM((RB, S * 128), F32),
         pltpu.VMEM((SHARE, 144, 128), F32),
+        pltpu.VMEM((SHARE, 128, 128), F32),
         pltpu.VMEM((2, 144, 128), F32),
         pltpu.VMEM((2, 16, 128), F32),
         pltpu.VMEM((2, 16, 128), F32),
@@ -610,7 +676,8 @@
         pltpu.VMEM((2, 2, 2, NZ, 256), F32),
         pltpu.VMEM((2, 2, 2, NZ, 256), F32),
         pltpu.VMEM((2, NZ, 8, 256), F32),
-        dma((2, 2)), dma((2, 2)), dma((2,)), dma((2,)), dma, dma((16,)), dma, dma, dma, dma, dma,
+        dma((2, 2)), dma((2, 2)), dma((2,)), dma((2,)),
+        dma, dma((16,)), dma, dma((16,)), dma, dma, dma, dma, dma,
     ]
     ret, new_u, new_v = pl.pallas_call(
         step_kernel,
@@ -627,8 +694,15 @@
         jnp.asarray(trig), card_map.reshape(256, 128), speed, jnp.asarray(dirs), couple_point, ocean_u, ocean_v,
         mixing, jnp.asarray(profile),
     )
-    new_spectra = ret.reshape(KC, 128) * sea_mask.astype(F32)
-    return (new_spectra, new_u, new_v)
+    hbm = pl.BlockSpec(memory_space=pl.ANY)
+    return pl.pallas_call(
+        finish_kernel,
+        out_shape=(sds((KC, 128), F32), sds((NZ, 8, 256), F32), sds((NZ, 8, 256), F32)),
+        in_specs=[vmem, vmem, hbm, hbm],
+        out_specs=(vmem, hbm, hbm),
+        scratch_shapes=[dma((2,))],
+        name="finish",
+    )(ret.reshape(KC, 128), sea_mask.reshape(1, 128), new_u, new_v)
 
 
 def solution(mesh):

time: 86.2 us -> 99.2 us (1.15)
  Pallas kernels: 80.8 us -> 98 us
  local copies, waits for them, and re-layouts: 2.47 us -> 0 us
  other arithmetic: 2.02 us -> 0 us
    pallas_call x0 -> x1, Pallas kernels: none -> 22.9 us  [body(): pl.pallas_call(finish_kernel, out_shape=(sds((KC, 128), F32), sds((NZ, 8,...]
    pallas_call x1, Pallas kernels: 80.8 us -> 75.1 us  [body(): pl.pallas_call(step_kernel, out_shape=(sds((KC, 1, 128), F32), sds((NZ, 8...]
    unnamed x8 -> x0, local copies, waits for them, and re-layouts: 2.47 us -> none
    mul x1 -> x0, other arithmetic: 2.02 us -> none  [body(): new_spectra = ret.reshape(KC, 128) * sea_mask.astype(F32)]
where the time goes in v5:
time: 99.2 us; the launch traced here: 98.6 us
  Pallas kernels  98 us (99%)
    pallas_call x1, Pallas kernels, body(): pl.pallas_call(step_kernel, out_shape=(sds((KC, 1, 128), F32), sds((NZ, 8...  75.1 us
    pallas_call x1, Pallas kernels, body(): pl.pallas_call(finish_kernel, out_shape=(sds((KC, 128), F32), sds((NZ, 8,...  22.9 us

profile of v5, /device:TPU:1, one launch (start us, length us, event | category | flops | bytes accessed | tf_op | source)
XLA Modules:
  0.0 98.6 jit_solution(16005200926986460423)
XLA Ops:
  0.6 75.1 %step.1 = (f32[1296,1,128]{2,1,0:T(1,128)}, f32[40,8,256]{2,1,0:T(8,128)}, f32[40,8,256]{2,1,0:T(8,128)}) custom-call(f32[1296,128]{1,0:T(8,128)} %e_ref.1, s32[1,128]{1,0:T(1,128)} %bitcast.5, s32[4,1296]{1,0:T(4,128)} %table_ref.1, f32[1296]{0:T(1024)} %coef_ref.1, f32[1296]{0:T(1024)} %stokes_ref.1, f32[8,1408]{1,0:T(8,128)} %constant.6.clone.trig_ref, ...), custom_call_target="tpu_custom_call" | custom-call | tf_op jit(solution)/shard_map/step/pallas_call | solution.py:682
  75.7 22.9 %finish.1 = (f32[1296,128]{1,0:T(8,128)}, f32[40,8,256]{2,1,0:T(8,128)}, f32[40,8,256]{2,1,0:T(8,128)}) custom-call(f32[1296,128]{1,0:T(8,128)} %bitcast.3, s32[1,128]{1,0:T(1,128)} %bitcast.6, f32[40,8,256]{2,1,0:T(8,128)} %get-tuple-element.7.u_ref, f32[40,8,256]{2,1,0:T(8,128)} %get-tuple-element.8.v_ref), custom_call_target="tpu_custom_call" | custom-call | tf_op jit(solution)/shard_map/finish/pallas_call | solution.py:698

commit v6 on v5

--- a/solution.py
+++ b/solution.py
@@ -627,13 +627,10 @@
         wait_for(ret.at[pl.ds(0, KC - 10)], r_recv)
 
 
-def finish_kernel(r_ref, mask_ref, u_ref, v_ref, o_ref, ou_ref, ov_ref, sem):
-    copies = [pltpu.make_async_copy(u_ref, ou_ref, sem.at[0]), pltpu.make_async_copy(v_ref, ov_ref, sem.at[1])]
-    for copy in copies:
-        copy.start()
+def finish_kernel(r_ref, mask_ref, u_ref, v_ref, o_ref, ou_ref, ov_ref):
+    ou_ref[...] = u_ref[...]
+    ov_ref[...] = v_ref[...]
     o_ref[...] = r_ref[...] * mask_ref[...].astype(F32)
-    for copy in copies:
-        copy.wait()
 
 
 def body(spectra, sea_mask, card_map, dia_table, dia_coef, speed, stokes_weight, couple_point, ocean_u, ocean_v, mixing):
@@ -694,13 +691,11 @@
         jnp.asarray(trig), card_map.reshape(256, 128), speed, jnp.asarray(dirs), couple_point, ocean_u, ocean_v,
         mixing, jnp.asarray(profile),
     )
-    hbm = pl.BlockSpec(memory_space=pl.ANY)
     return pl.pallas_call(
         finish_kernel,
         out_shape=(sds((KC, 128), F32), sds((NZ, 8, 256), F32), sds((NZ, 8, 256), F32)),
-        in_specs=[vmem, vmem, hbm, hbm],
-        out_specs=(vmem, hbm, hbm),
-        scratch_shapes=[dma((2,))],
+        in_specs=[vmem] * 4,
+        out_specs=(vmem,) * 3,
         name="finish",
     )(ret.reshape(KC, 128), sea_mask.reshape(1, 128), new_u, new_v)
 

time: 99.2 us -> 78.7 us (0.79)
  Pallas kernels: 98 us -> 77.4 us
    pallas_call x1, Pallas kernels: 22.9 us -> 2.37 us  [body(): pl.pallas_call(finish_kernel, out_shape=(sds((KC, 128), F32), sds((NZ, 8,...]
where the time goes in v6:
time: 78.7 us; the launch traced here: 78.1 us
  Pallas kernels  77.4 us (98%)
    pallas_call x1, Pallas kernels, body(): pl.pallas_call(step_kernel, out_shape=(sds((KC, 1, 128), F32), sds((NZ, 8...  75.1 us
    pallas_call x1, Pallas kernels, body(): pl.pallas_call(finish_kernel, out_shape=(sds((KC, 128), F32), sds((NZ, 8,...  2.37 us

profile of v6, /device:TPU:1, one launch (start us, length us, event | category | flops | bytes accessed | tf_op | source)
XLA Modules:
  0.0 78.1 jit_solution(3555639214744091463)
XLA Ops:
  0.6 75.1 %step.1 = (f32[1296,1,128]{2,1,0:T(1,128)}, f32[40,8,256]{2,1,0:T(8,128)}, f32[40,8,256]{2,1,0:T(8,128)}) custom-call(f32[1296,128]{1,0:T(8,128)} %e_ref.1, s32[1,128]{1,0:T(1,128)} %bitcast.5, s32[4,1296]{1,0:T(4,128)} %table_ref.1, f32[1296]{0:T(1024)} %coef_ref.1, f32[1296]{0:T(1024)} %stokes_ref.1, f32[8,1408]{1,0:T(8,128)} %constant.6.clone.trig_ref, ...), custom_call_target="tpu_custom_call" | custom-call | tf_op jit(solution)/shard_map/step/pallas_call | solution.py:679
  75.7 2.4 %finish.1 = (f32[1296,128]{1,0:T(8,128)}, f32[40,8,256]{2,1,0:T(8,128)}, f32[40,8,256]{2,1,0:T(8,128)}) custom-call(f32[1296,128]{1,0:T(8,128)} %bitcast.3, s32[1,128]{1,0:T(1,128)} %bitcast.6, f32[40,8,256]{2,1,0:T(8,128)} %get-tuple-element.7.u_ref, f32[40,8,256]{2,1,0:T(8,128)} %get-tuple-element.8.v_ref), custom_call_target="tpu_custom_call" | custom-call | tf_op jit(solution)/shard_map/finish/pallas_call | solution.py:694

commit v7 on v6

--- a/solution.py
+++ b/solution.py
@@ -149,18 +149,6 @@
     )
     for dr in range(3):
         part[dr] = sums[dr * 8 : (dr + 1) * 8]
-
-    def stage_ocean(slot, a, b):
-        def level(z, _):
-            for side, line in ((0, 0), (1, 7)):
-                ostage[slot, side, 0, pl.ds(z, 1), :] = a(z)[line : line + 1]
-                ostage[slot, side, 1, pl.ds(z, 1), :] = b(z)[line : line + 1]
-            return 0
-
-        lax.fori_loop(0, NZ, level, 0, unroll=8)
-
-    stage_ocean(0, lambda z: u_ref[z], lambda z: v_ref[z])
-    build_maps(map_ref, grp * 128, CT, M, MF)
 
     trow_ref[...] = jnp.full((8, KP), -1, jnp.int32)
     trow_ref[0:4, :KC] = table_ref[...]
@@ -221,9 +209,17 @@
     def destination(n):
         return (((q16 - chunk_offset(n >> 3)) & 15) << 3) | ((dev + n) & 7)
 
-    forced_ref[KC:, :] = jnp.zeros((KP - KC, 128), F32)
-    weights = trig_ref[...] * jnp.concatenate([stokes_ref[...].reshape(1, KC), jnp.zeros((1, KP - KC), F32)], axis=1)
-    drift_own = jnp.dot(weights, forced_ref[...], precision=HIGH, preferred_element_type=F32)
+    def fill1(t, _):
+        for r in range(4):
+            d = t * 4 + r
+            base = start_of(d)
+            for k in range(HEAD):
+                pay1[d, k] = forced_ref[pl.ds(base + k, 1), :]
+        return 0
+
+    lax.fori_loop(0, 32, fill1, 0)
+
+    pl.semaphore_wait(barrier, 128 + jnp.where(crosses_down | crosses_up, 1, 0))
 
     def ocean_copy(slot, side):
         return pltpu.make_async_remote_copy(
@@ -257,23 +253,6 @@
             device_id=(grp, (dev + 127 + 2 * side) & 127),
             device_id_type=MESH,
         )
-
-    def fill(t, _):
-        for r in range(4):
-            d = t * 4 + r
-            base = start_of(d)
-            for k in range(HEAD):
-                pay1[d, k] = forced_ref[pl.ds(base + k, 1), :]
-            for k in range(3):
-                pay2[d, k] = forced_ref[pl.ds(base + HEAD + k, 1), :]
-            for q in range(2):
-                pay2[d, 3 + q] = drift_own[q : q + 1]
-            pay2[d, 7] = forced_ref[pl.ds(base + 10, 1), :]
-        return 0
-
-    lax.fori_loop(0, 32, fill, 0)
-
-    pl.semaphore_wait(barrier, 128 + jnp.where(crosses_down | crosses_up, 1, 0))
 
     for side, there in ((0, dev > 0), (1, dev < 127)):
         @pl.when(there)
@@ -296,6 +275,35 @@
 
     lax.fori_loop(1, 128, send1, 0)
 
+    def stage_ocean(slot, a, b):
+        def level(z, _):
+            for side, line in ((0, 0), (1, 7)):
+                ostage[slot, side, 0, pl.ds(z, 1), :] = a(z)[line : line + 1]
+                ostage[slot, side, 1, pl.ds(z, 1), :] = b(z)[line : line + 1]
+            return 0
+
+        lax.fori_loop(0, NZ, level, 0, unroll=8)
+
+    stage_ocean(0, lambda z: u_ref[z], lambda z: v_ref[z])
+    forced_ref[KC:, :] = jnp.zeros((KP - KC, 128), F32)
+    weights = trig_ref[...] * jnp.concatenate([stokes_ref[...].reshape(1, KC), jnp.zeros((1, KP - KC), F32)], axis=1)
+    drift_own = jnp.dot(weights, forced_ref[...], precision=HIGH, preferred_element_type=F32)
+
+    def fill2(t, _):
+        for r in range(4):
+            d = t * 4 + r
+            base = start_of(d)
+            for k in range(3):
+                pay2[d, k] = forced_ref[pl.ds(base + HEAD + k, 1), :]
+            for q in range(2):
+                pay2[d, 3 + q] = drift_own[q : q + 1]
+            pay2[d, 7] = forced_ref[pl.ds(base + 10, 1), :]
+        return 0
+
+    lax.fori_loop(0, 32, fill2, 0)
+
+    build_maps(map_ref, grp * 128, CT, M, MF)
+
     for side, there in ((0, dev > 0), (1, dev < 127)):
         @pl.when(there)
         def _(side=side):
@@ -349,6 +357,7 @@
         return 0
 
     lax.fori_loop(1, 128, send2, 0)
+    ocean_start(0)
     zero_row = jnp.zeros((1, 128), F32)
     top = grp == 0
 
@@ -404,7 +413,49 @@
 
         lax.fori_loop(0, 128 // S, chunk_step, 0)
 
+    oline = lax.broadcasted_iota(jnp.int32, (8, 256), 0)
+    olane = lax.broadcasted_iota(jnp.int32, (8, 256), 1)
+    coriolis = 0.5 + (linear * 8 + oline).astype(F32) / 2048.0
+
+    def ocean_step(slot, source, emit, drift):
+        def lap(a, z, q):
+            above = jnp.where(has_up, ohalo[slot, 0, q, pl.ds(z, 1), :], 0.0)
+            below = jnp.where(has_down, ohalo[slot, 1, q, pl.ds(z, 1), :], 0.0)
+            r = jnp.where(olane == 255, 0.0, pltpu.roll(a, 255, 1)) + jnp.where(olane == 0, 0.0, pltpu.roll(a, 1, 1))
+            r = r + jnp.where(oline == 0, above, pltpu.roll(a, 1, 0)) + jnp.where(oline == 7, below, pltpu.roll(a, 7, 0))
+            return r - 4.0 * a
+
+        def level(z, carry):
+            pu, pv = carry
+            u, v = source(0, z), source(1, z)
+            zn = jnp.minimum(z + 1, NZ - 1)
+            m0 = mix_ref[z]
+            m1 = jnp.where(z == NZ - 1, 0.0, mix_ref[zn])
+            nu, nv = source(0, zn), source(1, zn)
+            p = prof_ref[z]
+            wu = m1 * (nu - u) - m0 * (u - pu)
+            wv = m1 * (nv - v) - m0 * (v - pv)
+            emit(
+                z,
+                u + 0.2 * (0.2 * lap(u, z, 0) + wu + coriolis * v + (p * drift[0] if drift else 0.0)),
+                v + 0.2 * (0.2 * lap(v, z, 1) + wv - coriolis * u + (p * drift[1] if drift else 0.0)),
+            )
+            return u, v
+
+        zero = jnp.zeros((8, 256), F32)
+        lax.fori_loop(0, NZ, level, (zero, zero), unroll=8)
+
+    def emit1(z, u, v):
+        B[0, z] = u
+        B[1, z] = v
+
+    def emit2(z, u, v):
+        ou_ref[z] = u
+        ov_ref[z] = v
+
     forward(0, HEAD, False)
+    ocean_wait(0)
+    ocean_step(0, lambda q, z: (u_ref, v_ref)[q][z], emit1, None)
     forward(HEAD * 64, TAIL, True)
 
     for k in range(SHARE):
@@ -424,7 +475,34 @@
         src_ref=edge, dst_ref=halo, send_sem=h_send, recv_sem=h_recv, device_id=(1 - grp, dev), device_id_type=MESH
     )
     exchange.start()
-    ocean_start(0)
+
+    drift = dacc[0:8] + dacc[8:16]
+    wave_row = dev + lax.rem(lax.broadcasted_iota(jnp.int32, (8, 128), 0), 3) - 1
+    drift = jnp.where(wave_row >= 64, drift[:, 128:], drift[:, :128])
+    wide = jnp.dot(drift, spread_matrix(), precision=HIGH, preferred_element_type=F32)
+    masks = couple_masks(cp_ref[...], dev)
+    cells = []
+    for q in range(2):
+        sum_q = jnp.zeros((8, 256), F32)
+        for dr in range(3):
+            for delta in range(3):
+                sum_q = sum_q + masks[dr][delta] * wide[q * 3 + dr : q * 3 + dr + 1, delta * 256 : (delta + 1) * 256]
+        cells.append(sum_q)
+    us, vs = cells
+
+    drift_terms = (coriolis * vs, -coriolis * us)
+
+    def add_drift(z, _):
+        p = 0.2 * prof_ref[z]
+        for q in range(2):
+            b = B[q, z] + p * drift_terms[q]
+            B[q, z] = b
+            for side, line in ((0, 0), (1, 7)):
+                ostage[1, side, q, pl.ds(z, 1), :] = b[line : line + 1]
+        return 0
+
+    lax.fori_loop(0, NZ, add_drift, 0, unroll=8)
+    ocean_start(1)
 
     below_on = jnp.where(top, 1.0, 0.0)
     above_on = 1.0 - below_on
@@ -537,69 +615,7 @@
             hi, lo = split(H[k, h * 64 : 64 + h * 64, :])
             FF[k * 64 : (k + 1) * 64, h * 128 : (h + 1) * 128] = hi
             FF[RB + k * 64 : RB + (k + 1) * 64, h * 128 : (h + 1) * 128] = lo
-    lax.fori_loop(0, 5, backward, 0)
-
-    drift = dacc[0:8] + dacc[8:16]
-    wave_row = dev + lax.rem(lax.broadcasted_iota(jnp.int32, (8, 128), 0), 3) - 1
-    drift = jnp.where(wave_row >= 64, drift[:, 128:], drift[:, :128])
-    wide = jnp.dot(drift, spread_matrix(), precision=HIGH, preferred_element_type=F32)
-    masks = couple_masks(cp_ref[...], dev)
-    cells = []
-    for q in range(2):
-        sum_q = jnp.zeros((8, 256), F32)
-        for dr in range(3):
-            for delta in range(3):
-                sum_q = sum_q + masks[dr][delta] * wide[q * 3 + dr : q * 3 + dr + 1, delta * 256 : (delta + 1) * 256]
-        cells.append(sum_q)
-    us, vs = cells
-
-    oline = lax.broadcasted_iota(jnp.int32, (8, 256), 0)
-    olane = lax.broadcasted_iota(jnp.int32, (8, 256), 1)
-    coriolis = 0.5 + (linear * 8 + oline).astype(F32) / 2048.0
-    fvs, fus = coriolis * vs, coriolis * us
-
-    def ocean_step(slot, source, emit):
-        def lap(a, z, q):
-            above = jnp.where(has_up, ohalo[slot, 0, q, pl.ds(z, 1), :], 0.0)
-            below = jnp.where(has_down, ohalo[slot, 1, q, pl.ds(z, 1), :], 0.0)
-            r = jnp.where(olane == 255, 0.0, pltpu.roll(a, 255, 1)) + jnp.where(olane == 0, 0.0, pltpu.roll(a, 1, 1))
-            r = r + jnp.where(oline == 0, above, pltpu.roll(a, 1, 0)) + jnp.where(oline == 7, below, pltpu.roll(a, 7, 0))
-            return r - 4.0 * a
-
-        def level(z, carry):
-            pu, pv = carry
-            u, v = source(0, z), source(1, z)
-            zn = jnp.minimum(z + 1, NZ - 1)
-            m0 = mix_ref[z]
-            m1 = jnp.where(z == NZ - 1, 0.0, mix_ref[zn])
-            nu, nv = source(0, zn), source(1, zn)
-            p = prof_ref[z]
-            wu = m1 * (nu - u) - m0 * (u - pu)
-            wv = m1 * (nv - v) - m0 * (v - pv)
-            emit(
-                z,
-                u + 0.2 * (0.2 * lap(u, z, 0) + wu + coriolis * v + p * fvs),
-                v + 0.2 * (0.2 * lap(v, z, 1) + wv - coriolis * u - p * fus),
-            )
-            return u, v
-
-        zero = jnp.zeros((8, 256), F32)
-        lax.fori_loop(0, NZ, level, (zero, zero), unroll=8)
-
-    def emit1(z, u, v):
-        B[0, z] = u
-        B[1, z] = v
-
-    def emit2(z, u, v):
-        ou_ref[z] = u
-        ov_ref[z] = v
-
-    ocean_wait(0)
-    ocean_step(0, lambda q, z: (u_ref, v_ref)[q][z], emit1)
-    stage_ocean(1, lambda z: B[0, z], lambda z: B[1, z])
-    ocean_start(1)
-
-    lax.fori_loop(5, 128 // S, backward, 0)
+    lax.fori_loop(0, 128 // S, backward, 0)
     for k in range(10):
         ret[first + k] = out[dev, k]
 
@@ -608,7 +624,7 @@
         ret[first + 10] = out[dev, 10]
 
     ocean_wait(1)
-    ocean_step(1, lambda q, z: B[q, z], emit2)
+    ocean_step(1, lambda q, z: B[q, z], emit2, drift_terms)
 
     wait_for(pay1.at[pl.ds(0, 127)], a1_send)
 

time: 78.7 us -> 80.7 us (1.025)
  Pallas kernels: 77.4 us -> 79.5 us
    pallas_call x1, Pallas kernels: 75.1 us -> 77.2 us  [body(): pl.pallas_call(step_kernel, out_shape=(sds((KC, 1, 128), F32), sds((NZ, 8...]
where the time goes in v7:
time: 80.7 us; the launch traced here: 80.2 us
  Pallas kernels  79.5 us (99%)
    pallas_call x1, Pallas kernels, body(): pl.pallas_call(step_kernel, out_shape=(sds((KC, 1, 128), F32), sds((NZ, 8...  77.2 us
    pallas_call x1, Pallas kernels, body(): pl.pallas_call(finish_kernel, out_shape=(sds((KC, 128), F32), sds((NZ, 8,...  2.37 us

profile of v7, /device:TPU:1, one launch (start us, length us, event | category | flops | bytes accessed | tf_op | source)
XLA Modules:
  0.0 80.2 jit_solution(17914352695980692642)
XLA Ops:
  0.6 77.2 %step.1 = (f32[1296,1,128]{2,1,0:T(1,128)}, f32[40,8,256]{2,1,0:T(8,128)}, f32[40,8,256]{2,1,0:T(8,128)}) custom-call(f32[1296,128]{1,0:T(8,128)} %e_ref.1, s32[1,128]{1,0:T(1,128)} %bitcast.5, s32[4,1296]{1,0:T(4,128)} %table_ref.1, f32[1296]{0:T(1024)} %coef_ref.1, f32[1296]{0:T(1024)} %stokes_ref.1, f32[8,1408]{1,0:T(8,128)} %constant.6.clone.trig_ref, ...), custom_call_target="tpu_custom_call" | custom-call | tf_op jit(solution)/shard_map/step/pallas_call | solution.py:695
  77.8 2.4 %finish.1 = (f32[1296,128]{1,0:T(8,128)}, f32[40,8,256]{2,1,0:T(8,128)}, f32[40,8,256]{2,1,0:T(8,128)}) custom-call(f32[1296,128]{1,0:T(8,128)} %bitcast.3, s32[1,128]{1,0:T(1,128)} %bitcast.6, f32[40,8,256]{2,1,0:T(8,128)} %get-tuple-element.7.u_ref, f32[40,8,256]{2,1,0:T(8,128)} %get-tuple-element.8.v_ref), custom_call_target="tpu_custom_call" | custom-call | tf_op jit(solution)/shard_map/finish/pallas_call | solution.py:710

commit v8 on v7

--- a/solution.py
+++ b/solution.py
@@ -166,11 +166,14 @@
 
     def gather(i, _):
         rows = pl.ds(pl.multiple_of(i * CH, 16), CH)
-        lanes = lax.broadcasted_iota(jnp.int32, (CH, KP), 1).astype(F32)
+        lanes = lax.broadcasted_iota(jnp.int16, (CH, KP), 1)
         e = e_ref[rows, :]
         cols = col_ref[rows, :]
+        one, nil = jnp.ones((), BF16), jnp.zeros((), BF16)
         for m in range(4):
-            OH[m * CH : (m + 1) * CH, :] = jnp.where(lanes == cols[:, m : m + 1], 1.0, 0.0).astype(BF16)
+            OH[m * CH : (m + 1) * CH, :] = jnp.where(
+                lanes == jnp.broadcast_to(cols[:, m : m + 1].astype(jnp.int32), (CH, KP)).astype(jnp.int16), one, nil
+            )
         p = jnp.dot(OH[...], E[...], preferred_element_type=F32)
         p = p[:, :128] + p[:, 128:]
         g = [p[m * CH : (m + 1) * CH] for m in range(4)]
@@ -368,20 +371,22 @@
         n = count * 64
 
         def chunk_step(i, _):
-            chunk = (q16 + chunk_offset(i)) & 15
-            if last:
-                @pl.when(owner)
-                def _():
-                    wait_for(arr2.at[pl.ds(chunk * S, S)], a2_recv.at[chunk])
-
-                @pl.when(jnp.logical_not(owner))
-                def _():
-                    wait_for(arr2.at[pl.ds(chunk * S, S), pl.ds(0, 7)], a2_recv.at[chunk])
-            else:
-                wait_for(arr1.at[pl.ds(chunk * S, S)], a1_recv.at[chunk])
-
-            for j in range(S):
-                s = chunk * S + j
+            chunk = ((dev >> 4) + jnp.where((i & 1) == 1, (i + 1) >> 1, 8 - (i >> 1))) & 7
+            for half in range(2):
+                eighth = chunk * 2 + half
+                if last:
+                    @pl.when(owner)
+                    def _():
+                        wait_for(arr2.at[pl.ds(eighth * S, S)], a2_recv.at[eighth])
+
+                    @pl.when(jnp.logical_not(owner))
+                    def _():
+                        wait_for(arr2.at[pl.ds(eighth * S, S), pl.ds(0, 7)], a2_recv.at[eighth])
+                else:
+                    wait_for(arr1.at[pl.ds(eighth * S, S)], a1_recv.at[eighth])
+
+            for j in range(2 * S):
+                s = chunk * (2 * S) + j
                 cols = pl.ds(pl.multiple_of(s * 128, 128), 128)
                 c = slice(j * 128, (j + 1) * 128)
                 for k in range(count):
@@ -404,14 +409,14 @@
                     piece = jnp.concatenate(pieces, axis=0)
                     hi = piece.astype(BF16).astype(F32)
                     LH[2 * n : 2 * n + 16, c] = jnp.concatenate([hi, piece - hi], axis=0).astype(BF16)
-            c = CT[:, pl.ds(pl.multiple_of(chunk * (S * 128), 128), S * 128)]
+            c = CT[:, pl.ds(pl.multiple_of(chunk * (S * 256), 128), S * 256)]
             d = lax.dot_general(LH[: 2 * n + (16 if last else 0)], c, NT, preferred_element_type=F32)
             acc[low : low + n] += d[:n] + d[n : 2 * n]
             if last:
                 dacc[...] += d[2 * n :]
             return 0
 
-        lax.fori_loop(0, 128 // S, chunk_step, 0)
+        lax.fori_loop(0, 64 // S, chunk_step, 0)
 
     oline = lax.broadcasted_iota(jnp.int32, (8, 256), 0)
     olane = lax.broadcasted_iota(jnp.int32, (8, 256), 1)
@@ -437,8 +442,8 @@
             wv = m1 * (nv - v) - m0 * (v - pv)
             emit(
                 z,
-                u + 0.2 * (0.2 * lap(u, z, 0) + wu + coriolis * v + (p * drift[0] if drift else 0.0)),
-                v + 0.2 * (0.2 * lap(v, z, 1) + wv - coriolis * u + (p * drift[1] if drift else 0.0)),
+                u + 0.2 * (0.2 * lap(u, z, 0) + wu + coriolis * v + p * drift[0]),
+                v + 0.2 * (0.2 * lap(v, z, 1) + wv - coriolis * u + p * drift[1]),
             )
             return u, v
 
@@ -454,8 +459,6 @@
         ov_ref[z] = v
 
     forward(0, HEAD, False)
-    ocean_wait(0)
-    ocean_step(0, lambda q, z: (u_ref, v_ref)[q][z], emit1, None)
     forward(HEAD * 64, TAIL, True)
 
     for k in range(SHARE):
@@ -492,17 +495,6 @@
 
     drift_terms = (coriolis * vs, -coriolis * us)
 
-    def add_drift(z, _):
-        p = 0.2 * prof_ref[z]
-        for q in range(2):
-            b = B[q, z] + p * drift_terms[q]
-            B[q, z] = b
-            for side, line in ((0, 0), (1, 7)):
-                ostage[1, side, q, pl.ds(z, 1), :] = b[line : line + 1]
-        return 0
-
-    lax.fori_loop(0, NZ, add_drift, 0, unroll=8)
-    ocean_start(1)
 
     below_on = jnp.where(top, 1.0, 0.0)
     above_on = 1.0 - below_on
@@ -615,7 +607,12 @@
             hi, lo = split(H[k, h * 64 : 64 + h * 64, :])
             FF[k * 64 : (k + 1) * 64, h * 128 : (h + 1) * 128] = hi
             FF[RB + k * 64 : RB + (k + 1) * 64, h * 128 : (h + 1) * 128] = lo
-    lax.fori_loop(0, 128 // S, backward, 0)
+    lax.fori_loop(0, 5, backward, 0)
+    ocean_wait(0)
+    ocean_step(0, lambda q, z: (u_ref, v_ref)[q][z], emit1, drift_terms)
+    stage_ocean(1, lambda z: B[0, z], lambda z: B[1, z])
+    ocean_start(1)
+    lax.fori_loop(5, 128 // S, backward, 0)
     for k in range(10):
         ret[first + k] = out[dev, k]
 
@@ -674,7 +671,7 @@
         pltpu.VMEM((256, 16384), BF16),
         pltpu.VMEM((64, 16384), BF16),
         pltpu.VMEM((64, 16384), F32),
-        pltpu.VMEM((128 * HEAD, S * 128), BF16),
+        pltpu.VMEM((128 * HEAD, S * 256), BF16),
         pltpu.VMEM((2 * RB, 256), BF16),
         pltpu.VMEM((R, 256), F32),
         pltpu.VMEM((16, 256), F32),

time: 80.7 us -> 75.4 us (0.934)
  Pallas kernels: 79.5 us -> 74.6 us
    pallas_call x1, Pallas kernels: 77.2 us -> 72.3 us  [body(): pl.pallas_call(step_kernel, out_shape=(sds((KC, 1, 128), F32), sds((NZ, 8...]
where the time goes in v8:
time: 75.4 us; the launch traced here: 75.3 us
  Pallas kernels  74.6 us (99%)
    pallas_call x1, Pallas kernels, body(): pl.pallas_call(step_kernel, out_shape=(sds((KC, 1, 128), F32), sds((NZ, 8...  72.3 us
    pallas_call x1, Pallas kernels, body(): pl.pallas_call(finish_kernel, out_shape=(sds((KC, 128), F32), sds((NZ, 8,...  2.37 us

profile of v8, /device:TPU:1, one launch (start us, length us, event | category | flops | bytes accessed | tf_op | source)
XLA Modules:
  0.0 75.3 jit_solution(9628312613381668578)
XLA Ops:
  0.6 72.3 %step.1 = (f32[1296,1,128]{2,1,0:T(1,128)}, f32[40,8,256]{2,1,0:T(8,128)}, f32[40,8,256]{2,1,0:T(8,128)}) custom-call(f32[1296,128]{1,0:T(8,128)} %e_ref.1, s32[1,128]{1,0:T(1,128)} %bitcast.5, s32[4,1296]{1,0:T(4,128)} %table_ref.1, f32[1296]{0:T(1024)} %coef_ref.1, f32[1296]{0:T(1024)} %stokes_ref.1, f32[8,1408]{1,0:T(8,128)} %constant.6.clone.trig_ref, ...), custom_call_target="tpu_custom_call" | custom-call | tf_op jit(solution)/shard_map/step/pallas_call | solution.py:692
  72.9 2.4 %finish.1 = (f32[1296,128]{1,0:T(8,128)}, f32[40,8,256]{2,1,0:T(8,128)}, f32[40,8,256]{2,1,0:T(8,128)}) custom-call(f32[1296,128]{1,0:T(8,128)} %bitcast.3, s32[1,128]{1,0:T(1,128)} %bitcast.6, f32[40,8,256]{2,1,0:T(8,128)} %get-tuple-element.7.u_ref, f32[40,8,256]{2,1,0:T(8,128)} %get-tuple-element.8.v_ref), custom_call_target="tpu_custom_call" | custom-call | tf_op jit(solution)/shard_map/finish/pallas_call | solution.py:707
